TPU v7x, 32 devices: a whole 2x2x4 slice. The times are simulated.
32 devices in a mesh: seq: 8 (over y, x, core), head: 4 (over z).
Axes of the slice: x: 2, y: 2, z: 4, core: 2. Of those that a mesh axis runs over, the one named last changes fastest.
Arguments:
- tokens: bfloat16 [1, 8192, 768], P(None, 'seq'), may hold values from -6 to 6
- starts: int32 [1, 8192], P(None, 'seq'), may hold values from 0 to 1, as said below
- norm_in_gain: float32 [768], replicated, may hold values from 0.1 to 1.9
- inner_weight: bfloat16 [768, 2, 1536], P(None, None, 'head'), may hold values from -0.21875 to 0.21875
- state_weight: bfloat16 [768, 2, 128], P(None, None, 'head'), may hold values from -0.21875 to 0.21875
- step_weight: bfloat16 [768, 24], P(None, 'head'), may hold values from -0.21875 to 0.21875
- conv_inner: bfloat16 [4, 1536], P(None, 'head'), may hold values from -3 to 3
- conv_inner_bias: bfloat16 [1536], P('head'), may hold values from -3 to 3
- conv_state: bfloat16 [4, 2, 128], P(None, None, 'head'), may hold values from -3 to 3
- conv_state_bias: bfloat16 [2, 128], P(None, 'head'), may hold values from -3 to 3
- step_bias: float32 [24], P('head'), may hold values from -7 to -2
- decay_log: float32 [24], P('head'), may hold values from -7 to 0.5
- skip_gain: float32 [24], P('head'), may hold values from 0.5 to 1.5
- norm_out_gain: float32 [1536], P('head'), may hold values from 0.1 to 1.9
- out_weight: bfloat16 [1536, 768], P('head'), may hold values from -0.15625 to 0.15625
- cotangent: bfloat16 [1, 8192, 768], P(None, 'seq'), may hold values from -6 to 6
Outputs:
- output: bfloat16 [1, 8192, 768], P(None, 'seq', 'head')
- grad_tokens: float32 [1, 8192, 768], P(None, 'seq', 'head')
- grad_norm_in_gain: float32 [768], P('head')
- grad_inner_weight: float32 [768, 2, 1536], P(None, None, 'head')
- grad_state_weight: float32 [768, 2, 128], P(None, None, 'head')
- grad_step_weight: float32 [768, 24], P(None, 'head')
- grad_conv_inner: float32 [4, 1536], P(None, 'head')
- grad_conv_inner_bias: float32 [1536], P('head')
- grad_conv_state: float32 [4, 2, 128], P(None, None, 'head')
- grad_conv_state_bias: float32 [2, 128], P(None, 'head')
- grad_step_bias: float32 [24], P('head')
- grad_decay_log: float32 [24], P('head')
- grad_skip_gain: float32 [24], P('head')
- grad_norm_out_gain: float32 [1536], P('head')
- grad_out_weight: float32 [1536, 768], P('head')
Inputs may be any that keep to these rules, and one draw needn't show every extreme that they name: `starts`: 1 marks the first token of a document; the first token of every sequence is marked, and in every draw one sequence has marks only within its first 512 and its last 512 positions.
All inputs are finite; a program needn't handle non-finite values.
Results may differ from a plain program's by a relative error of at most 0.0085.
The roundings to bfloat16 on the way count: a program that leaves them out, or rounds other values in their place, can miss the bound.
Values may be sent and summed in bfloat16 or wider, within the bound.
No kernel may reach another device: no remote copies, remote signals or barrier semaphores. Data moves between devices by JAX's collectives and lax.ppermute only.
A program may use at most 192 MiB of HBM per device.

v0:
```python
import jax
import jax.numpy as jnp
from jax import lax
from jax.sharding import PartitionSpec as P

K = 4
GROUP = 256
DI = 1536


EPSILON = 1e-05
HIGHEST = lax.Precision.HIGHEST


def shifted(block, axis, distance):
    devices = range(lax.axis_size(axis))
    route = [(i - distance, i) for i in devices if i - distance in devices]
    return lax.ppermute(block, axis, route)


def prefix(part, axis, combine, identity, reverse):
    count = lax.axis_size(axis)
    place = lax.axis_index(axis)
    ahead = count - 1 - place if reverse else place
    gathered = jax.tree.map(lambda a: lax.all_gather(a, axis), part)
    state = jax.tree.map(lambda a, e: jnp.zeros_like(a) + jnp.asarray(e, a.dtype), part, identity)

    def one(step, state):
        source = count - 1 - step if reverse else step
        return combine(
            state, jax.tree.map(lambda a: lax.dynamic_index_in_dim(a, source, 0, False), gathered)
        )

    return lax.fori_loop(0, ahead, one, state)


def rounded(tensor):
    return tensor.astype(jnp.bfloat16)


def sigmoid_linear(tensor):
    return tensor * jax.nn.sigmoid(tensor)


def swish_slope(tensor):
    squash = jax.nn.sigmoid(tensor)
    return squash * (1.0 + tensor * (1.0 - squash))


def shifted_keep(keeping, offset):
    if offset == 0:
        return keeping
    padding = jnp.ones(keeping.shape[:-1] + (offset,), jnp.float32)
    return jnp.concatenate([padding, keeping[..., : keeping.shape[-1] - offset]], axis=-1)


def tail_factors(keeping):
    length = keeping.shape[1]
    factors = [jnp.ones_like(keeping[:, 0])]
    for offset in range(1, K - 1):
        factors.append(factors[-1] * keeping[:, length - offset])
    return jnp.stack(factors[::-1], axis=1)


def conv_forward(extended, kernel, offset_bias, run_factors):
    length = extended.shape[1] - (K - 1)
    summed = offset_bias + kernel[K - 1] * extended[:, K - 1 :]
    for offset in range(1, K):
        begin_row = K - 1 - offset
        summed = (
            summed
            + kernel[begin_row]
            * extended[:, begin_row : begin_row + length]
            * run_factors[offset - 1][..., None]
        )
    return summed


def conv_backward(extended, kernel, grad_out, run_factors):
    length = grad_out.shape[1]
    grad_ext = jnp.pad(kernel[K - 1] * grad_out, ((0, 0), (K - 1, 0), (0, 0)))
    grad_kernel = [None] * K
    grad_kernel[K - 1] = jnp.sum(grad_out * extended[:, K - 1 :], axis=(0, 1))
    for offset in range(1, K):
        masked = grad_out * run_factors[offset - 1][..., None]
        begin_row = K - 1 - offset
        grad_kernel[begin_row] = jnp.sum(
            masked * extended[:, begin_row : begin_row + length], axis=(0, 1)
        )
        grad_ext = grad_ext + jnp.pad(
            kernel[begin_row] * masked, ((0, 0), (begin_row, offset), (0, 0))
        )
    return (grad_ext, jnp.stack(grad_kernel), jnp.sum(grad_out, axis=(0, 1)))


def group_core(carried, inputs, step_sizes, log_rates, state_in, read_out, marked):
    length = marked.shape[0]
    cumulative = jnp.cumsum(log_rates, axis=0)
    counts = jnp.cumsum(marked)
    position = jnp.arange(length)
    connected = (position[:, None] >= position[None, :]) & (counts[:, None] == counts[None, :])
    log_gaps = jnp.where(
        connected[:, :, None], cumulative[:, None, :] - cumulative[None, :, :], 0.0
    )
    decays = jnp.exp(log_gaps) * connected[:, :, None].astype(jnp.float32)
    scores = jnp.dot(read_out, state_in.T, precision=HIGHEST)
    mixing = scores[:, :, None] * decays * step_sizes[None, :, :]
    inside = jnp.einsum("ijh,jhp->ihp", mixing, inputs, precision=HIGHEST)
    living = (counts == 0).astype(jnp.float32)
    reaching = jnp.exp(cumulative) * living[:, None]
    outside = reaching[:, :, None] * jnp.einsum("in,hpn->ihp", read_out, carried, precision=HIGHEST)
    ending = (counts == counts[-1]).astype(jnp.float32)
    weights = jnp.exp(cumulative[-1][None, :] - cumulative) * ending[:, None] * step_sizes
    fresh_state = jnp.einsum("jh,jhp,jn->hpn", weights, inputs, state_in, precision=HIGHEST)
    fading = jnp.exp(cumulative[-1]) * living[-1]
    return (fading[:, None, None] * carried + fresh_state, inside + outside)


def local_row(inputs, step_sizes, decay_rate, state_in, read_out, marked):
    length, head_count, head_width = inputs.shape
    group_count = length // GROUP

    def advance(carried, pieces):
        return group_core(
            carried, pieces[0], pieces[1], pieces[1] * decay_rate, pieces[2], pieces[3], pieces[4]
        )

    pieces = (
        inputs.reshape(group_count, GROUP, head_count, head_width),
        step_sizes.reshape(group_count, GROUP, head_count),
        state_in.reshape(group_count, GROUP, -1),
        read_out.reshape(group_count, GROUP, -1),
        marked.reshape(group_count, GROUP),
    )
    initial = jnp.zeros((head_count, head_width, state_in.shape[1]), jnp.float32)
    final_state, outputs = lax.scan(advance, initial, pieces)
    fading = jnp.exp(jnp.sum(step_sizes * decay_rate, axis=0)) * (jnp.sum(marked) == 0).astype(
        jnp.float32
    )
    return (outputs.reshape(inputs.shape), fading, final_state)


def inbound_row(carried, step_sizes, decay_rate, read_out, marked):
    cumulative = jnp.cumsum(step_sizes * decay_rate, axis=0)
    living = (jnp.cumsum(marked) == 0).astype(jnp.float32)
    reaching = jnp.exp(cumulative) * living[:, None]
    return reaching[:, :, None] * jnp.einsum("in,hpn->ihp", read_out, carried, precision=HIGHEST)


def compose(earlier, later):
    return (earlier[0] * later[0], later[0][..., None, None] * earlier[1] + later[1])


def on_device(
    tokens,
    starts,
    norm_in_gain,
    inner_weight,
    state_weight,
    step_weight,
    conv_inner,
    conv_inner_bias,
    conv_state,
    conv_state_bias,
    step_bias,
    decay_log,
    skip_gain,
    norm_out_gain,
    out_weight,
    cotangent,
):
    row_count, length, model_width = tokens.shape
    head_count = step_weight.shape[1]
    channels = inner_weight.shape[2]
    state_part = state_weight.shape[2]
    keeping = 1.0 - starts.astype(jnp.float32)
    run_factors = []
    running = jnp.ones_like(keeping)
    for offset in range(1, K):
        running = running * shifted_keep(keeping, offset - 1)
        run_factors.append(running)
    ending_keep = tail_factors(keeping)[..., None]
    edge_start = length - (K - 1)
    token_float = tokens.astype(jnp.float32)
    inv_scale = lax.rsqrt(jnp.mean(token_float * token_float, axis=-1, keepdims=True) + EPSILON)
    normed_in = rounded(token_float * inv_scale * norm_in_gain)
    projected = jnp.einsum(
        "rsd,dkc->rskc", normed_in, inner_weight, preferred_element_type=jnp.float32
    )
    inner_pre = rounded(projected[:, :, 0])
    gate_pre = projected[:, :, 1]
    step_raw = jnp.einsum("rsd,dh->rsh", normed_in, step_weight, preferred_element_type=jnp.float32)
    state_full, conv_full, bias_full = (state_weight, conv_state, conv_state_bias)
    state_pre = rounded(
        jnp.einsum("rsd,dkn->rskn", normed_in, state_full, preferred_element_type=jnp.float32)
    )
    state_cols = state_pre.shape[3]
    state_flat = state_pre.reshape(row_count, length, 2 * state_cols)
    tail_inner = inner_pre[:, edge_start:] * rounded(ending_keep)
    tail_state = state_flat[:, edge_start:] * rounded(ending_keep)
    halo_inner, halo_state = shifted((tail_inner, tail_state), "seq", 1)
    ext_inner = jnp.concatenate([halo_inner, inner_pre], axis=1).astype(jnp.float32)
    ext_state = jnp.concatenate([halo_state, state_flat], axis=1).astype(jnp.float32)
    conv_out_inner = conv_forward(
        ext_inner, conv_inner.astype(jnp.float32), conv_inner_bias.astype(jnp.float32), run_factors
    )
    conv_out_state = conv_forward(
        ext_state,
        conv_full.astype(jnp.float32).reshape(K, -1),
        bias_full.astype(jnp.float32).reshape(-1),
        run_factors,
    )
    inner_act = rounded(sigmoid_linear(conv_out_inner))
    state_act = rounded(sigmoid_linear(conv_out_state)).reshape(row_count, length, 2, state_cols)
    state_all = lax.all_gather(state_act, "head", axis=3, tiled=True)
    step_pre = step_raw + step_bias
    step_sizes = jax.nn.softplus(step_pre)
    decay_rate = -jnp.exp(decay_log)
    inputs = inner_act.astype(jnp.float32).reshape(row_count, length, head_count, -1)
    state_in = state_all[:, :, 0].astype(jnp.float32)
    read_out = state_all[:, :, 1].astype(jnp.float32)

    def local_all(inputs_arg, steps_arg, rate_arg, state_arg, read_arg):
        return jax.vmap(local_row, in_axes=(0, 0, None, 0, 0, 0))(
            inputs_arg, steps_arg, rate_arg, state_arg, read_arg, starts
        )

    def inbound_all(carried_arg, steps_arg, rate_arg, read_arg):
        return jax.vmap(inbound_row, in_axes=(0, 0, None, 0, 0))(
            carried_arg, steps_arg, rate_arg, read_arg, starts
        )

    local_parts, local_pullback = jax.vjp(
        local_all, inputs, step_sizes, decay_rate, state_in, read_out
    )
    local_out, fading, final_state = local_parts
    identity = (jnp.ones_like(fading), jnp.zeros_like(final_state))
    incoming = prefix((fading, final_state), "seq", compose, identity, False)[1]
    inbound_value, inbound_pullback = jax.vjp(
        inbound_all, incoming, step_sizes, decay_rate, read_out
    )
    mixer_out = local_out + inbound_value + skip_gain[:, None] * inputs
    mixer_flat = mixer_out.reshape(row_count, length, channels)
    gate_act = sigmoid_linear(gate_pre)
    gated = mixer_flat * gate_act
    square_sum = lax.psum(jnp.sum(gated * gated, axis=-1), "head")
    out_scale = lax.rsqrt(square_sum / DI + EPSILON)[..., None]
    normed_out = rounded(gated * out_scale * norm_out_gain)
    branch_part = jnp.einsum(
        "rsc,cd->rsd", normed_out, out_weight, preferred_element_type=jnp.float32
    )
    branch = lax.psum_scatter(branch_part, "head", scatter_dimension=2, tiled=True)
    own_width = branch.shape[2]
    column_start = lax.axis_index("head") * own_width
    own_tokens = lax.dynamic_slice_in_dim(token_float, column_start, own_width, 2)
    output = rounded(own_tokens + branch)
    grad_out_weight = jnp.einsum(
        "rsc,rsd->cd", normed_out, cotangent, preferred_element_type=jnp.float32
    )
    grad_normed = jnp.einsum(
        "rsd,cd->rsc", cotangent, out_weight, preferred_element_type=jnp.float32
    )
    scaled_grad = grad_normed * norm_out_gain
    grad_norm_out = jnp.sum(grad_normed * gated * out_scale, axis=(0, 1))
    cross_sum = lax.psum(jnp.sum(scaled_grad * gated, axis=-1), "head")
    grad_gated = out_scale * scaled_grad - gated * out_scale**3 * (cross_sum / DI)[..., None]
    grad_mixer = (grad_gated * gate_act).reshape(mixer_out.shape)
    grad_gate = rounded(grad_gated * mixer_flat * swish_slope(gate_pre))
    grad_skip = jnp.sum(grad_mixer * inputs, axis=(0, 1, 3))
    grad_incoming, grad_steps_in, grad_rate_in, grad_read_in = inbound_pullback(grad_mixer)
    grad_final = prefix((fading, grad_incoming), "seq", compose, identity, True)[1]
    grad_fading = jnp.sum(grad_final * incoming, axis=(2, 3))
    grad_inputs, grad_steps, grad_rate, grad_state_in, grad_read = local_pullback(
        (grad_mixer, grad_fading, grad_final)
    )
    grad_inputs = grad_inputs + skip_gain[:, None] * grad_mixer
    grad_steps = grad_steps + grad_steps_in
    grad_rate = grad_rate + grad_rate_in
    grad_read = grad_read + grad_read_in
    grad_decay_log = grad_rate * decay_rate
    grad_step_pre = grad_steps * jax.nn.sigmoid(step_pre)
    grad_step_bias = jnp.sum(grad_step_pre, axis=(0, 1))
    grad_step_raw = rounded(grad_step_pre)
    grad_state_act = lax.psum_scatter(
        jnp.stack([grad_state_in, grad_read], axis=2), "head", scatter_dimension=3, tiled=True
    )
    own_state, own_ext = (conv_out_state, ext_state)
    grad_conv_inner_out = grad_inputs.reshape(row_count, length, channels) * swish_slope(
        conv_out_inner
    )
    grad_conv_state_out = grad_state_act.reshape(row_count, length, -1) * swish_slope(own_state)
    grad_ext_inner, grad_conv_inner, grad_conv_inner_bias = conv_backward(
        ext_inner, conv_inner.astype(jnp.float32), grad_conv_inner_out, run_factors
    )
    grad_ext_state, grad_conv_state, grad_conv_state_bias = conv_backward(
        own_ext, conv_state.astype(jnp.float32).reshape(K, -1), grad_conv_state_out, run_factors
    )
    back_inner, back_state = shifted(
        (grad_ext_inner[:, : K - 1], grad_ext_state[:, : K - 1]), "seq", -1
    )
    pad_rows = ((0, 0), (edge_start, 0), (0, 0))
    grad_inner_pre = rounded(
        grad_ext_inner[:, K - 1 :] + jnp.pad(back_inner * ending_keep, pad_rows)
    )
    grad_state_pre = rounded(
        grad_ext_state[:, K - 1 :] + jnp.pad(back_state * ending_keep, pad_rows)
    ).reshape(row_count, length, 2, state_part)
    grad_projected = jnp.stack([grad_inner_pre, grad_gate], axis=2)
    grad_inner_weight = jnp.einsum(
        "rsd,rskc->dkc", normed_in, grad_projected, preferred_element_type=jnp.float32
    )
    grad_state_weight = jnp.einsum(
        "rsd,rskn->dkn", normed_in, grad_state_pre, preferred_element_type=jnp.float32
    )
    grad_step_weight = jnp.einsum(
        "rsd,rsh->dh", normed_in, grad_step_raw, preferred_element_type=jnp.float32
    )
    grad_normed_in = (
        jnp.einsum(
            "rskc,dkc->rsd", grad_projected, inner_weight, preferred_element_type=jnp.float32
        )
        + jnp.einsum(
            "rskn,dkn->rsd", grad_state_pre, state_weight, preferred_element_type=jnp.float32
        )
        + jnp.einsum("rsh,dh->rsd", grad_step_raw, step_weight, preferred_element_type=jnp.float32)
    )
    scaled_in = grad_normed_in * norm_in_gain
    grad_gain_part = jnp.sum(grad_normed_in * token_float * inv_scale, axis=(0, 1))
    grad_token_part = inv_scale * scaled_in - token_float * inv_scale**3 * jnp.mean(
        scaled_in * token_float, axis=-1, keepdims=True
    )
    grad_token_sum, grad_gain_own = (
        lax.psum_scatter(grad_token_part, "head", scatter_dimension=2, tiled=True),
        lax.psum_scatter(grad_gain_part, "head", scatter_dimension=0, tiled=True),
    )
    grad_tokens = (
        lax.dynamic_slice_in_dim(cotangent, column_start, own_width, 2).astype(jnp.float32)
        + grad_token_sum
    )
    summed = lax.psum(
        (
            grad_gain_own,
            grad_inner_weight,
            grad_state_weight,
            grad_step_weight,
            grad_conv_inner,
            grad_conv_inner_bias,
            grad_conv_state.reshape(conv_state.shape),
            grad_conv_state_bias.reshape(conv_state_bias.shape),
            grad_step_bias,
            grad_decay_log,
            grad_skip,
            grad_norm_out,
            grad_out_weight,
        ),
        "seq",
    )
    return (output, grad_tokens) + tuple(summed)


def solution(mesh):
    return jax.shard_map(
        on_device,
        mesh=mesh,
        in_specs=(
            P(None, "seq", None),
            P(None, "seq"),
            P(),
            P(None, None, "head"),
            P(None, None, "head"),
            P(None, "head"),
            P(None, "head"),
            P("head"),
            P(None, None, "head"),
            P(None, "head"),
            P("head"),
            P("head"),
            P("head"),
            P("head"),
            P("head", None),
            P(None, "seq", None),
        ),
        out_specs=(
            P(None, "seq", "head"),
            P(None, "seq", "head"),
            P("head"),
            P(None, None, "head"),
            P(None, None, "head"),
            P(None, "head"),
            P(None, "head"),
            P("head"),
            P(None, None, "head"),
            P(None, "head"),
            P("head"),
            P("head"),
            P("head"),
            P("head"),
            P("head", None),
        ),
        check_vma=False,
    )
```

profile of v0, /device:TPU:0, one launch (start us, length us, event | category | flops | bytes accessed | tf_op | source)
XLA Modules:
  0.0 1068.2 jit_solution(12792381649834675468)
XLA Ops:
  35.8 16.2 %all_gather.21 = bf16[1,1024,2,128]{1,2,0,3:T(2,128)(2,1)S(1)} all-gather(bf16[1,1024,2,32]{1,2,0,3:T(2,128)(2,1)S(1)} %copy.317), channel_id=1, replica_groups=mesh['seq'=8,'head'=4] {'head'}, dimensions={3}, use_global_device_ids=true | all-gather | bytes 655360 | tf_op jit(solution)/shard_map/all_gather | solution.py:215
  70.9 186.5 %while.113 = (s32[]{:T(128)}, f32[1,6,64,128]{3,2,1,0:T(8,128)S(1)}, f32[4,1,256,6,64]{2,0,4,3,1:T(4,128)}, pred[4,1,256,256,6]{3,2,4,1,0:T(32,128)(4,1)}, f32[4...) while((s32[]{:T(128)}, f32[1,6,64,128]{3,2,1,0:T(8,128)S(1)}, ...), condition=%wide.region_6.7_spmd.clone.clone, body=%wide.region_1.6_spmd.clone.clone.sunk | while | flops 709979648 | bytes 17954120 | solution.py:136
  90.1 9.5 dynamic_update_slice.273
  136.8 9.5 dynamic_update_slice.273
  183.4 9.5 dynamic_update_slice.273
  230.0 9.5 dynamic_update_slice.273
  263.4 12.1 %all-reduce.13 = f32[48]{0:T(128)S(1)} all-reduce(f32[48]{0:T(128)S(1)} %multiply_dynamic-update-slice_fusion.1), channel_id=2, replica_groups=mesh['seq'=8,'head'=4] {'seq'}, use_global_device_ids=true, to_apply=%add.13 | all-reduce | flops 48 | bytes 384
  296.6 12.5 %psum.105 = f32[1,1024]{1,0:T(1,128)S(1)} all-reduce(f32[1,1024]{1,0:T(1,128)S(1)} %bitcast.968), channel_id=1, replica_groups=mesh['seq'=8,'head'=4] {'head'}, use_global_device_ids=true, to_apply=%region_16.17 | all-reduce | flops 1024 | bytes 8192 | tf_op jit(solution)/shard_map/psum | solution.py:246
  362.6 8.5 copy.331
  390.9 276.4 %while.112 = (s32[]{:T(128)}, f32[6]{0:T(128)}, f32[1,6,64,128]{3,2,1,0:T(8,128)}, f32[4,1,256,6,64]{2,0,4,3,1:T(4,128)}, f32[4,1,256,6]{2,3,1,0:T(8,128)}, /*in...) while((s32[]{:T(128)}, f32[6]{0:T(128)}, ...), condition=%wide.region_33.34_spmd.clone, body=%wide.region_22.33_spmd.clone.sunk | while | flops 1414818816 | bytes 28193976 | solution.py:136
  417.0 8.8 reduce-window.102
  437.1 9.5 dynamic_update_slice.260
  485.7 8.8 reduce-window.102
  505.7 9.5 dynamic_update_slice.260
  554.9 8.8 reduce-window.102
  575.0 9.5 dynamic_update_slice.260
  624.2 8.8 reduce-window.102
  644.3 9.5 dynamic_update_slice.260
  691.9 45.1 %all-reduce.25.cloned.1.call-done = f32[1,1024,2,128]{1,2,0,3:T(2,128)} async-done(((f32[1,1024,2,128]{1,2,0,3:T(2,128)}), f32[1,1024,2,128]{1,2,0,3:T(2,128)}) %all-reduce.25.cloned.1.call-update) | async-done | bytes 1048592
  753.3 8.6 copy.364
  769.9 10.2 all-reduce.17
  780.1 24.1 %all-reduce.18 = (f32[192]{0:T(256)}, f32[768,6]{0,1:T(8,128)}, f32[4,384]{1,0:T(4,128)}, f32[384]{0:T(512)}, f32[4,2,32]{2,1,0:T(2,128)}, /*index=5*/f32[2,32]{...) all-reduce(f32[192]{0:T(256)S(1)} %dynamic-slice.8, ...), channel_id=1, replica_groups=mesh['seq'=8,'head'=4] {'seq'}, use_global_device_ids=true, to_apply=%region_43.44 | all-reduce | flops 7442 | bytes 59536 | tf_op jit(solution)/shard_map/psum | solution.py:340
  804.2 18.7 %all-reduce.27.cloned.1.call-done = (f32[768,2,384]{2,0,1:T(8,128)}, f32[768,2,32]{0,2,1:T(8,128)}, f32[384,768]{1,0:T(8,128)}) async-done(((f32[768,2,384]{2,0,1:T(8,128)}, f32[768,2,32]{0,2,1:T(8,128)}, f32[384,768]{1,0:T(8,128)}), (f32[768,2,384]{2,0,1:T(8,128)}, f32[768,2,32]{0,2,1:T(8,128)}, f32[384,768]{1,0:T(8,128)})) %all-reduce.27.cloned.1.call-update) | async-done | bytes 3735568 | tf_op jit(solution)/shard_map/psum | solution.py:340
  827.8 220.8 %all-reduce.29.cloned.1.call-done = (f32[1,1024,768]{1,0,2:T(1,128)}, f32[1,1024,768]{1,0,2:T(1,128)}) async-done(((f32[1,1024,768]{1,0,2:T(1,128)}, f32[1,1024,768]{1,0,2:T(1,128)}), (f32[1,1024,768]{1,0,2:T(1,128)}, f32[1,1024,768]{1,0,2:T(1,128)})) %all-reduce.29.cloned.1.call-update) | async-done | bytes 6291472
  (825 shorter events, 564.7 us)
Async XLA Ops:
  7.2 305.0 %copy-start = (bf16[1,1024,768]{2,1,0:T(8,128)(2,1)S(1)}, bf16[1,1024,768]{2,1,0:T(8,128)(2,1)}, u32[]{:S(2)}) copy-start(bf16[1,1024,768]{2,1,0:T(8,128)(2,1)} %param.39) | copy-start | bytes 4718596
  7.2 282.5 %all-gather.6.cloned.1.call-start = ((), (), s32[]{:S(2)}) async-start(), calls=%async_computation | async-start | bytes 1769472 | tf_op jit(solution)/shard_map/all_gather | solution.py:25
  8.1 50.0 %copy-start.38 = (f32[1,1024]{1,0:T(1,128)}, f32[1,1024]{1,0:T(1,128)S(1)}, u32[]{:S(2)}) copy-start(f32[1,1024]{1,0:T(1,128)S(1)} %convert_subtract_fusion) | copy-start | bytes 12292
  11.1 18.0 %copy-start.55 = (f32[1024]{0:T(1024)}, f32[1024]{0:T(1024)S(1)}, u32[]{:S(2)}) copy-start(f32[1024]{0:T(1024)S(1)} %get-tuple-element.2220) | copy-start | bytes 12292
  17.2 39.6 %collective-permute-start = (bf16[1,3,384]{2,1,0:T(4,128)(2,1)}, bf16[1,3,384]{2,1,0:T(4,128)(2,1)}, u32[]{:S(2)}, u32[]{:S(2)}) collective-permute-start(bf16[1,3,384]{2,1,0:T(4,128)(2,1)} %slice_multiply_fusion.1), channel_id=1, source_target_pairs={{0,4},{4,8},{8,12},{12,16},{16,20},{20,24},{24,28},{1,5},{5,9},{9,... | collective-permute-start | bytes 6920 | tf_op jit(solution)/shard_map/ppermute | solution.py:18
  21.6 11.4 %collective-permute-start.1 = (bf16[1,3,64]{1,2,0:T(8,128)(2,1)}, bf16[1,3,64]{1,2,0:T(8,128)(2,1)}, u32[]{:S(2)}, u32[]{:S(2)}) collective-permute-start(bf16[1,3,64]{1,2,0:T(8,128)(2,1)} %slice_multiply_fusion), channel_id=1, source_target_pairs={{0,4},{4,8},{8,12},{12,16},{16,20},{20,24},{24,28},{1,5},{5,9},{9,... | collective-permute-start | bytes 1160 | tf_op jit(solution)/shard_map/ppermute | solution.py:18
  26.4 31.7 %copy-start.58 = (f32[384]{0:T(512)}, f32[384]{0:T(512)S(1)}, u32[]{:S(2)}) copy-start(f32[384]{0:T(512)S(1)} %get-tuple-element.1978) | copy-start | bytes 4612
  26.4 31.7 %copy-start.60 = (f32[384]{0:T(512)}, f32[384]{0:T(512)S(1)}, u32[]{:S(2)}) copy-start(f32[384]{0:T(512)S(1)} %get-tuple-element.1979) | copy-start | bytes 4612
  26.4 31.7 %copy-start.62 = (f32[384]{0:T(512)}, f32[384]{0:T(512)S(1)}, u32[]{:S(2)}) copy-start(f32[384]{0:T(512)S(1)} %get-tuple-element.1980) | copy-start | bytes 4612
  26.4 31.7 %copy-start.64 = (f32[384]{0:T(512)}, f32[384]{0:T(512)S(1)}, u32[]{:S(2)}) copy-start(f32[384]{0:T(512)S(1)} %get-tuple-element.1981) | copy-start | bytes 4612
  29.1 29.1 %copy-start.45 = (f32[1,1024]{1,0:T(1,128)}, f32[1,1024]{1,0:T(1,128)S(1)}, u32[]{:S(2)}) copy-start(f32[1,1024]{1,0:T(1,128)S(1)} %get-tuple-element.2175) | copy-start | bytes 12292
  29.1 29.1 %copy-start.47 = (f32[1,1024]{1,0:T(1,128)}, f32[1,1024]{1,0:T(1,128)S(1)}, u32[]{:S(2)}) copy-start(f32[1,1024]{1,0:T(1,128)S(1)} %get-tuple-element.2176) | copy-start | bytes 12292
  33.9 19.6 %copy-start.11 = (f32[1,1027,64]{1,2,0:T(8,128)}, f32[1,1027,64]{1,2,0:T(8,128)S(1)}, u32[]{:S(2)}) copy-start(f32[1,1027,64]{1,2,0:T(8,128)S(1)} %maximum_convert_fusion.1) | copy-start | bytes 788740
  258.0 120.7 %all-gather.8.cloned.1.call-start = ((), (), s32[]{:S(2)}) async-start(), calls=%async_computation.1 | async-start | bytes 1769472 | tf_op jit(solution)/shard_map/all_gather | solution.py:25
  338.7 398.4 %all-reduce.25.cloned.1.call-start = ((), (), s32[]{:S(2)}) async-start(), calls=%async_computation.2 | async-start | bytes 2097152
  680.4 5.8 collective-permute-start.2
  686.1 136.9 %all-reduce.27.cloned.1.call-start = ((), (), s32[]{:S(2)}) async-start(), calls=%async_computation.3 | async-start | bytes 7471104 | tf_op jit(solution)/shard_map/psum | solution.py:340
  691.9 46.2 %copy-start.12 = (f32[1,1027,64]{1,2,0:T(8,128)S(1)}, f32[1,1027,64]{1,2,0:T(8,128)}, u32[]{:S(2)}) copy-start(f32[1,1027,64]{1,2,0:T(8,128)} %copy-done.11) | copy-start | bytes 788740
  691.9 47.7 %copy-start.82 = (f32[64]{0:T(128)S(1)}, f32[64]{0:T(128)}, u32[]{:S(2)}) copy-start(f32[64]{0:T(128)} %copy-done.81) | copy-start | bytes 772
  691.9 47.7 %copy-start.83 = (f32[64]{0:T(128)S(1)}, f32[64]{0:T(128)}, u32[]{:S(2)}) copy-start(f32[64]{0:T(128)} %mul.1314) | copy-start | bytes 772
  691.9 47.7 %copy-start.84 = (f32[64]{0:T(128)S(1)}, f32[64]{0:T(128)}, u32[]{:S(2)}) copy-start(f32[64]{0:T(128)} %mul.1319) | copy-start | bytes 772
  691.9 47.7 %copy-start.86 = (f32[64]{0:T(128)S(1)}, f32[64]{0:T(128)}, u32[]{:S(2)}) copy-start(f32[64]{0:T(128)} %copy-done.85) | copy-start | bytes 772
  740.0 3.1 collective-permute-start.3
  744.6 304.1 %all-reduce.29.cloned.1.call-start = ((), (), s32[]{:S(2)}) async-start(), calls=%async_computation.4 | async-start | bytes 12582912
  (116 other events, 491.2 us)
Sparse Core Ops, SparseCore 0:
  258.2 26.2 all-gather.5
  338.8 28.7 all-gather.7
  686.2 50.8 all-reduce.24
  744.7 78.2 all-reduce.26
  825.3 223.2 all-reduce.28
where the time goes:
time: 1080 us; the launch traced here: 1070 us
  local copies, waits for them, and re-layouts  316 us (29%)
  waiting for transfers between devices  286 us (26%)
  other arithmetic  199 us (18%)
  matrix products  150 us (14%)
  blocking collectives  83.4 us (8%)
  between operations  19.1 us (2%)
    unnamed x7, waiting for transfers between devices  266 us
    dynamic_update_slice x60, local copies, waits for them, and re-layouts, local_row(): final_state, outputs = lax.scan(advance, initial, pieces)  137 us
    another operation x55, other arithmetic  65.1 us
    dot_general x12, matrix products, group_core(): inside = jnp.einsum('ijh,jhp->ihp', mixing, inputs, precision=HIGHEST)  45.2 us
    dynamic_update_slice x24, other arithmetic, local_row(): final_state, outputs = lax.scan(advance, initial, pieces)  36.9 us
    another operation x74, local copies, waits for them, and re-layouts  32.6 us
    dynamic_slice x40, local copies, waits for them, and re-layouts, local_row(): final_state, outputs = lax.scan(advance, initial, pieces)  32 us
    unnamed x187, local copies, waits for them, and re-layouts  31.8 us
  transfers between devices with their start and end apart: 9, of which 4 were waited for; matrix products, arithmetic and copies ran while one was open for 10% of the time, Pallas kernels for 0%

commit v1 on v0

v1 whole, which is shorter than its diff:
```python
import functools

import jax
import jax.numpy as jnp
from jax import lax
from jax.experimental import pallas as pl
from jax.experimental.pallas import tpu as pltpu
from jax.sharding import PartitionSpec as P

K = 4
GROUP = 256
DI = 1536
WIDTH = 64
LANES = 128
EDGE = 16
EPSILON = 1e-05
HIGHEST = lax.Precision.HIGHEST
F32 = jnp.float32
BF16 = jnp.bfloat16
FAR = -1e30
PARAMS = pltpu.CompilerParams(
    dimension_semantics=("arbitrary", "arbitrary"), vmem_limit_bytes=50 * 2**20
)


def rounded(tensor):
    return tensor.astype(BF16)


def dot(a, b, exact=False):
    return jnp.dot(a, b, preferred_element_type=F32, precision=HIGHEST if exact else None)


def dot_nt(a, b, exact=False):
    return lax.dot_general(
        a, b, (((1,), (1,)), ((), ())), preferred_element_type=F32,
        precision=HIGHEST if exact else None,
    )


def dot_tn(a, b, exact=False):
    return lax.dot_general(
        a, b, (((0,), (0,)), ((), ())), preferred_element_type=F32,
        precision=HIGHEST if exact else None,
    )


def iota(shape, dim):
    return lax.broadcasted_iota(jnp.int32, shape, dim)


def halves(tensor):
    high = rounded(tensor)
    return high, rounded(tensor - high.astype(F32))


def expand(tensor, channels):
    both = jnp.concatenate(halves(tensor), axis=1)
    table = iota((2 * LANES, channels), 1) // WIDTH == iota((2 * LANES, channels), 0) % LANES
    return dot(both, table.astype(F32).astype(BF16))


def collect(tensor):
    channels = tensor.shape[1]
    table = iota((channels, LANES), 0) // WIDTH == iota((channels, LANES), 1)
    table = table.astype(F32).astype(BF16)
    high, low = halves(tensor)
    return dot(high, table) + dot(low, table)


def expand_row(row, channels):
    return expand(jnp.broadcast_to(row, (8, LANES)), channels)[:1]


def collect_row(row):
    return collect(jnp.broadcast_to(row, (8, row.shape[1])))[:1]


def triangle(compare):
    return compare(iota((GROUP, GROUP), 0), iota((GROUP, GROUP), 1)).astype(F32).astype(BF16)


def running_counts(marked):
    return dot(marked.astype(BF16), triangle(lambda i, j: i <= j))


def fade_of(cum, counts):
    return jnp.exp(cum[GROUP - 1 :, :]) * (counts[:1, GROUP - 1 :] == 0).astype(F32)


def pack_state(ref, state, fade):
    ref[:LANES, :] = state
    ref[LANES:, :] = jnp.broadcast_to(fade, (8, fade.shape[1]))


def fold_states(pieces):
    state = jnp.zeros((LANES, pieces[0].shape[1]), F32)
    for piece in reversed(pieces):
        state = piece[LANES : LANES + 1, :] * state + piece[:LANES, :]
    return state


def rms_scale(tokens):
    return lax.rsqrt(jnp.mean(tokens * tokens, axis=-1, keepdims=True) + EPSILON)


def head_parts(channels):
    for start in range(0, channels, LANES):
        width = min(LANES, channels - start)
        yield start, width, [start // WIDTH + i for i in range(width // WIDTH)]


def project_kernel(tok, gain, win, wst, hp, normed, xpre, gate, spre, step, cum):
    channels = xpre.shape[-1]
    tokens = tok[...].astype(F32)
    row = rounded(tokens * rms_scale(tokens) * gain[...])
    normed[...] = row
    product = dot(row, win[...])
    xpre[...] = rounded(product[:, :channels])
    gate[...] = product[:, channels:]
    raw = dot(row, wst[...]) + hp[0:1, :]
    sizes = jax.nn.softplus(raw)
    spre[...] = raw
    step[...] = sizes
    rates = sizes * -jnp.exp(hp[1:2, :])
    lower = triangle(lambda i, j: i >= j)
    high, rest = rounded(rates), rates - rounded(rates).astype(F32)
    middle, low = halves(rest)
    cum[...] = dot(lower, high) + dot(lower, middle) + dot(lower, low)


def convolve(ext, taps, runs):
    summed = taps[K : K + 1, :] + taps[K - 1 : K, :] * ext[pl.ds(EDGE, GROUP), :]
    for lag in range(1, K):
        summed = summed + (
            taps[K - 1 - lag : K - lag, :] * ext[pl.ds(EDGE - lag, GROUP), :]
        ) * runs[lag - 1]
    return summed


def edge_rows(halo, gain, width):
    tokens = halo[:, :width].astype(F32)
    return tokens, rounded(tokens * rms_scale(tokens) * gain[...])


def forward_kernel(count, *refs):
    pieces = refs[:count]
    (
        marked, normed, xpre, step, cum, win, halo, gain, ci,
        yin, xact, bc, spre, fresh, fades, message, halo_x, halo_s, run_out, ws, cs,
        ext_x, ext_s, ext_k, state, total,
    ) = refs[count:]
    group = pl.program_id(1)
    channels = xpre.shape[-1]
    width = normed.shape[-1]
    own = pieces[0].shape[0] // 2

    @pl.when((group == 0) & (pl.program_id(0) == 0))
    def _():
        for place, piece in enumerate(pieces):
            for kind in range(2):
                row = (kind * count + place) * own
                ws[row : row + own, :] = piece[kind * own : (kind + 1) * own, :width]
        taps = jnp.concatenate(
            [p[kind * own : (kind + 1) * own, width:] for kind in range(2) for p in pieces], axis=0
        )
        cs[...] = taps.astype(F32).T[:8]

    @pl.when(group == 0)
    def _():
        _, row = edge_rows(halo, gain, width)
        edge_x = rounded(dot(row, win[:, :channels]))
        edge_s = rounded(dot_nt(row, ws[...]))
        halo_x[...] = edge_x
        halo_s[...] = edge_s
        ext_x[pl.ds(0, EDGE), :] = edge_x.astype(F32)
        ext_s[pl.ds(0, EDGE), :] = edge_s.astype(F32)
        ext_k[pl.ds(0, EDGE), :] = 1.0 - halo[:, width:].astype(F32)
        state[...] = jnp.zeros_like(state)
        total[...] = jnp.ones_like(total)

    @pl.when(group > 0)
    def _():
        ext_x[pl.ds(0, EDGE), :] = ext_x[pl.ds(GROUP, EDGE), :]
        ext_s[pl.ds(0, EDGE), :] = ext_s[pl.ds(GROUP, EDGE), :]
        ext_k[pl.ds(0, EDGE), :] = ext_k[pl.ds(GROUP, EDGE), :]

    counts = running_counts(marked[...])
    counts_column = counts.T[:, :1]
    run1 = 1.0 - marked[...].T[:, :1]
    ext_k[pl.ds(EDGE, GROUP), :] = jnp.broadcast_to(run1, (GROUP, LANES))
    run2 = run1 * ext_k[pl.ds(EDGE - 1, GROUP), :1]
    run3 = run2 * ext_k[pl.ds(EDGE - 2, GROUP), :1]
    runs = (run1, run2, run3)
    lane = iota((GROUP, LANES), 1)
    run_out[...] = jnp.where(lane == 0, run1, jnp.where(lane == 1, run2, run3))
    state_pre = rounded(dot_nt(normed[...], ws[...]))
    spre[...] = state_pre
    ext_s[pl.ds(EDGE, GROUP), :] = state_pre.astype(F32)
    ext_x[pl.ds(EDGE, GROUP), :] = xpre[...].astype(F32)
    conv_x = convolve(ext_x, ci, runs)
    conv_s = convolve(ext_s, cs, runs)
    x = rounded(conv_x * jax.nn.sigmoid(conv_x))
    both = rounded(conv_s * jax.nn.sigmoid(conv_s))
    xact[...] = x
    bc[...] = both
    half = both.shape[1] // 2
    b, c = both[:, :half], both[:, half:]
    cums = cum[...]
    causal = iota((GROUP, GROUP), 0) >= iota((GROUP, GROUP), 1)
    mask = jnp.where(causal & (counts_column == counts[:1]), 0.0, FAR)
    scores = dot_nt(c, b)
    weighted = x.astype(F32) * expand(step[...], channels)
    scaled = rounded(weighted)
    cum_rows = cums.T
    for start, size, heads in head_parts(channels):
        part = scaled[:, start : start + size]
        results = []
        for head in heads:
            decay = jnp.exp(cums[:, head : head + 1] - cum_rows[head : head + 1, :] + mask)
            results.append(dot(rounded(scores * decay), part))
        if len(results) == 2:
            results = [jnp.where(iota((GROUP, size), 1) < WIDTH, results[0], results[1])]
        yin[:, start : start + size] = results[0]
    ending = (counts_column == counts[:1, GROUP - 1 :]).astype(F32)
    reach_end = jnp.exp(cums[GROUP - 1 :, :] - cums) * ending
    new = dot_tn(b, rounded(weighted * expand(reach_end, channels)))
    fresh[...] = new
    fade = expand_row(fade_of(cums, counts), channels)
    fades[...] = jnp.broadcast_to(fade, (8, channels))
    state[...] = fade * state[...] + new
    total[...] = total[...] * fade

    @pl.when(group == pl.num_programs(1) - 1)
    def _():
        pack_state(message, state[...], total[0:1, :])


def mix_kernel(count, *refs):
    pieces = refs[:count]
    (
        yin, x, c, gate, dn, cum, marked, gain, hp, fresh, fades,
        mixer, sums, states, state,
    ) = refs[count:]
    channels = x.shape[-1]

    @pl.when(pl.program_id(1) == 0)
    def _():
        state[...] = fold_states(pieces)

    counts = running_counts(marked[...])
    living = (counts.T[:, :1] == 0).astype(F32)
    now = state[...]
    states[...] = now
    reach = expand(jnp.exp(cum[...]) * living, channels)
    skip = expand_row(hp[2:3, :], channels)
    high, low = halves(now)
    reads = c[...]
    mixed = yin[...] + reach * (dot(reads, high) + dot(reads, low)) + skip * x[...].astype(F32)
    mixer[...] = mixed
    gates = gate[...]
    gated = mixed * (gates * jax.nn.sigmoid(gates))
    square = jnp.sum(gated * gated, axis=1, keepdims=True)
    cross = jnp.sum(gated * (dn[...] * gain[...]), axis=1, keepdims=True)
    lane = iota((GROUP, LANES), 1)
    sums[...] = jnp.where(lane == 0, square, cross).T[:8]
    state[...] = fades[0:1, :] * now + fresh[...]


def gate_kernel(count, *refs):
    pieces = refs[:count]
    (
        mixer, gate, dn, x, c, cum, marked, gain, hp, fades,
        dy, dgate, normed_out, entering, message, grad_gain, grad_skip, state, total,
    ) = refs[count:]
    channels = x.shape[-1]
    last = pl.program_id(1) == 0

    @pl.when(last & (pl.program_id(0) == 0))
    def _():
        grad_gain[...] = jnp.zeros_like(grad_gain)
        grad_skip[...] = jnp.zeros_like(grad_skip)

    @pl.when(last)
    def _():
        state[...] = jnp.zeros_like(state)
        total[...] = jnp.ones_like(total)

    sums = pieces[0][...]
    for piece in pieces[1:]:
        sums = sums + piece[...]
    columns = sums.T
    scale = lax.rsqrt(columns[:, 0:1] / DI + EPSILON)
    pull = scale * scale * scale * (columns[:, 1:2] / DI)
    counts = running_counts(marked[...])
    living = (counts.T[:, :1] == 0).astype(F32)
    mixed = mixer[...]
    gates = gate[...]
    squash = jax.nn.sigmoid(gates)
    act = gates * squash
    gated = mixed * act
    norm_grad = dn[...]
    grad_gated = scale * (norm_grad * gain[...]) - gated * pull
    down = grad_gated * act
    dy[...] = down
    dgate[...] = rounded(grad_gated * mixed * (squash * (1.0 + gates * (1.0 - squash))))
    scaled = gated * scale
    normed_out[...] = rounded(scaled * gain[...])
    grad_gain[...] += jnp.sum(norm_grad * scaled, axis=0, keepdims=True)
    grad_skip[...] += jnp.sum(down * x[...].astype(F32), axis=0, keepdims=True)
    reach = expand(jnp.exp(cum[...]) * living, channels)
    new = dot_tn(c[...], rounded(reach * down))
    entering[...] = new
    fade = fades[0:1, :]
    state[...] = fade * state[...] + new
    total[...] = total[...] * fade

    @pl.when(pl.program_id(1) == pl.num_programs(1) - 1)
    def _():
        pack_state(message, state[...], total[0:1, :])


def store_parts(refs, tensor, me):
    width = tensor.shape[1]
    own = width // len(refs)
    turned = rounded(pltpu.roll(tensor, (len(refs) - me) % len(refs) * own, 1))
    for part, ref in enumerate(refs):
        ref[...] = turned[:, part * own : (part + 1) * own]


def out_kernel(parts, me, normed_out, cot, dgate, normed, wout, win, gain, skip, back, grads, *branch):
    channels = wout.shape[0]
    width = wout.shape[1]

    @pl.when((pl.program_id(1) == 0) & (pl.program_id(0) == 0))
    def _():
        grads[...] = jnp.zeros_like(grads)
        grads[2 * channels : 2 * channels + 1, :channels] = gain[...]
        grads[2 * channels + 1 : 2 * channels + 2, :channels] = skip[...]

    store_parts(branch, dot(normed_out[...], wout[...]), me[0])
    grads[:channels, :] += dot_tn(normed_out[...], cot[...])
    grads[channels : 2 * channels, :] += dot_tn(dgate[...], normed[...])
    back[...] = dot_nt(dgate[...], win[:, channels:])


def token_grad(tokens, gain, down):
    scale = rms_scale(tokens)
    pulled = down * gain
    inner = jnp.mean(pulled * tokens, axis=-1, keepdims=True)
    grad = scale * pulled - tokens * (scale * scale * scale * inner)
    return grad, jnp.sum(down * tokens * scale, axis=0, keepdims=True)


def deconvolve(ext, buffers, taps, runs, grad_out, grad_taps):
    rows = GROUP + EDGE
    grad_taps[K : K + 1, :] += jnp.sum(grad_out, axis=0, keepdims=True)
    result = None
    for lag in range(K):
        masked = grad_out if lag == 0 else grad_out * runs[lag - 1]
        buffer = buffers.at[lag]
        buffer[pl.ds(EDGE, GROUP), :] = masked
        tap = K - 1 - lag
        grad_taps[tap : tap + 1, :] += jnp.sum(
            masked * ext[pl.ds(EDGE - lag, GROUP), :], axis=0, keepdims=True
        )
        piece = taps[tap : tap + 1, :] * buffer[pl.ds(lag, rows), :]
        result = piece if result is None else result + piece
        buffer[pl.ds(EDGE + GROUP, 8), :] = masked[:8]
    return rounded(result)


def swish_slope(tensor):
    squash = jax.nn.sigmoid(tensor)
    return squash * (1.0 + tensor * (1.0 - squash))


def backward_kernel(start_call, end_call, count, parts, *refs):
    pieces, refs = refs[:count], refs[count:]
    carried, refs = (refs[:0], refs) if start_call else (refs[:6], refs[6:])
    (
        me, tok, halo, marked, normed, xpre, xprev, halo_x, spre, sprev, halo_s, xact, bc, yin, dy,
        back, step, cum, raw, run_in, states, entering, fades, win, ws, wst, hp, ci, cs, gain,
    ), refs = refs[:30], refs[30:]
    gtok, refs = refs[:parts], refs[parts:]
    if end_call:
        (packed, *rest), refs = refs[: 1 + 2 * parts], refs[1 + 2 * parts :]
        edge_out, state_out = rest[:parts], rest[parts:]
    else:
        carry_out, refs = refs[:6], refs[6:]
    ext_x, ext_s, buf_x, buf_s, state, grad_x, grad_s, grad_misc, grad_ci, grad_cs = refs
    channels = xact.shape[-1]
    width = tok.shape[-1]
    half = bc.shape[-1] // 2
    order = pl.program_id(1)
    row_id = pl.program_id(0)
    closing = order == pl.num_programs(1) - 1
    sums = (grad_x, grad_s, grad_misc, grad_ci, grad_cs)

    @pl.when((order == 0) & (row_id == 0))
    def _():
        if start_call:
            for ref in sums:
                ref[...] = jnp.zeros_like(ref)
        else:
            grad_x[...] = carried[3][:channels]
            grad_s[...] = carried[3][channels : channels + 2 * half]
            grad_misc[...] = carried[3][channels + 2 * half :]
            grad_ci[...] = carried[4][...]
            grad_cs[...] = carried[5][...]

    @pl.when(order == 0)
    def _():
        for buf in (buf_x, buf_s):
            buf[...] = jnp.zeros_like(buf)
        if start_call:
            state[...] = fold_states(pieces)
        else:
            state[...] = carried[0][...]
            buf_x[:, pl.ds(EDGE + GROUP, 8), :] = carried[1][...]
            buf_s[:, pl.ds(EDGE + GROUP, 8), :] = carried[2][...]

    first_group = closing if end_call else False
    ext_x[pl.ds(EDGE, GROUP), :] = xpre[...].astype(F32)
    ext_s[pl.ds(EDGE, GROUP), :] = spre[...].astype(F32)
    before_x, before_s = xprev[...].astype(F32), sprev[...].astype(F32)
    if end_call:
        before_x = jnp.where(first_group, halo_x[...].astype(F32), before_x)
        before_s = jnp.where(first_group, halo_s[...].astype(F32), before_s)
    ext_x[pl.ds(0, EDGE), :] = before_x
    ext_s[pl.ds(0, EDGE), :] = before_s

    counts = running_counts(marked[...])
    counts_column = counts.T[:, :1]
    runs = [run_in[:, lag : lag + 1] for lag in range(K - 1)]
    living = (counts_column == 0).astype(F32)
    x = xact[...].astype(F32)
    both = bc[...]
    b, c = both[:, :half], both[:, half:]
    cums = cum[...]
    cum_rows = cums.T
    steps = step[...]
    step_wide = expand(steps, channels)
    weighted = x * step_wide
    scaled = rounded(weighted)
    down = dy[...]
    down_low = rounded(down)
    causal = iota((GROUP, GROUP), 0) <= iota((GROUP, GROUP), 1)
    mask = jnp.where(causal & (counts_column == counts[:1]), 0.0, FAR)
    scores = dot_nt(b, c)
    grad_scores = jnp.zeros((GROUP, GROUP), F32)
    inside = []
    for start, size, heads in head_parts(channels):
        part = scaled[:, start : start + size]
        slope = down_low[:, start : start + size]
        lane = iota((GROUP, size), 1)
        results = []
        for place, head in enumerate(heads):
            decay = jnp.exp(cum_rows[head : head + 1, :] - cums[:, head : head + 1] + mask)
            results.append(dot(rounded(scores * decay), slope))
            own = part
            if len(heads) == 2:
                keep = (lane < WIDTH) if place == 0 else (lane >= WIDTH)
                own = jnp.where(keep, part, jnp.zeros_like(part))
            grad_scores = grad_scores + dot_nt(own, slope) * decay
        if len(results) == 2:
            results = [jnp.where(lane < WIDTH, results[0], results[1])]
        inside.append(results[0])
    inside = jnp.concatenate(inside, axis=1) if len(inside) > 1 else inside[0]

    later = state[...]
    later_high, later_low = halves(later)
    now = states[...]
    now_high, now_low = halves(now)
    ending = (counts_column == counts[:1, GROUP - 1 :]).astype(F32)
    reach_end = expand(jnp.exp(cums[GROUP - 1 :, :] - cums) * ending, channels)
    reach = expand(jnp.exp(cums) * living, channels)
    arriving = reach_end * (dot(b, later_high) + dot(b, later_low))
    grad_weighted = inside + arriving
    reached = reach * down
    outside = reached * (dot(c, now_high) + dot(c, now_low))
    fade = fades[0:1, :]
    fade_grad = collect_row(fade * jnp.sum(later * now, axis=0, keepdims=True))
    per_position = collect(
        down_low.astype(F32) * yin[...] - scaled.astype(F32) * inside + outside
    )
    per_ending = collect(weighted * arriving)
    direct = collect(x * grad_weighted)
    position_high, position_low = halves(per_position)
    ending_high, ending_low = halves(per_ending)
    upper = triangle(lambda i, j: i <= j)
    under = triangle(lambda i, j: i > j)
    grad_rate = (
        dot(upper, position_high) + dot(upper, position_low)
        + dot(under, ending_high) + dot(under, ending_low) + fade_grad
    )
    rate = -jnp.exp(hp[1:2, :])
    grad_pre = (direct + rate * grad_rate) * jax.nn.sigmoid(raw[...])
    grad_raw = rounded(grad_pre)
    skip = expand_row(hp[2:3, :], channels)
    grad_inputs = step_wide * grad_weighted + skip * down
    low_scores = rounded(grad_scores)
    ended = rounded(weighted * reach_end)
    reached_low = rounded(reached)
    grad_b = dot(low_scores, c) + dot_nt(ended, later_high) + dot_nt(ended, later_low)
    grad_c = dot_tn(low_scores, b) + dot_nt(reached_low, now_high) + dot_nt(reached_low, now_low)
    state[...] = fade * later + entering[...]

    conv_x = convolve(ext_x, ci, runs)
    grad_x_out = grad_inputs * swish_slope(conv_x)
    conv_s = convolve(ext_s, cs, runs)
    grad_s_out = jnp.concatenate([grad_b, grad_c], axis=1) * swish_slope(conv_s)
    back_x = deconvolve(ext_x, buf_x, ci, runs, grad_x_out, grad_ci)
    back_s = deconvolve(ext_s, buf_s, cs, runs, grad_s_out, grad_cs)
    row = normed[...]
    main_x, main_s = back_x[EDGE:], back_s[EDGE:]
    grad_x[...] += dot_tn(main_x, row)
    grad_s[...] += dot_tn(main_s, row)
    grad_normed = (
        back[...] + dot_nt(main_x, win[:, :channels]) + dot(main_s, ws[...])
        + dot_nt(grad_raw, wst[...])
    )
    grad, gain_part = token_grad(tok[...].astype(F32), gain[...], grad_normed)
    grad_misc[0:8, :] += dot_tn(grad_raw, row)[:8]
    grad_misc[8:9, :] += gain_part
    grad_misc[9:10, :LANES] += jnp.sum(grad_pre, axis=0, keepdims=True)
    grad_misc[10:11, :LANES] += rate * jnp.sum(steps * grad_rate, axis=0, keepdims=True)
    store_parts(gtok, grad, me[0])

    if not end_call:
        @pl.when(closing)
        def _():
            carry_out[0][...] = state[...]
            carry_out[1][...] = buf_x[:, pl.ds(EDGE + GROUP, 8), :]
            carry_out[2][...] = buf_s[:, pl.ds(EDGE + GROUP, 8), :]

            @pl.when(row_id == pl.num_programs(0) - 1)
            def _():
                carry_out[3][:channels] = grad_x[...]
                carry_out[3][channels : channels + 2 * half] = grad_s[...]
                carry_out[3][channels + 2 * half :] = grad_misc[...]
                carry_out[4][...] = grad_ci[...]
                carry_out[5][...] = grad_cs[...]
        return

    @pl.when(closing)
    def _():
        tokens, edge_row = edge_rows(halo, gain, width)
        edge_x, edge_s = back_x[:EDGE], back_s[:EDGE]
        grad_x[...] += dot_tn(edge_x, edge_row)
        grad_s[...] += dot_tn(edge_s, edge_row)
        edge_grad = dot_nt(edge_x, win[:, :channels]) + dot(edge_s, ws[...])
        grad, gain_part = token_grad(tokens, gain[...], edge_grad)
        grad_misc[8:9, :] += gain_part
        everything = grad_misc[8:9, :]
        high = everything.astype(BF16).astype(F32)
        place = iota((EDGE, 1), 0)
        final = row_id == pl.num_programs(0) - 1
        nothing = jnp.zeros_like(high)
        high, rest = jnp.where(final, high, nothing), jnp.where(final, everything - high, nothing)
        edge = jnp.where(place == 0, high, jnp.where(place == 1, rest, grad))
        store_parts(edge_out, edge, me[0])

        @pl.when(final)
        def _():
            def padded(block):
                if block.shape[1] == width:
                    return block
                blank = jnp.zeros((8, width - block.shape[1]), F32)
                return jnp.concatenate([block, blank], axis=1)

            def both_halves(block):
                whole = padded(block)
                upper_half = whole.astype(BF16).astype(F32)
                return rounded(jnp.concatenate([upper_half, whole - upper_half], axis=0))

            packed[:channels, :] = rounded(grad_x[...])
            packed[channels : channels + EDGE, :] = rounded(grad_misc[...])
            packed[channels + EDGE : channels + 2 * EDGE, :] = both_halves(grad_ci[...])
            own = half // parts
            taps = grad_cs[...]
            for part, ref in enumerate(state_out):
                lo, hi = part * own, (part + 1) * own
                ref[:own, :] = rounded(grad_s[lo:hi, :])
                ref[own : 2 * own, :] = rounded(grad_s[half + lo : half + hi, :])
                ref[2 * own :, :] = both_halves(
                    jnp.concatenate([taps[:, lo:hi], taps[:, half + lo : half + hi]], axis=1)
                )


def ring(axis, distance):
    count = lax.axis_size(axis)
    return [(i, (i + distance) % count) for i in range(count)]


def shifted(block, axis, distance):
    devices = range(lax.axis_size(axis))
    return lax.ppermute(block, axis, [(i - distance, i) for i in devices if i - distance in devices])


def passed_on(parts, axis):
    total = parts[0].astype(F32)
    for distance, part in enumerate(parts[1:], 1):
        total = total + lax.ppermute(part, axis, ring(axis, distance)).astype(F32)
    return total


def all_sum(whole, axis):
    count = lax.axis_size(axis)
    chunk = whole.shape[0] // count
    parts = lax.all_to_all(whole.reshape(count, chunk, -1), axis, 0, 0, tiled=True)
    own = rounded(jnp.sum(parts.astype(F32), axis=0))
    return lax.all_gather(own, axis, axis=0, tiled=True).astype(F32)


def on_device(
    tokens, starts, norm_in_gain, inner_weight, state_weight, step_weight, conv_inner,
    conv_inner_bias, conv_state, conv_state_bias, step_bias, decay_log, skip_gain,
    norm_out_gain, out_weight, cotangent,
):
    rows, length, width = tokens.shape
    head_count = step_weight.shape[1]
    channels = inner_weight.shape[2]
    own_state = state_weight.shape[2]
    seq_count, head_devices = lax.axis_size("seq"), lax.axis_size("head")
    groups = length // GROUP
    grid = (rows, groups)
    states = 2 * own_state * head_devices
    own_width = width // head_devices
    me = lax.axis_index("head").reshape(1)

    def sds(shape, dtype=F32):
        return jax.ShapeDtypeStruct(shape, dtype)

    def whole(shape):
        return pl.BlockSpec(shape, lambda r, g: (0,) * len(shape))

    def place(g, reverse):
        return groups - 1 - g if reverse else g

    def block(cols, reverse=False, part=0):
        return pl.BlockSpec((None, GROUP, cols), lambda r, g: (r, place(g, reverse), part))

    def per_row(height, cols):
        return pl.BlockSpec((None, height, cols), lambda r, g: (r, 0, 0))

    def per_group(height, cols, reverse=False):
        return pl.BlockSpec(
            (None, None, height, cols), lambda r, g: (r, place(g, reverse), 0, 0)
        )

    scalar = pl.BlockSpec(memory_space=pltpu.SMEM)
    halo_width = width + LANES
    tail = jnp.concatenate(
        [
            tokens[:, length - EDGE :],
            jnp.broadcast_to(starts[:, length - EDGE :, None], (rows, EDGE, LANES)).astype(BF16),
        ],
        axis=2,
    )
    halo = shifted(tail, "seq", 1)
    state_own = jnp.concatenate(
        [
            state_weight, conv_state, conv_state_bias[None],
            jnp.zeros((LANES - K - 1, 2, own_state), BF16),
        ],
        axis=0,
    ).transpose(1, 2, 0).reshape(2 * own_state, width + LANES)
    found = [state_own] + [
        lax.ppermute(state_own, "head", ring("head", d)) for d in range(1, head_devices)
    ]

    gain_in = norm_in_gain[None]
    gain_out = norm_out_gain[None]
    win = inner_weight.reshape(width, 2 * channels)
    wst = jnp.pad(step_weight, ((0, 0), (0, LANES - head_count)))
    hp = jnp.pad(
        jnp.stack([step_bias, decay_log, skip_gain]), ((0, 5), (0, LANES - head_count))
    )
    ci = jnp.pad(
        jnp.concatenate([conv_inner, conv_inner_bias[None]], axis=0).astype(F32), ((0, 3), (0, 0))
    )
    marked = jnp.broadcast_to(
        starts.astype(F32).reshape(rows, groups, 1, GROUP), (rows, groups, 8, GROUP)
    )

    def act(cols, dtype=F32):
        return sds((rows, length, cols), dtype)

    normed, xpre, gate, raw, step, cum = pl.pallas_call(
        project_kernel,
        grid=grid,
        in_specs=[
            block(width), whole((1, width)), whole((width, 2 * channels)),
            whole((width, LANES)), whole((8, LANES)),
        ],
        out_specs=[
            block(width), block(channels), block(channels), block(LANES), block(LANES),
            block(LANES),
        ],
        out_shape=[
            act(width, BF16), act(channels, BF16), act(channels), act(LANES), act(LANES),
            act(LANES),
        ],
        compiler_params=PARAMS,
        name="project",
    )(tokens, gain_in, win, wst, hp)
    dn = jnp.einsum("rsd,cd->rsc", cotangent, out_weight, preferred_element_type=F32)

    (
        yin, xact, bc, spre, fresh, fades, message, halo_x, halo_s, run_all, ws, cs,
    ) = pl.pallas_call(
        functools.partial(forward_kernel, len(found)),
        grid=grid,
        in_specs=[whole((2 * own_state, width + LANES))] * len(found) + [
            per_group(8, GROUP), block(width), block(channels), block(LANES), block(LANES),
            whole((width, 2 * channels)), per_row(EDGE, halo_width), whole((1, width)),
            whole((8, channels)),
        ],
        out_specs=[
            block(channels), block(channels), block(states), block(states),
            per_group(LANES, channels), per_group(8, channels), per_row(LANES + 8, channels),
            per_row(EDGE, channels), per_row(EDGE, states), block(LANES),
            whole((states, width)), whole((8, states)),
        ],
        out_shape=[
            act(channels), act(channels, BF16), act(states, BF16), act(states, BF16),
            sds((rows, groups, LANES, channels)), sds((rows, groups, 8, channels)),
            sds((rows, LANES + 8, channels)), sds((rows, EDGE, channels), BF16),
            sds((rows, EDGE, states), BF16), act(LANES), sds((states, width), BF16),
            sds((8, states)),
        ],
        scratch_shapes=[
            pltpu.VMEM((GROUP + EDGE, channels), F32), pltpu.VMEM((GROUP + EDGE, states), F32),
            pltpu.VMEM((GROUP + EDGE, LANES), F32),
            pltpu.VMEM((LANES, channels), F32), pltpu.VMEM((8, channels), F32),
        ],
        compiler_params=PARAMS,
        name="forward",
    )(*found, marked, normed, xpre, step, cum, win, halo, gain_in, ci)

    arrived = [shifted(message, "seq", d) for d in range(1, seq_count)]
    mixer, sums, entry_states = pl.pallas_call(
        functools.partial(mix_kernel, len(arrived)),
        grid=grid,
        in_specs=[per_row(LANES + 8, channels)] * len(arrived) + [
            block(channels), block(channels), block(states // 2, part=1), block(channels),
            block(channels), block(LANES), per_group(8, GROUP), whole((1, channels)),
            whole((8, LANES)), per_group(LANES, channels), per_group(8, channels),
        ],
        out_specs=[block(channels), per_group(8, GROUP), per_group(LANES, channels)],
        out_shape=[
            act(channels), sds((rows, groups, 8, GROUP)), sds((rows, groups, LANES, channels)),
        ],
        scratch_shapes=[pltpu.VMEM((LANES, channels), F32)],
        compiler_params=PARAMS,
        name="mix",
    )(*arrived, yin, xact, bc, gate, dn, cum, marked, gain_out, hp, fresh, fades)

    sums_all = [sums] + [
        lax.ppermute(sums, "head", ring("head", d)) for d in range(1, head_devices)
    ]
    dy, dgate, normed_out, entering, back_message, grad_gain_out, grad_skip = pl.pallas_call(
        functools.partial(gate_kernel, len(sums_all)),
        grid=grid,
        in_specs=[per_group(8, GROUP, True)] * len(sums_all) + [
            block(channels, True), block(channels, True), block(channels, True),
            block(channels, True), block(states // 2, True, 1), block(LANES, True),
            per_group(8, GROUP, True), whole((1, channels)), whole((8, LANES)),
            per_group(8, channels, True),
        ],
        out_specs=[
            block(channels, True), block(channels, True), block(channels, True),
            per_group(LANES, channels, True), per_row(LANES + 8, channels),
            whole((1, channels)), whole((1, channels)),
        ],
        out_shape=[
            act(channels), act(channels, BF16), act(channels, BF16),
            sds((rows, groups, LANES, channels)), sds((rows, LANES + 8, channels)),
            sds((1, channels)), sds((1, channels)),
        ],
        scratch_shapes=[pltpu.VMEM((LANES, channels), F32), pltpu.VMEM((8, channels), F32)],
        compiler_params=PARAMS,
        name="gate",
    )(*sums_all, mixer, gate, dn, xact, bc, cum, marked, gain_out, hp, fades)

    returned = [shifted(back_message, "seq", -d) for d in range(1, seq_count)]
    back, early, *branch = pl.pallas_call(
        functools.partial(out_kernel, head_devices),
        grid=grid,
        in_specs=[
            scalar, block(channels), block(width), block(channels), block(width),
            whole((channels, width)), whole((width, 2 * channels)), whole((1, channels)),
            whole((1, channels)),
        ],
        out_specs=[block(width), whole((2 * channels + 8, width))]
        + [block(own_width)] * head_devices,
        out_shape=[act(width), sds((2 * channels + 8, width))]
        + [act(own_width, BF16)] * head_devices,
        compiler_params=PARAMS,
        name="out",
    )(me, normed_out, cotangent, dgate, normed, out_weight, win, grad_gain_out, grad_skip)

    column = lax.axis_index("head") * own_width
    own_tokens = lax.dynamic_slice_in_dim(tokens, column, own_width, 2).astype(F32)
    output = rounded(own_tokens + passed_on(branch, "head"))
    early = lax.psum(early, "seq")

    late_rows = channels + 3 * EDGE + 2 * own_state + EDGE
    chunk = -(-late_rows // (seq_count * EDGE)) * EDGE
    packed_rows = channels + 2 * EDGE
    piece_rows = 2 * own_state + EDGE

    def backward_call(start_call, end_call, offset, steps, carried):
        step_size = GROUP // EDGE

        def at(g):
            return offset + steps - 1 - g

        def tile(cols):
            return pl.BlockSpec((None, GROUP, cols), lambda r, g: (r, at(g), 0))

        def before(cols):
            return pl.BlockSpec(
                (None, EDGE, cols), lambda r, g: (r, jnp.maximum(at(g) * step_size - 1, 0), 0)
            )

        def group_tile(height, cols):
            return pl.BlockSpec((None, None, height, cols), lambda r, g: (r, at(g), 0, 0))

        carry_specs = [
            per_row(LANES, channels),
            pl.BlockSpec((None, K, 8, channels), lambda r, g: (r, 0, 0, 0)),
            pl.BlockSpec((None, K, 8, states), lambda r, g: (r, 0, 0, 0)),
            whole((channels + states + EDGE, width)), whole((8, channels)), whole((8, states)),
        ]
        carry_shapes = [
            sds((rows, LANES, channels)), sds((rows, K, 8, channels)), sds((rows, K, 8, states)),
            sds((channels + states + EDGE, width)), sds((8, channels)), sds((8, states)),
        ]
        local = pl.BlockSpec((None, GROUP, own_width), lambda r, g: (r, steps - 1 - g, 0))
        out_specs = [local] * head_devices
        out_shape = [sds((rows, steps * GROUP, own_width), BF16)] * head_devices
        if end_call:
            out_specs += [whole((packed_rows, width))]
            out_specs += [per_row(EDGE, own_width)] * head_devices
            out_specs += [whole((piece_rows, width))] * head_devices
            out_shape += [sds((packed_rows, width), BF16)]
            out_shape += [sds((rows, EDGE, own_width), BF16)] * head_devices
            out_shape += [sds((piece_rows, width), BF16)] * head_devices
        else:
            out_specs += carry_specs
            out_shape += carry_shapes
        lead = returned if start_call else []
        return pl.pallas_call(
            functools.partial(backward_kernel, start_call, end_call, len(lead), head_devices),
            grid=(rows, steps),
            in_specs=[per_row(LANES + 8, channels)] * len(lead)
            + ([] if start_call else carry_specs)
            + [
                scalar, tile(width), per_row(EDGE, halo_width), group_tile(8, GROUP), tile(width),
                tile(channels), before(channels), per_row(EDGE, channels), tile(states),
                before(states), per_row(EDGE, states), tile(channels), tile(states),
                tile(channels), tile(channels), tile(width), tile(LANES), tile(LANES),
                tile(LANES), tile(LANES), group_tile(LANES, channels),
                group_tile(LANES, channels), group_tile(8, channels),
                whole((width, 2 * channels)), whole((states, width)), whole((width, LANES)),
                whole((8, LANES)), whole((8, channels)), whole((8, states)), whole((1, width)),
            ],
            out_specs=out_specs,
            out_shape=out_shape,
            scratch_shapes=[
                pltpu.VMEM((GROUP + EDGE, channels), F32),
                pltpu.VMEM((GROUP + EDGE, states), F32),
                pltpu.VMEM((K, GROUP + 2 * EDGE, channels), F32),
                pltpu.VMEM((K, GROUP + 2 * EDGE, states), F32),
                pltpu.VMEM((LANES, channels), F32),
                pltpu.VMEM((channels, width), F32), pltpu.VMEM((states, width), F32),
                pltpu.VMEM((EDGE, width), F32), pltpu.VMEM((8, channels), F32),
                pltpu.VMEM((8, states), F32),
            ],
            compiler_params=PARAMS,
            name="backward",
        )(
            *lead, *carried, me, tokens, halo, marked, normed, xpre, xpre, halo_x, spre, spre,
            halo_s, xact, bc, yin, dy, back, step, cum, raw, run_all, entry_states, entering,
            fades, win, ws, wst, hp, ci, cs, gain_in,
        )

    first = groups // 2
    if first:
        outs = backward_call(True, False, first, groups - first, [])
        token_sums = [passed_on(outs[:head_devices], "head")]
        outs = backward_call(False, True, 0, first, outs[head_devices:])
    else:
        token_sums = []
        outs = backward_call(True, True, 0, groups, [])
    gtok, packed = outs[:head_devices], outs[head_devices]
    edge_parts = outs[head_devices + 1 : 2 * head_devices + 1]
    state_parts = outs[2 * head_devices + 1 :]

    state_total = state_parts[0].astype(F32)
    for d in range(1, head_devices):
        state_total = state_total + lax.ppermute(
            state_parts[d], "head", ring("head", -d)
        ).astype(F32)
    edge = passed_on(edge_parts, "head")
    token_sums = [passed_on(gtok, "head")] + token_sums
    own_cot = lax.dynamic_slice_in_dim(cotangent, column, own_width, 2).astype(F32)
    from_next = shifted(edge, "seq", -1)[:, EDGE - K + 1 :]
    padding = jnp.zeros((rows, length - K + 1, own_width), F32)
    grad_tokens = (
        own_cot + jnp.concatenate(token_sums, axis=1)
        + jnp.concatenate([padding, from_next], axis=1)
    )
    gain_row = (edge[rows - 1, 0] + edge[rows - 1, 1])[None]
    gain_high = gain_row.astype(BF16).astype(F32)
    gain_rows = jnp.pad(
        jnp.concatenate([gain_high, gain_row - gain_high]),
        ((0, EDGE - 2), (0, width - own_width)),
    )
    taps = state_total[2 * own_state : 2 * own_state + 8] + state_total[2 * own_state + 8 :]
    taps_high = taps.astype(BF16).astype(F32)
    late = jnp.concatenate(
        [
            packed, rounded(state_total[: 2 * own_state]), rounded(taps_high),
            rounded(taps - taps_high), rounded(gain_rows),
            jnp.zeros((chunk * seq_count - late_rows, width), BF16),
        ],
        axis=0,
    )
    late = all_sum(late, "seq")

    def take(start, count):
        return late[start : start + count]

    grad_inner = jnp.stack([take(0, channels), early[channels : 2 * channels]]).transpose(2, 0, 1)
    misc = take(channels, EDGE)
    conv = take(channels + EDGE, 8) + take(channels + EDGE + 8, 8)
    base = packed_rows
    grad_state = take(base, 2 * own_state).reshape(2, own_state, width).transpose(2, 0, 1)
    base += 2 * own_state
    taps = (take(base, 8) + take(base + 8, 8))[: K + 1, : 2 * own_state]
    taps = taps.reshape(K + 1, 2, own_state)
    gain = take(base + EDGE, 1) + take(base + EDGE + 1, 1)
    skip = early[2 * channels + 1, :channels].reshape(head_count, WIDTH).sum(axis=1)
    return (
        output, grad_tokens, gain[0, :own_width], grad_inner, grad_state,
        misc[:head_count].T, conv[:K, :channels], conv[K, :channels], taps[:K], taps[K],
        misc[9, :head_count], misc[10, :head_count], skip, early[2 * channels, :channels],
        early[:channels],
    )


def solution(mesh):
    return jax.shard_map(
        on_device,
        mesh=mesh,
        in_specs=(
            P(None, "seq", None), P(None, "seq"), P(), P(None, None, "head"),
            P(None, None, "head"), P(None, "head"), P(None, "head"), P("head"),
            P(None, None, "head"), P(None, "head"), P("head"), P("head"), P("head"), P("head"),
            P("head", None), P(None, "seq", None),
        ),
        out_specs=(
            P(None, "seq", "head"), P(None, "seq", "head"), P("head"), P(None, None, "head"),
            P(None, None, "head"), P(None, "head"), P(None, "head"), P("head"),
            P(None, None, "head"), P(None, "head"), P("head"), P("head"), P("head"), P("head"),
            P("head", None),
        ),
        check_vma=False,
    )
```

time: 1080 us -> 292 us (0.27)
  local copies, waits for them, and re-layouts: 316 us -> 34.6 us
  waiting for transfers between devices: 286 us -> 62.2 us
  other arithmetic: 199 us -> 14.8 us
  matrix products: 150 us -> 2.2 us
  starting transfers between devices: 10.4 us -> 84.1 us
  blocking collectives: 83.4 us -> 10.7 us
  Pallas kernels: 0 us -> 67.2 us
    unnamed x7 -> x1, waiting for transfers between devices: 266 us -> 0.02 us
    dot_general x61 -> x1, matrix products: 148 us -> 2.2 us  [on_device(): jnp.einsum('rsd,cd->rsc', cotangent, out_weight, preferred_element_type=F32)]
    dynamic_update_slice x60 -> x0, local copies, waits for them, and re-layouts: 137 us -> none  [local_row(): final_state, outputs = lax.scan(advance, initial, pieces)]
    another operation x60 -> x2, other arithmetic: 69.8 us -> 0.7 us  [the longest x1 0.7 us: on_device(): jnp.stack([step_bias, decay_log, skip_gain])]
    pallas_call x0 -> x7, Pallas kernels: none -> 67.2 us  [the longest x2 30 us: backward_call(): pl.pallas_call(functools.partial(backward_kernel, start_call, end_call, l...]
    ppermute x4 -> x37, waiting for transfers between devices: 1.51 us -> 62.1 us  [the longest x12 42.7 us: passed_on(): total = total + lax.ppermute(part, axis, ring(axis, distance)).astype(F32)]
    ppermute x4 -> x37, starting transfers between devices: 10.2 us -> 59.9 us  [the longest x16 27.4 us: shifted(): lax.ppermute(block, axis, [(i - distance, i) for i in devices if i - dist...]
    psum x3 -> x0, blocking collectives: 45 us -> none  [the longest x1 24.1 us: on_device(): lax.psum((grad_gain_own, grad_inner_weight, grad_state_weight, grad_step_...]
  transfers between devices with their start and end apart: 9 -> 39, of which waited for: 4 -> 12; matrix products, arithmetic and copies ran while one was open for 10% -> 10% of each run, Pallas kernels for 0% -> 15%
where the time goes in v1:
time: 292 us; the launch traced here: 290 us
  starting transfers between devices  84.1 us (29%)
  Pallas kernels  67.2 us (23%)
  waiting for transfers between devices  62.2 us (21%)
  local copies, waits for them, and re-layouts  34.6 us (12%)
  other arithmetic  14.8 us (5%)
  between operations  14.7 us (5%)
  blocking collectives  10.7 us (4%)
    ppermute x12, waiting for transfers between devices, passed_on(): total = total + lax.ppermute(part, axis, ring(axis, distance)).astype(F32)  42.7 us
    pallas_call x2, Pallas kernels, backward_call(): pl.pallas_call(functools.partial(backward_kernel, start_call, end_call, l...  30 us
    ppermute x16, starting transfers between devices, shifted(): lax.ppermute(block, axis, [(i - distance, i) for i in devices if i - dist...  27.4 us
    all_to_all x1, starting transfers between devices, all_sum(): lax.all_to_all(whole.reshape(count, chunk, -1), axis, 0, 0, tiled=True)  24.1 us
    unnamed x94, local copies, waits for them, and re-layouts  22.8 us
    ppermute x16, waiting for transfers between devices, shifted(): lax.ppermute(block, axis, [(i - distance, i) for i in devices if i - dist...  17 us
    ppermute x12, starting transfers between devices, passed_on(): total = total + lax.ppermute(part, axis, ring(axis, distance)).astype(F32)  16.5 us
    all_gather x1, blocking collectives, all_sum(): return lax.all_gather(own, axis, axis=0, tiled=True).astype(F32)  10.7 us
  transfers between devices with their start and end apart: 39, of which 12 were waited for; matrix products, arithmetic and copies ran while one was open for 10% of the time, Pallas kernels for 15%

profile of v1, /device:TPU:0, one launch (start us, length us, event | category | flops | bytes accessed | tf_op | source)
XLA Modules:
  0.0 290.4 jit_solution(2129393920414726339)
XLA Ops:
  9.8 3.0 %collective-permute-start = (bf16[64,896]{1,0:T(8,128)(2,1)S(1)}, bf16[64,896]{1,0:T(8,128)(2,1)S(1)}, u32[]{:S(2)}, u32[]{:S(2)}) collective-permute-start(bf16[64,896]{1,0:T(8,128)(2,1)S(1)} %bitcast.48), channel_id=1, source_target_pairs={{0,1},{1,2},{2,3},{3,0},{4,5},{5,6},{6,7},{7,4},{8,9},{9,10},{10,1... | collective-permute-start | bytes 344072 | tf_op jit(solution)/shard_map/ppermute | solution.py:670
  25.5 5.7 %project.1 = (bf16[1,1024,768]{2,1,0:T(8,128)(2,1)}, bf16[1,1024,384]{2,1,0:T(8,128)(2,1)S(1)}, f32[1,1024,384]{2,1,0:T(8,128)}, f32[1,1024,128]{2,1,0:T(8,128)S...) custom-call(bf16[1,1024,768]{2,1,0:T(8,128)(2,1)} %refs_7_.1, ...), custom_call_target="tpu_custom_call" | custom-call | tf_op jit(solution)/shard_map/project/pallas_call | solution.py:690
  37.6 10.3 %forward.1 = (f32[1,1024,384]{2,1,0:T(8,128)}, bf16[1,1024,384]{2,1,0:T(8,128)(2,1)}, bf16[1,1024,256]{2,1,0:T(8,128)(2,1)S(1)}, bf16[1,1024,256]{2,1,0:T(8,128)...) custom-call(bf16[64,896]{1,0:T(8,128)(2,1)S(1)} %bitcast.51, ...), custom_call_target="tpu_custom_call" | custom-call | tf_op jit(solution)/shard_map/forward/pallas_call | solution.py:712
  47.9 4.1 %collective-permute-start.4 = (f32[1,136,384]{2,1,0:T(8,128)S(1)}, f32[1,136,384]{2,1,0:T(8,128)S(1)}, u32[]{:S(2)}, u32[]{:S(2)}) collective-permute-start(f32[1,136,384]{2,1,0:T(8,128)S(1)} %get-tuple-element.76), channel_id=1, source_target_pairs={{0,4},{4,8},{8,12},{12,16},{16,20},{20,24},{24,28},{1,5},{5,9},{9,... | collective-permute-start | bytes 626696 | tf_op jit(solution)/shard_map/ppermute | solution.py:598
  52.1 3.4 %collective-permute-start.5 = (f32[1,136,384]{2,1,0:T(8,128)S(1)}, f32[1,136,384]{2,1,0:T(8,128)S(1)}, u32[]{:S(2)}, u32[]{:S(2)}) collective-permute-start(f32[1,136,384]{2,1,0:T(8,128)S(1)} %get-tuple-element.76), channel_id=1, source_target_pairs={{0,8},{4,12},{8,16},{12,20},{16,24},{20,28},{1,9},{5,13},{9,17},{1... | collective-permute-start | bytes 626696 | tf_op jit(solution)/shard_map/ppermute | solution.py:598
  55.5 2.7 collective-permute-start.6
  67.8 4.4 %collective-permute-done.8.refs_4_ = f32[1,136,384]{2,1,0:T(8,128)S(1)} collective-permute-done((f32[1,136,384]{2,1,0:T(8,128)S(1)}, f32[1,136,384]{2,1,0:T(8,128)S(1)}, u32[]{:S(2)}, u32[]{:S(2)}) %collective-permute-start.8) | collective-permute-done | bytes 208928 | tf_op jit(solution)/shard_map/ppermute | solution.py:598
  72.2 6.5 %mix.1 = (f32[1,1024,384]{2,1,0:T(8,128)}, f32[1,4,8,256]{3,2,1,0:T(8,128)S(1)}, f32[1,4,128,384]{3,2,1,0:T(8,128)S(1)}) custom-call(f32[1,136,384]{2,1,0:T(8,128)S(1)} %collective-permute-done.4.refs_0_, f32[1,136,384]{2,1,0:T(8,128)S(1)} %collective-permute-done.5.refs_1_, f32[1,136,384]{2,1,0:T(8,128)S(1)} %collective-permute-done.6.refs_2_, ...), custom_call_target="tpu_custom_call" | custom-call | tf_op jit(solution)/shard_map/mix/pallas_call | solution.py:743
  80.5 2.8 collective-permute-start.13
  85.8 6.7 %gate.1 = (f32[1,1024,384]{2,1,0:T(8,128)}, bf16[1,1024,384]{2,1,0:T(8,128)(2,1)S(1)}, bf16[1,1024,384]{2,1,0:T(8,128)(2,1)S(1)}, f32[1,4,128,384]{3,2,1,0:T(8,1...) custom-call(f32[1,4,8,256]{3,2,1,0:T(8,128)S(1)} %get-tuple-element.83.refs_0_, ...), custom_call_target="tpu_custom_call" | custom-call | tf_op jit(solution)/shard_map/gate/pallas_call | solution.py:763
  103.0 7.8 %collective-permute-done.18.refs_1_ = f32[1,136,384]{2,1,0:T(8,128)S(1)} collective-permute-done((f32[1,136,384]{2,1,0:T(8,128)}, f32[1,136,384]{2,1,0:T(8,128)S(1)}, u32[]{:S(2)}, u32[]{:S(2)}) %collective-permute-start.18) | collective-permute-done | bytes 208928 | tf_op jit(solution)/shard_map/ppermute | solution.py:598
  113.2 8.0 %out.1 = (f32[1,1024,768]{2,1,0:T(8,128)}, f32[776,768]{1,0:T(8,128)}, bf16[1,1024,192]{2,1,0:T(8,128)(2,1)S(1)}, bf16[1,1024,192]{2,1,0:T(8,128)(2,1)S(1)}, bf1...) custom-call(s32[1]{0:T(128)} %bitcast.me.refs_7_.refs_6_, bf16[1,1024,384]{2,1,0:T(8,128)(2,1)S(1)} %copy-done.13, ...), custom_call_target="tpu_custom_call" | custom-call | tf_op jit(solution)/shard_map/out/pallas_call | solution.py:788
  122.1 3.5 %collective-permute-start.16 = (bf16[1,1024,192]{2,1,0:T(8,128)(2,1)}, bf16[1,1024,192]{2,1,0:T(8,128)(2,1)}, u32[]{:S(2)}, u32[]{:S(2)}) collective-permute-start(bf16[1,1024,192]{2,1,0:T(8,128)(2,1)} %get-tuple-element.92), channel_id=1, source_target_pairs={{0,3},{1,0},{2,1},{3,2},{4,7},{5,4},{6,5},{7,6},{8,11},{9,8},{10,9... | collective-permute-start | bytes 1179656 | tf_op jit(solution)/shard_map/ppermute | solution.py:604
  126.9 14.7 %backward.2 = (bf16[1,512,192]{2,1,0:T(8,128)(2,1)S(1)}, bf16[1,512,192]{2,1,0:T(8,128)(2,1)S(1)}, bf16[1,512,192]{2,1,0:T(8,128)(2,1)}, bf16[1,512,192]{2,1,0:T...) custom-call(f32[1,136,384]{2,1,0:T(8,128)S(1)} %collective-permute-d, ...), custom_call_target="tpu_custom_call" | custom-call | tf_op jit(solution)/shard_map/backward/pallas_call | solution.py:855
  142.3 15.3 %backward.3 = (bf16[1,512,192]{2,1,0:T(8,128)(2,1)S(1)}, bf16[1,512,192]{2,1,0:T(8,128)(2,1)S(1)}, bf16[1,512,192]{2,1,0:T(8,128)(2,1)S(1)}, bf16[1,512,192]{2,1...) custom-call(f32[1,128,384]{2,1,0:T(8,128)S(1)} %get-tuple-element.10, ...), custom_call_target="tpu_custom_call" | custom-call | tf_op jit(solution)/shard_map/backward/pallas_call | solution.py:855
  157.6 3.3 %collective-permute-start.32 = (bf16[1,16,192]{2,1,0:T(8,128)(2,1)S(1)}, bf16[1,16,192]{2,1,0:T(8,128)(2,1)S(1)}, u32[]{:S(2)}, u32[]{:S(2)}) collective-permute-start(bf16[1,16,192]{2,1,0:T(8,128)(2,1)S(1)} %get-tuple-element.122), channel_id=1, source_target_pairs={{0,3},{1,0},{2,1},{3,2},{4,7},{5,4},{6,5},{7,6},{8,11},{9,8},{10,9... | collective-permute-start | bytes 18440 | tf_op jit(solution)/shard_map/ppermute | solution.py:604
  163.6 2.8 collective-permute-start.36
  179.5 24.1 %all-to-all-start = ((bf16[8,64,768]{2,1,0:T(8,128)(2,1)}), bf16[8,64,768]{2,1,0:T(8,128)(2,1)}, u32[]{:S(2)}, u32[]{:S(2)}) async-start(bf16[8,64,768]{2,1,0:T(8,128)(2,1)} %bitcast.12), calls=%async_computation | async-start | bytes 1572864 | tf_op jit(solution)/shard_map/all_to_all | solution.py:611
  204.7 16.3 %collective-permute-done.15 = bf16[1,1024,192]{2,1,0:T(8,128)(2,1)} collective-permute-done((bf16[1,1024,192]{2,1,0:T(8,128)(2,1)}, bf16[1,1024,192]{2,1,0:T(8,128)(2,1)}, u32[]{:S(2)}, u32[]{:S(2)}) %collective-permute-start.15) | collective-permute-done | bytes 393248 | tf_op jit(solution)/shard_map/ppermute | solution.py:604
  227.1 16.4 %collective-permute-done.28 = bf16[1,512,192]{2,1,0:T(8,128)(2,1)} collective-permute-done((bf16[1,512,192]{2,1,0:T(8,128)(2,1)}, bf16[1,512,192]{2,1,0:T(8,128)(2,1)}, u32[]{:S(2)}, u32[]{:S(2)}) %collective-permute-start.28) | collective-permute-done | bytes 196640 | tf_op jit(solution)/shard_map/ppermute | solution.py:604
  244.6 10.0 %collective-permute-done.25 = bf16[1,512,192]{2,1,0:T(8,128)(2,1)} collective-permute-done((bf16[1,512,192]{2,1,0:T(8,128)(2,1)S(1)}, bf16[1,512,192]{2,1,0:T(8,128)(2,1)}, u32[]{:S(2)}, u32[]{:S(2)}) %collective-permute-start.25) | collective-permute-done | bytes 196640 | tf_op jit(solution)/shard_map/ppermute | solution.py:604
  259.6 10.7 %all_gather.3 = bf16[512,768]{1,0:T(8,128)(2,1)S(1)} all-gather(bf16[64,768]{1,0:T(8,128)(2,1)S(1)} %reduce_sum.21), channel_id=1, replica_groups=mesh['seq'=8,'head'=4] {'seq'}, dimensions={0}, use_global_device_ids=true | all-gather | bytes 884736 | tf_op jit(solution)/shard_map/all_gather | solution.py:613
  275.5 2.8 fusion.24
  278.4 3.0 %copy.36 = f32[768,2,384]{2,1,0:T(2,128)} copy(f32[768,2,384]{0,2,1:T(8,128)S(1)} %maximum_bitcast_fusion) | data formatting | bytes 4718592
  (207 shorter events, 87.4 us)
Async XLA Ops:
  7.2 268.3 %all-reduce.7.cloned.1.call-start = ((), (), s32[]{:S(2)}) async-start(), calls=%async_computation.1 | async-start | bytes 4767744 | tf_op jit(solution)/shard_map/psum | solution.py:807
  9.8 22.3 %collective-permute-start = (bf16[64,896]{1,0:T(8,128)(2,1)S(1)}, bf16[64,896]{1,0:T(8,128)(2,1)S(1)}, u32[]{:S(2)}, u32[]{:S(2)}) collective-permute-start(bf16[64,896]{1,0:T(8,128)(2,1)S(1)} %bitcast.48), channel_id=1, source_target_pairs={{0,1},{1,2},{2,3},{3,0},{4,5},{5,6},{6,7},{7,4},{8,9},{9,10},{10,1... | collective-permute-start | bytes 344072 | tf_op jit(solution)/shard_map/ppermute | solution.py:670
  12.9 20.0 %collective-permute-start.1 = (bf16[64,896]{1,0:T(8,128)(2,1)S(1)}, bf16[64,896]{1,0:T(8,128)(2,1)S(1)}, u32[]{:S(2)}, u32[]{:S(2)}) collective-permute-start(bf16[64,896]{1,0:T(8,128)(2,1)S(1)} %bitcast.49), channel_id=1, source_target_pairs={{0,2},{1,3},{2,0},{3,1},{4,6},{5,7},{6,4},{7,5},{8,10},{9,11},{10,... | collective-permute-start | bytes 344072 | tf_op jit(solution)/shard_map/ppermute | solution.py:670
  15.5 18.0 %collective-permute-start.2 = (bf16[64,896]{1,0:T(8,128)(2,1)S(1)}, bf16[64,896]{1,0:T(8,128)(2,1)S(1)}, u32[]{:S(2)}, u32[]{:S(2)}) collective-permute-start(bf16[64,896]{1,0:T(8,128)(2,1)S(1)} %bitcast.50), channel_id=1, source_target_pairs={{0,3},{1,0},{2,1},{3,2},{4,7},{5,4},{6,5},{7,6},{8,11},{9,8},{10,9... | collective-permute-start | bytes 344072 | tf_op jit(solution)/shard_map/ppermute | solution.py:670
  18.4 13.8 %collective-permute-start.3 = (bf16[1,16,896]{2,1,0:T(8,128)(2,1)S(1)}, bf16[1,16,896]{2,1,0:T(8,128)(2,1)S(1)}, u32[]{:S(2)}, u32[]{:S(2)}) collective-permute-start(bf16[1,16,896]{2,1,0:T(8,128)(2,1)S(1)} %pad_maximum_fusion), channel_id=1, source_target_pairs={{0,4},{4,8},{8,12},{12,16},{16,20},{20,24},{24,28},{1,5},{5,9},{9,... | collective-permute-start | bytes 86024 | tf_op jit(solution)/shard_map/ppermute | solution.py:598
  47.9 12.9 %collective-permute-start.4 = (f32[1,136,384]{2,1,0:T(8,128)S(1)}, f32[1,136,384]{2,1,0:T(8,128)S(1)}, u32[]{:S(2)}, u32[]{:S(2)}) collective-permute-start(f32[1,136,384]{2,1,0:T(8,128)S(1)} %get-tuple-element.76), channel_id=1, source_target_pairs={{0,4},{4,8},{8,12},{12,16},{16,20},{20,24},{24,28},{1,5},{5,9},{9,... | collective-permute-start | bytes 626696 | tf_op jit(solution)/shard_map/ppermute | solution.py:598
  59.5 12.6 %collective-permute-start.8 = (f32[1,136,384]{2,1,0:T(8,128)S(1)}, f32[1,136,384]{2,1,0:T(8,128)S(1)}, u32[]{:S(2)}, u32[]{:S(2)}) collective-permute-start(f32[1,136,384]{2,1,0:T(8,128)S(1)} %get-tuple-element.76), channel_id=1, source_target_pairs={{0,20},{4,24},{8,28},{1,21},{5,25},{9,29},{2,22},{6,26},{10,30},{3... | collective-permute-start | bytes 626696 | tf_op jit(solution)/shard_map/ppermute | solution.py:598
  60.9 11.3 %collective-permute-start.9 = (f32[1,136,384]{2,1,0:T(8,128)S(1)}, f32[1,136,384]{2,1,0:T(8,128)S(1)}, u32[]{:S(2)}, u32[]{:S(2)}) collective-permute-start(f32[1,136,384]{2,1,0:T(8,128)S(1)} %get-tuple-element.76), channel_id=1, source_target_pairs={{0,24},{4,28},{1,25},{5,29},{2,26},{6,30},{3,27},{7,31}} | collective-permute-start | bytes 626696 | tf_op jit(solution)/shard_map/ppermute | solution.py:598
  96.5 14.3 %collective-permute-start.18 = (f32[1,136,384]{2,1,0:T(8,128)}, f32[1,136,384]{2,1,0:T(8,128)S(1)}, u32[]{:S(2)}, u32[]{:S(2)}) collective-permute-start(f32[1,136,384]{2,1,0:T(8,128)} %get-tuple-element.93), channel_id=1, source_target_pairs={{8,0},{12,4},{16,8},{20,12},{24,16},{28,20},{9,1},{13,5},{17,9},{2... | collective-permute-start | bytes 626696 | tf_op jit(solution)/shard_map/ppermute | solution.py:598
  97.8 24.3 %collective-permute-start.19 = (f32[1,136,384]{2,1,0:T(8,128)}, f32[1,136,384]{2,1,0:T(8,128)S(1)}, u32[]{:S(2)}, u32[]{:S(2)}) collective-permute-start(f32[1,136,384]{2,1,0:T(8,128)} %get-tuple-element.93), channel_id=1, source_target_pairs={{12,0},{16,4},{20,8},{24,12},{28,16},{13,1},{17,5},{21,9},{25,13},... | collective-permute-start | bytes 626696 | tf_op jit(solution)/shard_map/ppermute | solution.py:598
  99.1 27.0 %collective-permute-start.20 = (f32[1,136,384]{2,1,0:T(8,128)}, f32[1,136,384]{2,1,0:T(8,128)S(1)}, u32[]{:S(2)}, u32[]{:S(2)}) collective-permute-start(f32[1,136,384]{2,1,0:T(8,128)} %get-tuple-element.93), channel_id=1, source_target_pairs={{16,0},{20,4},{24,8},{28,12},{17,1},{21,5},{25,9},{29,13},{18,2},{... | collective-permute-start | bytes 626696 | tf_op jit(solution)/shard_map/ppermute | solution.py:598
  100.4 26.4 %collective-permute-start.21 = (f32[1,136,384]{2,1,0:T(8,128)}, f32[1,136,384]{2,1,0:T(8,128)S(1)}, u32[]{:S(2)}, u32[]{:S(2)}) collective-permute-start(f32[1,136,384]{2,1,0:T(8,128)} %get-tuple-element.93), channel_id=1, source_target_pairs={{20,0},{24,4},{28,8},{21,1},{25,5},{29,9},{22,2},{26,6},{30,10},{2... | collective-permute-start | bytes 626696 | tf_op jit(solution)/shard_map/ppermute | solution.py:598
  101.7 25.1 %collective-permute-start.22 = (f32[1,136,384]{2,1,0:T(8,128)}, f32[1,136,384]{2,1,0:T(8,128)}, u32[]{:S(2)}, u32[]{:S(2)}) collective-permute-start(f32[1,136,384]{2,1,0:T(8,128)} %get-tuple-element.93), channel_id=1, source_target_pairs={{24,0},{28,4},{25,1},{29,5},{26,2},{30,6},{27,3},{31,7}} | collective-permute-start | bytes 626696 | tf_op jit(solution)/shard_map/ppermute | solution.py:598
  110.7 16.1 %collective-permute-start.23 = (f32[1,136,384]{2,1,0:T(8,128)}, f32[1,136,384]{2,1,0:T(8,128)}, u32[]{:S(2)}, u32[]{:S(2)}) collective-permute-start(f32[1,136,384]{2,1,0:T(8,128)} %get-tuple-element.93), channel_id=1, source_target_pairs={{28,0},{29,1},{30,2},{31,3}} | collective-permute-start | bytes 626696 | tf_op jit(solution)/shard_map/ppermute | solution.py:598
  122.1 81.5 %collective-permute-start.16 = (bf16[1,1024,192]{2,1,0:T(8,128)(2,1)}, bf16[1,1024,192]{2,1,0:T(8,128)(2,1)}, u32[]{:S(2)}, u32[]{:S(2)}) collective-permute-start(bf16[1,1024,192]{2,1,0:T(8,128)(2,1)} %get-tuple-element.92), channel_id=1, source_target_pairs={{0,3},{1,0},{2,1},{3,2},{4,7},{5,4},{6,5},{7,6},{8,11},{9,8},{10,9... | collective-permute-start | bytes 1179656 | tf_op jit(solution)/shard_map/ppermute | solution.py:604
  171.9 49.1 %collective-permute-start.15 = (bf16[1,1024,192]{2,1,0:T(8,128)(2,1)}, bf16[1,1024,192]{2,1,0:T(8,128)(2,1)}, u32[]{:S(2)}, u32[]{:S(2)}) collective-permute-start(bf16[1,1024,192]{2,1,0:T(8,128)(2,1)} %get-tuple-element.91), channel_id=1, source_target_pairs={{0,2},{1,3},{2,0},{3,1},{4,6},{5,7},{6,4},{7,5},{8,10},{9,11},{10,... | collective-permute-start | bytes 1179656 | tf_op jit(solution)/shard_map/ppermute | solution.py:604
  172.9 48.1 %collective-permute-start.14 = (bf16[1,1024,192]{2,1,0:T(8,128)(2,1)S(1)}, bf16[1,1024,192]{2,1,0:T(8,128)(2,1)}, u32[]{:S(2)}, u32[]{:S(2)}) collective-permute-start(bf16[1,1024,192]{2,1,0:T(8,128)(2,1)S(1)} %copy-done.32), channel_id=1, source_target_pairs={{0,1},{1,2},{2,3},{3,0},{4,5},{5,6},{6,7},{7,4},{8,9},{9,10},{10,1... | collective-permute-start | bytes 1179656 | tf_op jit(solution)/shard_map/ppermute | solution.py:604
  174.5 50.4 %collective-permute-start.29 = (bf16[1,512,192]{2,1,0:T(8,128)(2,1)}, bf16[1,512,192]{2,1,0:T(8,128)(2,1)S(1)}, u32[]{:S(2)}, u32[]{:S(2)}) collective-permute-start(bf16[1,512,192]{2,1,0:T(8,128)(2,1)} %get-tuple-element.118), channel_id=1, source_target_pairs={{0,3},{1,0},{2,1},{3,2},{4,7},{5,4},{6,5},{7,6},{8,11},{9,8},{10,9... | collective-permute-start | bytes 589832 | tf_op jit(solution)/shard_map/ppermute | solution.py:604
  176.8 66.7 %collective-permute-start.28 = (bf16[1,512,192]{2,1,0:T(8,128)(2,1)}, bf16[1,512,192]{2,1,0:T(8,128)(2,1)}, u32[]{:S(2)}, u32[]{:S(2)}) collective-permute-start(bf16[1,512,192]{2,1,0:T(8,128)(2,1)} %get-tuple-element.117), channel_id=1, source_target_pairs={{0,2},{1,3},{2,0},{3,1},{4,6},{5,7},{6,4},{7,5},{8,10},{9,11},{10,... | collective-permute-start | bytes 589832 | tf_op jit(solution)/shard_map/ppermute | solution.py:604
  179.5 78.8 %all-to-all-start = ((bf16[8,64,768]{2,1,0:T(8,128)(2,1)}), bf16[8,64,768]{2,1,0:T(8,128)(2,1)}, u32[]{:S(2)}, u32[]{:S(2)}) async-start(bf16[8,64,768]{2,1,0:T(8,128)(2,1)} %bitcast.12), calls=%async_computation | async-start | bytes 1572864 | tf_op jit(solution)/shard_map/all_to_all | solution.py:611
  203.6 39.8 %collective-permute-start.27 = (bf16[1,512,192]{2,1,0:T(8,128)(2,1)S(1)}, bf16[1,512,192]{2,1,0:T(8,128)(2,1)}, u32[]{:S(2)}, u32[]{:S(2)}) collective-permute-start(bf16[1,512,192]{2,1,0:T(8,128)(2,1)S(1)} %copy-done.34), channel_id=1, source_target_pairs={{0,1},{1,2},{2,3},{3,0},{4,5},{5,6},{6,7},{7,4},{8,9},{9,10},{10,1... | collective-permute-start | bytes 589832 | tf_op jit(solution)/shard_map/ppermute | solution.py:604
  221.0 23.6 %collective-permute-start.26 = (bf16[1,512,192]{2,1,0:T(8,128)(2,1)S(1)}, bf16[1,512,192]{2,1,0:T(8,128)(2,1)S(1)}, u32[]{:S(2)}, u32[]{:S(2)}) collective-permute-start(bf16[1,512,192]{2,1,0:T(8,128)(2,1)S(1)} %copy-done.38), channel_id=1, source_target_pairs={{0,3},{1,0},{2,1},{3,2},{4,7},{5,4},{6,5},{7,6},{8,11},{9,8},{10,9... | collective-permute-start | bytes 589832 | tf_op jit(solution)/shard_map/ppermute | solution.py:604
  221.0 33.6 %collective-permute-start.25 = (bf16[1,512,192]{2,1,0:T(8,128)(2,1)S(1)}, bf16[1,512,192]{2,1,0:T(8,128)(2,1)}, u32[]{:S(2)}, u32[]{:S(2)}) collective-permute-start(bf16[1,512,192]{2,1,0:T(8,128)(2,1)S(1)} %copy-done.36), channel_id=1, source_target_pairs={{0,2},{1,3},{2,0},{3,1},{4,6},{5,7},{6,4},{7,5},{8,10},{9,11},{10,... | collective-permute-start | bytes 589832 | tf_op jit(solution)/shard_map/ppermute | solution.py:604
  224.9 29.7 %collective-permute-start.24 = (bf16[1,512,192]{2,1,0:T(8,128)(2,1)S(1)}, bf16[1,512,192]{2,1,0:T(8,128)(2,1)S(1)}, u32[]{:S(2)}, u32[]{:S(2)}) collective-permute-start(bf16[1,512,192]{2,1,0:T(8,128)(2,1)S(1)} %get-tuple-element.112), channel_id=1, source_target_pairs={{0,1},{1,2},{2,3},{3,0},{4,5},{5,6},{6,7},{7,4},{8,9},{9,10},{10,1... | collective-permute-start | bytes 589832 | tf_op jit(solution)/shard_map/ppermute | solution.py:604
  (58 other events, 680.4 us)
Sparse Core Ops, SparseCore 0:
  122.2 65.7 all-reduce.6

commit v2 on v1

--- a/solution.py
+++ b/solution.py
@@ -19,8 +19,14 @@
 BF16 = jnp.bfloat16
 FAR = -1e30
 PARAMS = pltpu.CompilerParams(
-    dimension_semantics=("arbitrary", "arbitrary"), vmem_limit_bytes=50 * 2**20
+    dimension_semantics=("arbitrary", "arbitrary"), vmem_limit_bytes=62 * 2**20
 )
+
+
+def cost(microseconds):
+    return pl.CostEstimate(
+        flops=int(microseconds * 1e9), bytes_accessed=int(microseconds * 1e5), transcendentals=0
+    )
 
 
 def rounded(tensor):
@@ -324,8 +330,13 @@
     width = tensor.shape[1]
     own = width // len(refs)
     turned = rounded(pltpu.roll(tensor, (len(refs) - me) % len(refs) * own, 1))
-    for part, ref in enumerate(refs):
-        ref[...] = turned[:, part * own : (part + 1) * own]
+    blocks = [turned[:, part * own : (part + 1) * own] for part in range(len(refs))]
+    if len(refs) == 4:
+        odd = me % 2 == 1
+        swapped = [jnp.where(odd, blocks[4 - part], blocks[part]) for part in (1, 3)]
+        blocks = [blocks[0], swapped[0], blocks[2], swapped[1]]
+    for block, ref in zip(blocks, refs):
+        ref[...] = block
 
 
 def out_kernel(parts, me, normed_out, cot, dgate, normed, wout, win, gain, skip, back, grads, *branch):
@@ -336,7 +347,7 @@
     def _():
         grads[...] = jnp.zeros_like(grads)
         grads[2 * channels : 2 * channels + 1, :channels] = gain[...]
-        grads[2 * channels + 1 : 2 * channels + 2, :channels] = skip[...]
+        grads[2 * channels + 1 : 2 * channels + 2, :LANES] = collect_row(skip[...])
 
     store_parts(branch, dot(normed_out[...], wout[...]), me[0])
     grads[:channels, :] += dot_tn(normed_out[...], cot[...])
@@ -575,7 +586,11 @@
                 return rounded(jnp.concatenate([upper_half, whole - upper_half], axis=0))
 
             packed[:channels, :] = rounded(grad_x[...])
-            packed[channels : channels + EDGE, :] = rounded(grad_misc[...])
+            misc = grad_misc[...]
+            fine = misc - misc.astype(BF16).astype(F32)
+            packed[channels : channels + EDGE, :] = rounded(
+                jnp.concatenate([misc[:11], fine[9:11], misc[13:]], axis=0)
+            )
             packed[channels + EDGE : channels + 2 * EDGE, :] = both_halves(grad_ci[...])
             own = half // parts
             taps = grad_cs[...]
@@ -588,6 +603,43 @@
                 )
 
 
+def unpack_kernel(
+    own_width, head_count, late, early, gain, inner, state, step, conv, conv_bias, taps,
+    taps_bias, step_bias, decay, skip, gain_out, out_weight,
+):
+    channels, width = out_weight.shape
+    own = state.shape[-1]
+    inner[:, 0, :] = late[:channels, :].astype(F32).T
+    inner[:, 1, :] = early[channels : 2 * channels, :].T
+    base = channels
+    misc = late[base : base + EDGE, :].astype(F32)
+    step[...] = misc.T[:, :head_count]
+    step_bias[...] = (misc[9:10] + misc[11:12])[:, :head_count]
+    decay[...] = (misc[10:11] + misc[12:13])[:, :head_count]
+    base += EDGE
+    block = late[base : base + EDGE, :].astype(F32)
+    block = block[:8] + block[8:]
+    conv[...] = block[:K, :channels]
+    conv_bias[...] = block[K : K + 1, :channels]
+    base += EDGE
+    weights = late[base : base + 2 * own, :].astype(F32).T
+    state[:, 0, :] = weights[:, :own]
+    state[:, 1, :] = weights[:, own:]
+    base += 2 * own
+    block = late[base : base + EDGE, :].astype(F32)
+    block = block[:8] + block[8:]
+    taps[:, 0, :] = block[:K, :own]
+    taps[:, 1, :] = block[:K, own : 2 * own]
+    taps_bias[0:1, :] = block[K : K + 1, :own]
+    taps_bias[1:2, :] = block[K : K + 1, own : 2 * own]
+    base += EDGE
+    block = late[base : base + EDGE, :].astype(F32)
+    gain[...] = (block[0:1] + block[1:2])[:, :own_width]
+    out_weight[...] = early[:channels, :]
+    gain_out[...] = early[2 * channels : 2 * channels + 1, :channels]
+    skip[...] = early[2 * channels + 1 : 2 * channels + 2, :head_count]
+
+
 def ring(axis, distance):
     count = lax.axis_size(axis)
     return [(i, (i + distance) % count) for i in range(count)]
@@ -598,11 +650,49 @@
     return lax.ppermute(block, axis, [(i - distance, i) for i in devices if i - distance in devices])
 
 
-def passed_on(parts, axis):
+def crossed(block, axis, mask):
+    return lax.ppermute(block, axis, [(i, i ^ mask) for i in range(lax.axis_size(axis))])
+
+
+def send_near(parts, axis):
+    if len(parts) == 4:
+        return [crossed(parts[3], axis, 1), crossed(parts[1], axis, 1)]
+    return [lax.ppermute(part, axis, ring(axis, d)) for d, part in enumerate(parts[1:], 1)]
+
+
+def send_far(parts, near, axis):
+    if len(parts) == 4:
+        return [crossed(rounded(parts[2].astype(F32) + near[0].astype(F32)), axis, 2)]
+    return []
+
+
+def add_up(parts, near, far):
     total = parts[0].astype(F32)
-    for distance, part in enumerate(parts[1:], 1):
-        total = total + lax.ppermute(part, axis, ring(axis, distance)).astype(F32)
+    for piece in (near[1:] if far else near) + far:
+        total = total + piece.astype(F32)
     return total
+
+
+def ordered(*groups):
+    flat, tree = jax.tree.flatten(groups)
+    return jax.tree.unflatten(tree, lax.optimization_barrier(flat))
+
+
+def chained(message, reverse):
+    count = lax.axis_size("seq")
+    core = lax.axis_index("seq") % 2
+    later = core == (0 if reverse else 1)
+    other = crossed(message, "seq", 1)
+    fade, other_fade = message[:, LANES:], other[:, LANES:]
+    state, other_state = message[:, :LANES], other[:, :LANES]
+    pair = jnp.where(
+        later, fade[:, :1] * other_state + state, other_fade[:, :1] * state + other_state
+    )
+    pair = jnp.concatenate([pair, fade * other_fade], axis=1)
+    neutral = (lax.broadcasted_iota(jnp.int32, message.shape, 1) >= LANES).astype(F32)
+    near = jnp.where(later, other, neutral)
+    sign = -2 if reverse else 2
+    return [near] + [shifted(pair, "seq", sign * d) for d in range(1, count // 2)]
 
 
 def all_sum(whole, axis):
@@ -704,6 +794,7 @@
         ],
         compiler_params=PARAMS,
         name="project",
+        cost_estimate=cost(6),
     )(tokens, gain_in, win, wst, hp)
     dn = jnp.einsum("rsd,cd->rsc", cotangent, out_weight, preferred_element_type=F32)
 
@@ -737,9 +828,10 @@
         ],
         compiler_params=PARAMS,
         name="forward",
+        cost_estimate=cost(10),
     )(*found, marked, normed, xpre, step, cum, win, halo, gain_in, ci)
 
-    arrived = [shifted(message, "seq", d) for d in range(1, seq_count)]
+    arrived = chained(message, False)
     mixer, sums, entry_states = pl.pallas_call(
         functools.partial(mix_kernel, len(arrived)),
         grid=grid,
@@ -755,6 +847,7 @@
         scratch_shapes=[pltpu.VMEM((LANES, channels), F32)],
         compiler_params=PARAMS,
         name="mix",
+        cost_estimate=cost(6),
     )(*arrived, yin, xact, bc, gate, dn, cum, marked, gain_out, hp, fresh, fades)
 
     sums_all = [sums] + [
@@ -782,9 +875,10 @@
         scratch_shapes=[pltpu.VMEM((LANES, channels), F32), pltpu.VMEM((8, channels), F32)],
         compiler_params=PARAMS,
         name="gate",
+        cost_estimate=cost(6),
     )(*sums_all, mixer, gate, dn, xact, bc, cum, marked, gain_out, hp, fades)
 
-    returned = [shifted(back_message, "seq", -d) for d in range(1, seq_count)]
+    returned = chained(back_message, True)
     back, early, *branch = pl.pallas_call(
         functools.partial(out_kernel, head_devices),
         grid=grid,
@@ -799,11 +893,12 @@
         + [act(own_width, BF16)] * head_devices,
         compiler_params=PARAMS,
         name="out",
+        cost_estimate=cost(8),
     )(me, normed_out, cotangent, dgate, normed, out_weight, win, grad_gain_out, grad_skip)
 
     column = lax.axis_index("head") * own_width
     own_tokens = lax.dynamic_slice_in_dim(tokens, column, own_width, 2).astype(F32)
-    output = rounded(own_tokens + passed_on(branch, "head"))
+    branch_near = send_near(branch, "head")
     early = lax.psum(early, "seq")
 
     late_rows = channels + 3 * EDGE + 2 * own_state + EDGE
@@ -881,6 +976,7 @@
             ],
             compiler_params=PARAMS,
             name="backward",
+            cost_estimate=cost(15),
         )(
             *lead, *carried, me, tokens, halo, marked, normed, xpre, xpre, halo_x, spre, spre,
             halo_s, xact, bc, yin, dy, back, step, cum, raw, run_all, entry_states, entering,
@@ -890,29 +986,31 @@
     first = groups // 2
     if first:
         outs = backward_call(True, False, first, groups - first, [])
-        token_sums = [passed_on(outs[:head_devices], "head")]
-        outs = backward_call(False, True, 0, first, outs[head_devices:])
+        outs, branch_near = ordered(outs, branch_near)
+        branch_far = send_far(branch, branch_near, "head")
+        late_parts, carried = outs[:head_devices], outs[head_devices:]
+        late_near = send_near(late_parts, "head")
+        outs = backward_call(False, True, 0, first, carried)
+        outs, branch_far, late_near = ordered(outs, branch_far, late_near)
     else:
-        token_sums = []
         outs = backward_call(True, True, 0, groups, [])
+        branch_far = send_far(branch, branch_near, "head")
     gtok, packed = outs[:head_devices], outs[head_devices]
     edge_parts = outs[head_devices + 1 : 2 * head_devices + 1]
     state_parts = outs[2 * head_devices + 1 :]
-
+    state_pieces = [
+        lax.ppermute(state_parts[d], "head", ring("head", -d)) for d in range(1, head_devices)
+    ]
+    edge_near = send_near(edge_parts, "head")
+    edge_far = send_far(edge_parts, edge_near, "head")
     state_total = state_parts[0].astype(F32)
-    for d in range(1, head_devices):
-        state_total = state_total + lax.ppermute(
-            state_parts[d], "head", ring("head", -d)
-        ).astype(F32)
-    edge = passed_on(edge_parts, "head")
-    token_sums = [passed_on(gtok, "head")] + token_sums
-    own_cot = lax.dynamic_slice_in_dim(cotangent, column, own_width, 2).astype(F32)
-    from_next = shifted(edge, "seq", -1)[:, EDGE - K + 1 :]
-    padding = jnp.zeros((rows, length - K + 1, own_width), F32)
-    grad_tokens = (
-        own_cot + jnp.concatenate(token_sums, axis=1)
-        + jnp.concatenate([padding, from_next], axis=1)
-    )
+    for piece in state_pieces:
+        state_total = state_total + piece.astype(F32)
+    edge = add_up(edge_parts, edge_near, edge_far)
+    gtok_near = send_near(gtok, "head")
+    if first:
+        late_far = send_far(late_parts, late_near, "head")
+    output = rounded(own_tokens + add_up(branch, branch_near, branch_far))
     gain_row = (edge[rows - 1, 0] + edge[rows - 1, 1])[None]
     gain_high = gain_row.astype(BF16).astype(F32)
     gain_rows = jnp.pad(
@@ -929,26 +1027,38 @@
         ],
         axis=0,
     )
-    late = all_sum(late, "seq")
-
-    def take(start, count):
-        return late[start : start + count]
-
-    grad_inner = jnp.stack([take(0, channels), early[channels : 2 * channels]]).transpose(2, 0, 1)
-    misc = take(channels, EDGE)
-    conv = take(channels + EDGE, 8) + take(channels + EDGE + 8, 8)
-    base = packed_rows
-    grad_state = take(base, 2 * own_state).reshape(2, own_state, width).transpose(2, 0, 1)
-    base += 2 * own_state
-    taps = (take(base, 8) + take(base + 8, 8))[: K + 1, : 2 * own_state]
-    taps = taps.reshape(K + 1, 2, own_state)
-    gain = take(base + EDGE, 1) + take(base + EDGE + 1, 1)
-    skip = early[2 * channels + 1, :channels].reshape(head_count, WIDTH).sum(axis=1)
-    return (
-        output, grad_tokens, gain[0, :own_width], grad_inner, grad_state,
-        misc[:head_count].T, conv[:K, :channels], conv[K, :channels], taps[:K], taps[K],
-        misc[9, :head_count], misc[10, :head_count], skip, early[2 * channels, :channels],
-        early[:channels],
+    parts = lax.all_to_all(late.reshape(seq_count, chunk, -1), "seq", 0, 0, tiled=True)
+    parts, gtok_near = ordered(parts, gtok_near)
+    gtok_far = send_far(gtok, gtok_near, "head")
+    from_next = shifted(edge, "seq", -1)[:, EDGE - K + 1 :]
+    late = lax.all_gather(
+        rounded(jnp.sum(parts.astype(F32), axis=0)), "seq", axis=0, tiled=True
+    )
+    token_sums = [add_up(gtok, gtok_near, gtok_far)]
+    if first:
+        token_sums.append(add_up(late_parts, late_near, late_far))
+    own_cot = lax.dynamic_slice_in_dim(cotangent, column, own_width, 2).astype(F32)
+    padding = jnp.zeros((rows, length - K + 1, own_width), F32)
+    grad_tokens = (
+        own_cot + jnp.concatenate(token_sums, axis=1)
+        + jnp.concatenate([padding, from_next], axis=1)
+    )
+    outs = pl.pallas_call(
+        functools.partial(unpack_kernel, own_width, head_count),
+        out_shape=[
+            sds((1, own_width)), sds((width, 2, channels)), sds((width, 2, own_state)),
+            sds((width, head_count)), sds((K, channels)), sds((1, channels)),
+            sds((K, 2, own_state)), sds((2, own_state)), sds((1, head_count)),
+            sds((1, head_count)), sds((1, head_count)), sds((1, channels)),
+            sds((channels, width)),
+        ],
+        compiler_params=pltpu.CompilerParams(vmem_limit_bytes=62 * 2**20),
+        cost_estimate=cost(4),
+        name="unpack",
+    )(late, early)
+    one_row = (0, 5, 8, 9, 10, 11)
+    return (output, grad_tokens) + tuple(
+        out[0] if place in one_row else out for place, out in enumerate(outs)
     )
 
 

time: 292 us -> 251 us (0.86)
  starting transfers between devices: 84.1 us -> 47 us
  local copies, waits for them, and re-layouts: 34.6 us -> 18.9 us
  Pallas kernels: 67.2 us -> 77 us
    ppermute x15 -> x17, waiting for transfers between devices: 42.7 us -> 20.6 us  [the longest x14 20.6 us: crossed(): lax.ppermute(block, axis, [(i, i ^ mask) for i in range(lax.axis_size(axi...]
    all_to_all x1, starting transfers between devices: 24.1 us -> 3.55 us  [on_device(): lax.all_to_all(late.reshape(seq_count, chunk, -1), 'seq', 0, 0, tiled=True)]
    psum x1, waiting for transfers between devices: 0.02 us -> 16.9 us  [on_device(): early = lax.psum(early, 'seq')]
    ppermute x16 -> x8, starting transfers between devices: 27.4 us -> 13.5 us  [shifted(): lax.ppermute(block, axis, [(i - distance, i) for i in devices if i - dist...]
    unnamed x94 -> x95, local copies, waits for them, and re-layouts: 22.8 us -> 13.9 us
    slice x9 -> x4, local copies, waits for them, and re-layouts: 6.75 us -> 0.78 us  [the longest x2 0.74 us: chained(): fade[:, :1] * other_state + state]
    pallas_call x0 -> x1, Pallas kernels: none -> 5.14 us  [on_device(): pl.pallas_call(functools.partial(unpack_kernel, own_width, head_count), o...]
    ppermute x15 -> x17, starting transfers between devices: 21.8 us -> 20.5 us  [the longest x14 18.1 us: crossed(): lax.ppermute(block, axis, [(i, i ^ mask) for i in range(lax.axis_size(axi...]
  transfers between devices with their start and end apart: 39 -> 33, of which waited for: 12 -> 12; matrix products, arithmetic and copies ran while one was open for 10% -> 11% of each run, Pallas kernels for 15% -> 21%
where the time goes in v2:
time: 251 us; the launch traced here: 249 us
  Pallas kernels  77 us (31%)
  waiting for transfers between devices  59.7 us (24%)
  starting transfers between devices  47 us (19%)
  local copies, waits for them, and re-layouts  18.9 us (8%)
  other arithmetic  17.7 us (7%)
  between operations  14.7 us (6%)
  blocking collectives  12.2 us (5%)
    pallas_call x2, Pallas kernels, backward_call(): pl.pallas_call(functools.partial(backward_kernel, start_call, end_call, l...  31.4 us
    ppermute x14, waiting for transfers between devices, crossed(): lax.ppermute(block, axis, [(i, i ^ mask) for i in range(lax.axis_size(axi...  20.6 us
    ppermute x14, starting transfers between devices, crossed(): lax.ppermute(block, axis, [(i, i ^ mask) for i in range(lax.axis_size(axi...  18.1 us
    ppermute x8, waiting for transfers between devices, shifted(): lax.ppermute(block, axis, [(i - distance, i) for i in devices if i - dist...  17.2 us
    psum x1, waiting for transfers between devices, on_device(): early = lax.psum(early, 'seq')  16.9 us
    unnamed x95, local copies, waits for them, and re-layouts  13.9 us
    ppermute x8, starting transfers between devices, shifted(): lax.ppermute(block, axis, [(i - distance, i) for i in devices if i - dist...  13.5 us
    all_gather x1, blocking collectives, on_device(): lax.all_gather(rounded(jnp.sum(parts.astype(F32), axis=0)), 'seq', axis=0...  12.2 us
  transfers between devices with their start and end apart: 33, of which 12 were waited for; matrix products, arithmetic and copies ran while one was open for 11% of the time, Pallas kernels for 21%

profile of v2, /device:TPU:0, one launch (start us, length us, event | category | flops | bytes accessed | tf_op | source)
XLA Modules:
  0.0 249.5 jit_solution(5608821745488759417)
XLA Ops:
  9.9 3.1 %collective-permute-start = (bf16[64,896]{1,0:T(8,128)(2,1)S(1)}, bf16[64,896]{1,0:T(8,128)(2,1)S(1)}, u32[]{:S(2)}, u32[]{:S(2)}) collective-permute-start(bf16[64,896]{1,0:T(8,128)(2,1)S(1)} %bitcast.37), channel_id=1, source_target_pairs={{0,1},{1,2},{2,3},{3,0},{4,5},{5,6},{6,7},{7,4},{8,9},{9,10},{10,1... | collective-permute-start | bytes 344072 | tf_op jit(solution)/shard_map/ppermute | solution.py:760
  13.0 2.6 %collective-permute-start.1 = (bf16[64,896]{1,0:T(8,128)(2,1)S(1)}, bf16[64,896]{1,0:T(8,128)(2,1)S(1)}, u32[]{:S(2)}, u32[]{:S(2)}) collective-permute-start(bf16[64,896]{1,0:T(8,128)(2,1)S(1)} %bitcast.38), channel_id=1, source_target_pairs={{0,2},{1,3},{2,0},{3,1},{4,6},{5,7},{6,4},{7,5},{8,10},{9,11},{10,... | collective-permute-start | bytes 344072 | tf_op jit(solution)/shard_map/ppermute | solution.py:760
  19.7 2.5 %copy.38 = bf16[96,8,2,384]{3,1,2,0:T(8,128)(2,1)} copy(bf16[96,8,2,384]{3,2,1,0:T(2,128)(2,1)} %bitcast.31) | data formatting | bytes 2359296
  26.6 6.2 %project.1 = (bf16[1,1024,768]{2,1,0:T(8,128)(2,1)}, bf16[1,1024,384]{2,1,0:T(8,128)(2,1)}, f32[1,1024,384]{2,1,0:T(8,128)}, f32[1,1024,128]{2,1,0:T(8,128)}, f3...) custom-call(bf16[1,1024,768]{2,1,0:T(8,128)(2,1)} %refs_7_.1, f32[1,768]{1,0:T(1,128)} %broadcast_in_dim.34.gain.refs_11_.refs_33_.refs_35_, ...), custom_call_target="tpu_custom_call" | custom-call | flops 6000000000 | bytes 600000 | tf_op jit(solution)/shard_map/project/pallas_call | solution.py:780
  34.8 11.0 %forward.1 = (f32[1,1024,384]{2,1,0:T(8,128)}, bf16[1,1024,384]{2,1,0:T(8,128)(2,1)}, bf16[1,1024,256]{2,1,0:T(8,128)(2,1)}, bf16[1,1024,256]{2,1,0:T(8,128)(2,1...) custom-call(bf16[64,896]{1,0:T(8,128)(2,1)} %bitcast.40, ...), custom_call_target="tpu_custom_call" | custom-call | flops 10000000000 | bytes 1000000 | tf_op jit(solution)/shard_map/forward/pallas_call | solution.py:803
  45.8 2.3 collective-permute-start.4
  51.2 3.4 %collective-permute-start.5 = (f32[1,136,384]{2,1,0:T(8,128)S(1)}, f32[1,136,384]{2,1,0:T(8,128)S(1)}, u32[]{:S(2)}, u32[]{:S(2)}) collective-permute-start(f32[1,136,384]{2,1,0:T(8,128)S(1)} %pad_maximum_fusion), channel_id=1, source_target_pairs={{0,8},{4,12},{8,16},{12,20},{16,24},{20,28},{1,9},{5,13},{9,17},{1... | collective-permute-start | bytes 626696 | tf_op jit(solution)/shard_map/ppermute | solution.py:650
  60.1 4.8 %collective-permute-done.6.refs_2_ = f32[1,136,384]{2,1,0:T(8,128)S(1)} collective-permute-done((f32[1,136,384]{2,1,0:T(8,128)S(1)}, f32[1,136,384]{2,1,0:T(8,128)S(1)}, u32[]{:S(2)}, u32[]{:S(2)}) %collective-permute-start.6) | collective-permute-done | bytes 208928 | tf_op jit(solution)/shard_map/ppermute | solution.py:650
  65.7 7.3 %mix.1 = (f32[1,1024,384]{2,1,0:T(8,128)}, f32[1,4,8,256]{3,2,1,0:T(8,128)}, f32[1,4,128,384]{3,2,1,0:T(8,128)}) custom-call(f32[1,136,384]{2,1,0:T(8,128)} %broadcast_select_fusion.1.refs_0_, f32[1,136,384]{2,1,0:T(8,128)} %copy-done.32, f32[1,136,384]{2,1,0:T(8,128)} %copy-done.33, f32[1,136,384]{2,1,0:T(8,128)} %copy-done.34, ...), custom_call_target="tpu_custom_call" | custom-call | flops 6000000000 | bytes 600000 | tf_op jit(solution)/shard_map/mix/pallas_call | solution.py:835
  81.0 7.5 %gate.1 = (f32[1,1024,384]{2,1,0:T(8,128)}, bf16[1,1024,384]{2,1,0:T(8,128)(2,1)}, bf16[1,1024,384]{2,1,0:T(8,128)(2,1)}, f32[1,4,128,384]{3,2,1,0:T(8,128)}, f3...) custom-call(f32[1,4,8,256]{3,2,1,0:T(8,128)} %get-tuple-element.127.refs_0_, ...), custom_call_target="tpu_custom_call" | custom-call | flops 6000000000 | bytes 600000 | tf_op jit(solution)/shard_map/gate/pallas_call | solution.py:856
  88.6 8.5 %out.1 = (f32[1,1024,768]{2,1,0:T(8,128)}, f32[776,768]{1,0:T(8,128)}, bf16[1,1024,192]{2,1,0:T(8,128)(2,1)}, bf16[1,1024,192]{2,1,0:T(8,128)(2,1)}, bf16[1,1024...) custom-call(s32[1]{0:T(128)} %bitcast.me.refs_4_.refs_6_, bf16[1,1024,384]{2,1,0:T(8,128)(2,1)} %get-tuple-element.129.normed_out, ...), custom_call_target="tpu_custom_call" | custom-call | flops 8000000000 | bytes 800000 | tf_op jit(solution)/shard_map/out/pallas_call | solution.py:882
  104.2 4.2 %collective-permute-done.12.refs_1_ = f32[1,136,384]{2,1,0:T(8,128)S(1)} collective-permute-done((f32[1,136,384]{2,1,0:T(8,128)S(1)}, f32[1,136,384]{2,1,0:T(8,128)S(1)}, u32[]{:S(2)}, u32[]{:S(2)}) %collective-permute-start.12) | collective-permute-done | bytes 208928 | tf_op jit(solution)/shard_map/ppermute | solution.py:650
  108.4 6.9 %collective-permute-done.13.refs_2_ = f32[1,136,384]{2,1,0:T(8,128)S(1)} collective-permute-done((f32[1,136,384]{2,1,0:T(8,128)S(1)}, f32[1,136,384]{2,1,0:T(8,128)S(1)}, u32[]{:S(2)}, u32[]{:S(2)}) %collective-permute-start.13) | collective-permute-done | bytes 208928 | tf_op jit(solution)/shard_map/ppermute | solution.py:650
  116.1 15.2 %backward.2 = (bf16[1,512,192]{2,1,0:T(8,128)(2,1)}, bf16[1,512,192]{2,1,0:T(8,128)(2,1)}, bf16[1,512,192]{2,1,0:T(8,128)(2,1)}, bf16[1,512,192]{2,1,0:T(8,128)(...) custom-call(f32[1,136,384]{2,1,0:T(8,128)} %broadcast_select_fusion., ...), custom_call_target="tpu_custom_call" | custom-call | flops 15000000512 | bytes 1500000 | tf_op jit(solution)/shard_map/backward/pallas_call | solution.py:950
  135.1 16.2 %backward.3 = (bf16[1,512,192]{2,1,0:T(8,128)(2,1)}, bf16[1,512,192]{2,1,0:T(8,128)(2,1)}, bf16[1,512,192]{2,1,0:T(8,128)(2,1)}, bf16[1,512,192]{2,1,0:T(8,128)(...) custom-call(f32[1,128,384]{2,1,0:T(8,128)} %get-tuple-element.159.re, ...), custom_call_target="tpu_custom_call" | custom-call | flops 15000000512 | bytes 1500000 | tf_op jit(solution)/shard_map/backward/pallas_call | solution.py:950
  151.3 5.3 %collective-permute-done.19 = bf16[1,512,192]{2,1,0:T(8,128)(2,1)S(1)} collective-permute-done((bf16[1,512,192]{2,1,0:T(8,128)(2,1)}, bf16[1,512,192]{2,1,0:T(8,128)(2,1)S(1)}, u32[]{:S(2)}, u32[]{:S(2)}) %collective-permute-start.19) | collective-permute-done | bytes 196640 | tf_op jit(solution)/shard_map/ppermute | solution.py:654
  161.2 2.6 %collective-permute-start.25 = (bf16[1,16,192]{2,1,0:T(8,128)(2,1)S(1)}, bf16[1,16,192]{2,1,0:T(8,128)(2,1)S(1)}, u32[]{:S(2)}, u32[]{:S(2)}) collective-permute-start(bf16[1,16,192]{2,1,0:T(8,128)(2,1)S(1)} %add_convert_fusion.4), channel_id=1, source_target_pairs={{0,2},{1,3},{2,0},{3,1},{4,6},{5,7},{6,4},{7,5},{8,10},{9,11},{10,... | collective-permute-start | bytes 18440 | tf_op jit(solution)/shard_map/ppermute | solution.py:654
  166.0 5.7 %collective-permute-done.25 = bf16[1,16,192]{2,1,0:T(8,128)(2,1)S(1)} collective-permute-done((bf16[1,16,192]{2,1,0:T(8,128)(2,1)S(1)}, bf16[1,16,192]{2,1,0:T(8,128)(2,1)S(1)}, u32[]{:S(2)}, u32[]{:S(2)}) %collective-permute-start.25) | collective-permute-done | bytes 6176 | tf_op jit(solution)/shard_map/ppermute | solution.py:654
  174.5 3.5 %all-to-all-start = ((bf16[8,64,768]{2,1,0:T(8,128)(2,1)}), bf16[8,64,768]{2,1,0:T(8,128)(2,1)S(1)}, u32[]{:S(2)}, u32[]{:S(2)}) async-start(bf16[8,64,768]{2,1,0:T(8,128)(2,1)} %bitcast.12), calls=%async_computation | async-start | bytes 1572864 | tf_op jit(solution)/shard_map/all_to_all | solution.py:1030
  178.8 3.5 %collective-permute-start.29 = (bf16[1,512,192]{2,1,0:T(8,128)(2,1)}, bf16[1,512,192]{2,1,0:T(8,128)(2,1)}, u32[]{:S(2)}, u32[]{:S(2)}) collective-permute-start(bf16[1,512,192]{2,1,0:T(8,128)(2,1)} %add_convert_fusion.2), channel_id=1, source_target_pairs={{0,2},{1,3},{2,0},{3,1},{4,6},{5,7},{6,4},{7,5},{8,10},{9,11},{10,... | collective-permute-start | bytes 589832 | tf_op jit(solution)/shard_map/ppermute | solution.py:654
  186.2 8.9 %collective-permute-done.29 = bf16[1,512,192]{2,1,0:T(8,128)(2,1)} collective-permute-done((bf16[1,512,192]{2,1,0:T(8,128)(2,1)}, bf16[1,512,192]{2,1,0:T(8,128)(2,1)}, u32[]{:S(2)}, u32[]{:S(2)}) %collective-permute-start.29) | collective-permute-done | bytes 196640 | tf_op jit(solution)/shard_map/ppermute | solution.py:654
  198.5 12.2 %all_gather.3.late = bf16[512,768]{1,0:T(8,128)(2,1)} all-gather(bf16[64,768]{1,0:T(8,128)(2,1)S(1)} %reduce_sum.12), channel_id=1, replica_groups=mesh['seq'=8,'head'=4] {'seq'}, dimensions={0}, use_global_device_ids=true | all-gather | bytes 884736 | tf_op jit(solution)/shard_map/all_gather | solution.py:1034
  210.7 16.9 %all-reduce.7.cloned.1.call-done.early = f32[776,768]{1,0:T(8,128)} async-done(((f32[776,768]{1,0:T(8,128)}), f32[776,768]{1,0:T(8,128)}) %all-reduce.7.cloned.1.call-update) | async-done | bytes 2383888 | tf_op jit(solution)/shard_map/psum | solution.py:902
  227.6 5.1 %unpack.1 = (f32[1,192]{1,0:T(1,128)}, f32[768,2,384]{2,1,0:T(2,128)}, f32[768,2,32]{2,1,0:T(2,128)}, f32[768,6]{1,0:T(8,128)}, f32[4,384]{1,0:T(4,128)}, /*inde...) custom-call(bf16[512,768]{1,0:T(8,128)(2,1)} %all_gather.3.late, ...), custom_call_target="tpu_custom_call" | custom-call | flops 4000000000 | bytes 400000 | tf_op jit(solution)/shard_map/unpack/pallas_call | solution.py:1046
  (197 shorter events, 69.2 us)
Async XLA Ops:
  7.2 220.4 %all-reduce.7.cloned.1.call-start = ((), (), s32[]{:S(2)}) async-start(), calls=%async_computation.1 | async-start | bytes 4767744 | tf_op jit(solution)/shard_map/psum | solution.py:902
  9.9 24.3 %collective-permute-start = (bf16[64,896]{1,0:T(8,128)(2,1)S(1)}, bf16[64,896]{1,0:T(8,128)(2,1)S(1)}, u32[]{:S(2)}, u32[]{:S(2)}) collective-permute-start(bf16[64,896]{1,0:T(8,128)(2,1)S(1)} %bitcast.37), channel_id=1, source_target_pairs={{0,1},{1,2},{2,3},{3,0},{4,5},{5,6},{6,7},{7,4},{8,9},{9,10},{10,1... | collective-permute-start | bytes 344072 | tf_op jit(solution)/shard_map/ppermute | solution.py:760
  13.0 21.2 %collective-permute-start.1 = (bf16[64,896]{1,0:T(8,128)(2,1)S(1)}, bf16[64,896]{1,0:T(8,128)(2,1)S(1)}, u32[]{:S(2)}, u32[]{:S(2)}) collective-permute-start(bf16[64,896]{1,0:T(8,128)(2,1)S(1)} %bitcast.38), channel_id=1, source_target_pairs={{0,2},{1,3},{2,0},{3,1},{4,6},{5,7},{6,4},{7,5},{8,10},{9,11},{10,... | collective-permute-start | bytes 344072 | tf_op jit(solution)/shard_map/ppermute | solution.py:760
  15.5 18.6 %collective-permute-start.2 = (bf16[64,896]{1,0:T(8,128)(2,1)S(1)}, bf16[64,896]{1,0:T(8,128)(2,1)}, u32[]{:S(2)}, u32[]{:S(2)}) collective-permute-start(bf16[64,896]{1,0:T(8,128)(2,1)S(1)} %bitcast.39), channel_id=1, source_target_pairs={{0,3},{1,0},{2,1},{3,2},{4,7},{5,4},{6,5},{7,6},{8,11},{9,8},{10,9... | collective-permute-start | bytes 344072 | tf_op jit(solution)/shard_map/ppermute | solution.py:760
  18.4 15.7 %collective-permute-start.3 = (bf16[1,16,896]{2,1,0:T(8,128)(2,1)S(1)}, bf16[1,16,896]{2,1,0:T(8,128)(2,1)S(1)}, u32[]{:S(2)}, u32[]{:S(2)}) collective-permute-start(bf16[1,16,896]{2,1,0:T(8,128)(2,1)S(1)} %pad_maximum_fusion.2), channel_id=1, source_target_pairs={{0,4},{4,8},{8,12},{12,16},{16,20},{20,24},{24,28},{1,5},{5,9},{9,... | collective-permute-start | bytes 86024 | tf_op jit(solution)/shard_map/ppermute | solution.py:650
  54.6 10.3 %collective-permute-start.6 = (f32[1,136,384]{2,1,0:T(8,128)S(1)}, f32[1,136,384]{2,1,0:T(8,128)S(1)}, u32[]{:S(2)}, u32[]{:S(2)}) collective-permute-start(f32[1,136,384]{2,1,0:T(8,128)S(1)} %pad_maximum_fusion), channel_id=1, source_target_pairs={{0,16},{4,20},{8,24},{12,28},{1,17},{5,21},{9,25},{13,29},{2,18},{... | collective-permute-start | bytes 626696 | tf_op jit(solution)/shard_map/ppermute | solution.py:650
  88.5 10.8 %collective-permute-start.11 = (f32[1,136,384]{2,1,0:T(8,128)}, f32[1,136,384]{2,1,0:T(8,128)S(1)}, u32[]{:S(2)}, u32[]{:S(2)}) collective-permute-start(f32[1,136,384]{2,1,0:T(8,128)} %get-tuple-element.134), channel_id=1, source_target_pairs={{0,4},{4,0},{8,12},{12,8},{16,20},{20,16},{24,28},{28,24},{1,5},{5... | collective-permute-start | bytes 626696 | tf_op jit(solution)/shard_map/ppermute | solution.py:654
  97.1 34.1 %collective-permute-start.15 = (bf16[1,1024,192]{2,1,0:T(8,128)(2,1)}, bf16[1,1024,192]{2,1,0:T(8,128)(2,1)S(1)}, u32[]{:S(2)}, u32[]{:S(2)}) collective-permute-start(bf16[1,1024,192]{2,1,0:T(8,128)(2,1)} %get-tuple-element.156), channel_id=1, source_target_pairs={{0,1},{1,0},{2,3},{3,2},{4,5},{5,4},{6,7},{7,6},{8,9},{9,8},{10,11... | collective-permute-start | bytes 1179656 | tf_op jit(solution)/shard_map/ppermute | solution.py:654
  97.5 33.7 %collective-permute-start.16 = (bf16[1,1024,192]{2,1,0:T(8,128)(2,1)}, bf16[1,1024,192]{2,1,0:T(8,128)(2,1)S(1)}, u32[]{:S(2)}, u32[]{:S(2)}) collective-permute-start(bf16[1,1024,192]{2,1,0:T(8,128)(2,1)} %get-tuple-element.157), channel_id=1, source_target_pairs={{0,1},{1,0},{2,3},{3,2},{4,5},{5,4},{6,7},{7,6},{8,9},{9,8},{10,11... | collective-permute-start | bytes 1179656 | tf_op jit(solution)/shard_map/ppermute | solution.py:654
  99.4 9.0 %collective-permute-start.12 = (f32[1,136,384]{2,1,0:T(8,128)S(1)}, f32[1,136,384]{2,1,0:T(8,128)S(1)}, u32[]{:S(2)}, u32[]{:S(2)}) collective-permute-start(f32[1,136,384]{2,1,0:T(8,128)S(1)} %pad_maximum_fusion.1), channel_id=1, source_target_pairs={{8,0},{12,4},{16,8},{20,12},{24,16},{28,20},{9,1},{13,5},{17,9},{2... | collective-permute-start | bytes 626696 | tf_op jit(solution)/shard_map/ppermute | solution.py:650
  100.7 14.6 %collective-permute-start.13 = (f32[1,136,384]{2,1,0:T(8,128)S(1)}, f32[1,136,384]{2,1,0:T(8,128)S(1)}, u32[]{:S(2)}, u32[]{:S(2)}) collective-permute-start(f32[1,136,384]{2,1,0:T(8,128)S(1)} %pad_maximum_fusion.1), channel_id=1, source_target_pairs={{16,0},{20,4},{24,8},{28,12},{17,1},{21,5},{25,9},{29,13},{18,2},{... | collective-permute-start | bytes 626696 | tf_op jit(solution)/shard_map/ppermute | solution.py:650
  102.0 13.3 %collective-permute-start.14 = (f32[1,136,384]{2,1,0:T(8,128)S(1)}, f32[1,136,384]{2,1,0:T(8,128)S(1)}, u32[]{:S(2)}, u32[]{:S(2)}) collective-permute-start(f32[1,136,384]{2,1,0:T(8,128)S(1)} %pad_maximum_fusion.1), channel_id=1, source_target_pairs={{24,0},{28,4},{25,1},{29,5},{26,2},{30,6},{27,3},{31,7}} | collective-permute-start | bytes 626696 | tf_op jit(solution)/shard_map/ppermute | solution.py:650
  132.2 24.5 %collective-permute-start.17 = (bf16[1,1024,192]{2,1,0:T(8,128)(2,1)S(1)}, bf16[1,1024,192]{2,1,0:T(8,128)(2,1)S(1)}, u32[]{:S(2)}, u32[]{:S(2)}) collective-permute-start(bf16[1,1024,192]{2,1,0:T(8,128)(2,1)S(1)} %add_convert_fusion.1), channel_id=1, source_target_pairs={{0,2},{1,3},{2,0},{3,1},{4,6},{5,7},{6,4},{7,5},{8,10},{9,11},{10,... | collective-permute-start | bytes 1179656 | tf_op jit(solution)/shard_map/ppermute | solution.py:654
  133.1 18.3 %collective-permute-start.18 = (bf16[1,512,192]{2,1,0:T(8,128)(2,1)}, bf16[1,512,192]{2,1,0:T(8,128)(2,1)S(1)}, u32[]{:S(2)}, u32[]{:S(2)}) collective-permute-start(bf16[1,512,192]{2,1,0:T(8,128)(2,1)} %get-tuple-element.180), channel_id=1, source_target_pairs={{0,1},{1,0},{2,3},{3,2},{4,5},{5,4},{6,7},{7,6},{8,9},{9,8},{10,11... | collective-permute-start | bytes 589832 | tf_op jit(solution)/shard_map/ppermute | solution.py:654
  134.7 21.9 %collective-permute-start.19 = (bf16[1,512,192]{2,1,0:T(8,128)(2,1)}, bf16[1,512,192]{2,1,0:T(8,128)(2,1)S(1)}, u32[]{:S(2)}, u32[]{:S(2)}) collective-permute-start(bf16[1,512,192]{2,1,0:T(8,128)(2,1)} %get-tuple-element.181), channel_id=1, source_target_pairs={{0,1},{1,0},{2,3},{3,2},{4,5},{5,4},{6,7},{7,6},{8,9},{9,8},{10,11... | collective-permute-start | bytes 589832 | tf_op jit(solution)/shard_map/ppermute | solution.py:654
  158.8 13.1 %collective-permute-start.20 = (bf16[80,768]{1,0:T(8,128)(2,1)}, bf16[80,768]{1,0:T(8,128)(2,1)S(1)}, u32[]{:S(2)}, u32[]{:S(2)}) collective-permute-start(bf16[80,768]{1,0:T(8,128)(2,1)} %get-tuple-element.186), channel_id=1, source_target_pairs={{0,3},{1,0},{2,1},{3,2},{4,7},{5,4},{6,5},{7,6},{8,11},{9,8},{10,9... | collective-permute-start | bytes 368648 | tf_op jit(solution)/shard_map/ppermute | solution.py:1002
  160.6 11.3 %collective-permute-start.21 = (bf16[80,768]{1,0:T(8,128)(2,1)}, bf16[80,768]{1,0:T(8,128)(2,1)S(1)}, u32[]{:S(2)}, u32[]{:S(2)}) collective-permute-start(bf16[80,768]{1,0:T(8,128)(2,1)} %get-tuple-element.187), channel_id=1, source_target_pairs={{0,2},{1,3},{2,0},{3,1},{4,6},{5,7},{6,4},{7,5},{8,10},{9,11},{10,... | collective-permute-start | bytes 368648 | tf_op jit(solution)/shard_map/ppermute | solution.py:1002
  160.6 11.3 %collective-permute-start.22 = (bf16[80,768]{1,0:T(8,128)(2,1)S(1)}, bf16[80,768]{1,0:T(8,128)(2,1)S(1)}, u32[]{:S(2)}, u32[]{:S(2)}) collective-permute-start(bf16[80,768]{1,0:T(8,128)(2,1)S(1)} %copy-done.35), channel_id=1, source_target_pairs={{0,1},{1,2},{2,3},{3,0},{4,5},{5,6},{6,7},{7,4},{8,9},{9,10},{10,1... | collective-permute-start | bytes 368648 | tf_op jit(solution)/shard_map/ppermute | solution.py:1002
  161.2 10.5 %collective-permute-start.25 = (bf16[1,16,192]{2,1,0:T(8,128)(2,1)S(1)}, bf16[1,16,192]{2,1,0:T(8,128)(2,1)S(1)}, u32[]{:S(2)}, u32[]{:S(2)}) collective-permute-start(bf16[1,16,192]{2,1,0:T(8,128)(2,1)S(1)} %add_convert_fusion.4), channel_id=1, source_target_pairs={{0,2},{1,3},{2,0},{3,1},{4,6},{5,7},{6,4},{7,5},{8,10},{9,11},{10,... | collective-permute-start | bytes 18440 | tf_op jit(solution)/shard_map/ppermute | solution.py:654
  164.7 31.4 %collective-permute-start.26 = (bf16[1,512,192]{2,1,0:T(8,128)(2,1)}, bf16[1,512,192]{2,1,0:T(8,128)(2,1)}, u32[]{:S(2)}, u32[]{:S(2)}) collective-permute-start(bf16[1,512,192]{2,1,0:T(8,128)(2,1)} %get-tuple-element.193), channel_id=1, source_target_pairs={{0,1},{1,0},{2,3},{3,2},{4,5},{5,4},{6,7},{7,6},{8,9},{9,8},{10,11... | collective-permute-start | bytes 589832 | tf_op jit(solution)/shard_map/ppermute | solution.py:654
  171.8 24.3 %collective-permute-start.27 = (bf16[1,512,192]{2,1,0:T(8,128)(2,1)}, bf16[1,512,192]{2,1,0:T(8,128)(2,1)}, u32[]{:S(2)}, u32[]{:S(2)}) collective-permute-start(bf16[1,512,192]{2,1,0:T(8,128)(2,1)} %get-tuple-element.194), channel_id=1, source_target_pairs={{0,1},{1,0},{2,3},{3,2},{4,5},{5,4},{6,7},{7,6},{8,9},{9,8},{10,11... | collective-permute-start | bytes 589832 | tf_op jit(solution)/shard_map/ppermute | solution.py:654
  174.5 21.7 %all-to-all-start = ((bf16[8,64,768]{2,1,0:T(8,128)(2,1)}), bf16[8,64,768]{2,1,0:T(8,128)(2,1)S(1)}, u32[]{:S(2)}, u32[]{:S(2)}) async-start(bf16[8,64,768]{2,1,0:T(8,128)(2,1)} %bitcast.12), calls=%async_computation | async-start | bytes 1572864 | tf_op jit(solution)/shard_map/all_to_all | solution.py:1030
  178.8 16.2 %collective-permute-start.29 = (bf16[1,512,192]{2,1,0:T(8,128)(2,1)}, bf16[1,512,192]{2,1,0:T(8,128)(2,1)}, u32[]{:S(2)}, u32[]{:S(2)}) collective-permute-start(bf16[1,512,192]{2,1,0:T(8,128)(2,1)} %add_convert_fusion.2), channel_id=1, source_target_pairs={{0,2},{1,3},{2,0},{3,1},{4,6},{5,7},{6,4},{7,5},{8,10},{9,11},{10,... | collective-permute-start | bytes 589832 | tf_op jit(solution)/shard_map/ppermute | solution.py:654
  197.3 41.7 %collective-permute-start.28 = (bf16[1,512,192]{2,1,0:T(8,128)(2,1)S(1)}, bf16[1,512,192]{2,1,0:T(8,128)(2,1)S(1)}, u32[]{:S(2)}, u32[]{:S(2)}) collective-permute-start(bf16[1,512,192]{2,1,0:T(8,128)(2,1)S(1)} %add_convert_fusion.3), channel_id=1, source_target_pairs={{0,2},{1,3},{2,0},{3,1},{4,6},{5,7},{6,4},{7,5},{8,10},{9,11},{10,... | collective-permute-start | bytes 589832 | tf_op jit(solution)/shard_map/ppermute | solution.py:654
  (52 other events, 389.0 us)
Sparse Core Ops, SparseCore 0:
  157.0 70.6 all-reduce.6

commit v3 on v2

--- a/solution.py
+++ b/solution.py
@@ -339,19 +339,25 @@
         ref[...] = block
 
 
-def out_kernel(parts, me, normed_out, cot, dgate, normed, wout, win, gain, skip, back, grads, *branch):
+def out_kernel(parts, me, normed_out, cot, dgate, normed, wout, win, back, grads, *rest):
     channels = wout.shape[0]
-    width = wout.shape[1]
+    branch, total = rest[:parts], rest[parts]
 
     @pl.when((pl.program_id(1) == 0) & (pl.program_id(0) == 0))
     def _():
-        grads[...] = jnp.zeros_like(grads)
-        grads[2 * channels : 2 * channels + 1, :channels] = gain[...]
-        grads[2 * channels + 1 : 2 * channels + 2, :LANES] = collect_row(skip[...])
+        total[...] = jnp.zeros_like(total)
 
     store_parts(branch, dot(normed_out[...], wout[...]), me[0])
-    grads[:channels, :] += dot_tn(normed_out[...], cot[...])
-    grads[channels : 2 * channels, :] += dot_tn(dgate[...], normed[...])
+    total[:channels, :] += dot_tn(normed_out[...], cot[...])
+    total[channels : 2 * channels, :] += dot_tn(dgate[...], normed[...])
+
+    @pl.when(
+        (pl.program_id(1) == pl.num_programs(1) - 1)
+        & (pl.program_id(0) == pl.num_programs(0) - 1)
+    )
+    def _():
+        grads[...] = rounded(total[...])
+
     back[...] = dot_nt(dgate[...], win[:, channels:])
 
 
@@ -391,15 +397,16 @@
     carried, refs = (refs[:0], refs) if start_call else (refs[:6], refs[6:])
     (
         me, tok, halo, marked, normed, xpre, xprev, halo_x, spre, sprev, halo_s, xact, bc, yin, dy,
-        back, step, cum, raw, run_in, states, entering, fades, win, ws, wst, hp, ci, cs, gain,
-    ), refs = refs[:30], refs[30:]
+        back, step, cum, raw, run_in, states, entering, fades, win, ws, wst, hp, ci, cs, gain, gain_out, skip_out,
+    ), refs = refs[:32], refs[32:]
     gtok, refs = refs[:parts], refs[parts:]
     if end_call:
-        (packed, *rest), refs = refs[: 1 + 2 * parts], refs[1 + 2 * parts :]
-        edge_out, state_out = rest[:parts], rest[parts:]
+        (packed, *state_out), refs = refs[: 1 + parts], refs[1 + parts :]
     else:
         carry_out, refs = refs[:6], refs[6:]
-    ext_x, ext_s, buf_x, buf_s, state, grad_x, grad_s, grad_misc, grad_ci, grad_cs = refs
+    (
+        ext_x, ext_s, buf_x, buf_s, state, grad_x, grad_s, grad_misc, grad_ci, grad_cs, edges,
+    ) = refs
     channels = xact.shape[-1]
     width = tok.shape[-1]
     half = bc.shape[-1] // 2
@@ -570,7 +577,7 @@
         nothing = jnp.zeros_like(high)
         high, rest = jnp.where(final, high, nothing), jnp.where(final, everything - high, nothing)
         edge = jnp.where(place == 0, high, jnp.where(place == 1, rest, grad))
-        store_parts(edge_out, edge, me[0])
+        edges[row_id] = edge
 
         @pl.when(final)
         def _():
@@ -591,6 +598,8 @@
             packed[channels : channels + EDGE, :] = rounded(
                 jnp.concatenate([misc[:11], fine[9:11], misc[13:]], axis=0)
             )
+            grad_ci[K + 1 : K + 2, :] = gain_out[...]
+            grad_ci[K + 2 : K + 3, :LANES] = collect_row(skip_out[...])
             packed[channels + EDGE : channels + 2 * EDGE, :] = both_halves(grad_ci[...])
             own = half // parts
             taps = grad_cs[...]
@@ -601,6 +610,45 @@
                 ref[2 * own :, :] = both_halves(
                     jnp.concatenate([taps[:, lo:hi], taps[:, half + lo : half + hi]], axis=1)
                 )
+            own = width // parts
+            for line in range(edges.shape[0]):
+                shift = (parts - me[0]) % parts * own
+                turned = rounded(pltpu.roll(edges[line], shift, 1))
+                for part, ref in enumerate(state_out):
+                    begin = (parts - part) % parts * own
+                    ref[2 * (half // parts) :, LANES + line * own : LANES + (line + 1) * own] = (
+                        turned[:, begin : begin + own]
+                    )
+
+
+def merge_kernel(own_width, packed, *refs):
+    *pieces, late, edge = refs
+    base = packed.shape[0]
+    total = pieces[0][...].astype(F32)
+    for piece in pieces[1:]:
+        total = total + piece[...].astype(F32)
+    body = total.shape[0] - EDGE
+    rows = edge.shape[0]
+    late[:base, :] = packed[...]
+    late[base : base + body, :] = rounded(total[:body])
+    tail = total[body:]
+    for line in range(rows):
+        edge[line] = tail[:, LANES + line * own_width : LANES + (line + 1) * own_width]
+
+    def both_halves(block):
+        upper_half = block.astype(BF16).astype(F32)
+        return jnp.concatenate([upper_half, block - upper_half], axis=0)
+
+    place = base + body
+    late[place : place + EDGE, :] = rounded(both_halves(tail[:8] + tail[8:]))
+    place += EDGE
+    begin = LANES + (rows - 1) * own_width
+    gain = jnp.broadcast_to(tail[0:1] + tail[1:2], (8, tail.shape[1]))
+    late[place : place + EDGE, :] = jnp.zeros((EDGE, tail.shape[1]), BF16)
+    late[place : place + EDGE, :own_width] = rounded(both_halves(gain))[:, begin : begin + own_width]
+    if late.shape[0] > place + EDGE:
+        rest = late.shape[0] - place - EDGE
+        late[place + EDGE :, :] = jnp.zeros((rest, tail.shape[1]), BF16)
 
 
 def unpack_kernel(
@@ -608,23 +656,24 @@
     taps_bias, step_bias, decay, skip, gain_out, out_weight,
 ):
     channels, width = out_weight.shape
-    own = state.shape[-1]
+    own = state.shape[1]
     inner[:, 0, :] = late[:channels, :].astype(F32).T
-    inner[:, 1, :] = early[channels : 2 * channels, :].T
+    inner[:, 1, :] = early[channels : 2 * channels, :].astype(F32).T
     base = channels
     misc = late[base : base + EDGE, :].astype(F32)
-    step[...] = misc.T[:, :head_count]
-    step_bias[...] = (misc[9:10] + misc[11:12])[:, :head_count]
-    decay[...] = (misc[10:11] + misc[12:13])[:, :head_count]
+    step[...] = misc[:head_count]
+    step_bias[...] = (misc[9] + misc[11])[:head_count]
+    decay[...] = (misc[10] + misc[12])[:head_count]
     base += EDGE
     block = late[base : base + EDGE, :].astype(F32)
     block = block[:8] + block[8:]
     conv[...] = block[:K, :channels]
-    conv_bias[...] = block[K : K + 1, :channels]
+    conv_bias[...] = block[K, :channels]
+    gain_out[...] = block[K + 1, :channels]
+    skip[...] = block[K + 2, :head_count]
     base += EDGE
-    weights = late[base : base + 2 * own, :].astype(F32).T
-    state[:, 0, :] = weights[:, :own]
-    state[:, 1, :] = weights[:, own:]
+    state[0] = late[base : base + own, :].astype(F32)
+    state[1] = late[base + own : base + 2 * own, :].astype(F32)
     base += 2 * own
     block = late[base : base + EDGE, :].astype(F32)
     block = block[:8] + block[8:]
@@ -634,10 +683,8 @@
     taps_bias[1:2, :] = block[K : K + 1, own : 2 * own]
     base += EDGE
     block = late[base : base + EDGE, :].astype(F32)
-    gain[...] = (block[0:1] + block[1:2])[:, :own_width]
-    out_weight[...] = early[:channels, :]
-    gain_out[...] = early[2 * channels : 2 * channels + 1, :channels]
-    skip[...] = early[2 * channels + 1 : 2 * channels + 2, :head_count]
+    gain[...] = (block[0] + block[8])[:own_width]
+    out_weight[...] = early[:channels, :].astype(F32)
 
 
 def ring(axis, distance):
@@ -664,6 +711,12 @@
     if len(parts) == 4:
         return [crossed(rounded(parts[2].astype(F32) + near[0].astype(F32)), axis, 2)]
     return []
+
+
+def send_all(parts, axis):
+    if len(parts) == 4:
+        return [crossed(part, axis, mask) for mask, part in enumerate(parts) if mask]
+    return send_near(parts, axis)
 
 
 def add_up(parts, near, far):
@@ -678,7 +731,7 @@
     return jax.tree.unflatten(tree, lax.optimization_barrier(flat))
 
 
-def chained(message, reverse):
+def chained(message, reverse, beside):
     count = lax.axis_size("seq")
     core = lax.axis_index("seq") % 2
     later = core == (0 if reverse else 1)
@@ -692,15 +745,13 @@
     neutral = (lax.broadcasted_iota(jnp.int32, message.shape, 1) >= LANES).astype(F32)
     near = jnp.where(later, other, neutral)
     sign = -2 if reverse else 2
-    return [near] + [shifted(pair, "seq", sign * d) for d in range(1, count // 2)]
-
-
-def all_sum(whole, axis):
-    count = lax.axis_size(axis)
-    chunk = whole.shape[0] // count
-    parts = lax.all_to_all(whole.reshape(count, chunk, -1), axis, 0, 0, tiled=True)
-    own = rounded(jnp.sum(parts.astype(F32), axis=0))
-    return lax.all_gather(own, axis, axis=0, tiled=True).astype(F32)
+    pair, beside = ordered(pair, beside)
+    return beside, [near] + [shifted(pair, "seq", sign * d) for d in range(1, count // 2)]
+
+
+def gather_sum(parts):
+    total = rounded(jnp.sum(parts.astype(F32), axis=0))
+    return lax.all_gather(total, "seq", axis=0, tiled=True)
 
 
 def on_device(
@@ -796,8 +847,6 @@
         name="project",
         cost_estimate=cost(6),
     )(tokens, gain_in, win, wst, hp)
-    dn = jnp.einsum("rsd,cd->rsc", cotangent, out_weight, preferred_element_type=F32)
-
     (
         yin, xact, bc, spre, fresh, fades, message, halo_x, halo_s, run_all, ws, cs,
     ) = pl.pallas_call(
@@ -831,7 +880,8 @@
         cost_estimate=cost(10),
     )(*found, marked, normed, xpre, step, cum, win, halo, gain_in, ci)
 
-    arrived = chained(message, False)
+    beside, arrived = chained(message, False, cotangent)
+    dn = jnp.einsum("rsd,cd->rsc", beside, out_weight, preferred_element_type=F32)
     mixer, sums, entry_states = pl.pallas_call(
         functools.partial(mix_kernel, len(arrived)),
         grid=grid,
@@ -878,28 +928,29 @@
         cost_estimate=cost(6),
     )(*sums_all, mixer, gate, dn, xact, bc, cum, marked, gain_out, hp, fades)
 
-    returned = chained(back_message, True)
+    normed_out, returned = chained(back_message, True, normed_out)
     back, early, *branch = pl.pallas_call(
         functools.partial(out_kernel, head_devices),
         grid=grid,
         in_specs=[
             scalar, block(channels), block(width), block(channels), block(width),
-            whole((channels, width)), whole((width, 2 * channels)), whole((1, channels)),
-            whole((1, channels)),
-        ],
-        out_specs=[block(width), whole((2 * channels + 8, width))]
+            whole((channels, width)), whole((width, 2 * channels)),
+        ],
+        out_specs=[block(width), whole((2 * channels, width))]
         + [block(own_width)] * head_devices,
-        out_shape=[act(width), sds((2 * channels + 8, width))]
+        out_shape=[act(width), sds((2 * channels, width), BF16)]
         + [act(own_width, BF16)] * head_devices,
+        scratch_shapes=[pltpu.VMEM((2 * channels, width), F32)],
         compiler_params=PARAMS,
         name="out",
         cost_estimate=cost(8),
-    )(me, normed_out, cotangent, dgate, normed, out_weight, win, grad_gain_out, grad_skip)
+    )(me, normed_out, cotangent, dgate, normed, out_weight, win)
 
     column = lax.axis_index("head") * own_width
     own_tokens = lax.dynamic_slice_in_dim(tokens, column, own_width, 2).astype(F32)
-    branch_near = send_near(branch, "head")
-    early = lax.psum(early, "seq")
+    early, returned = ordered(early, returned)
+    early = lax.all_to_all(early.reshape(seq_count, -1, width), "seq", 0, 0, tiled=True)
+    branch_near = send_all(branch, "head")
 
     late_rows = channels + 3 * EDGE + 2 * own_state + EDGE
     chunk = -(-late_rows // (seq_count * EDGE)) * EDGE
@@ -938,10 +989,8 @@
         out_shape = [sds((rows, steps * GROUP, own_width), BF16)] * head_devices
         if end_call:
             out_specs += [whole((packed_rows, width))]
-            out_specs += [per_row(EDGE, own_width)] * head_devices
             out_specs += [whole((piece_rows, width))] * head_devices
             out_shape += [sds((packed_rows, width), BF16)]
-            out_shape += [sds((rows, EDGE, own_width), BF16)] * head_devices
             out_shape += [sds((piece_rows, width), BF16)] * head_devices
         else:
             out_specs += carry_specs
@@ -961,6 +1010,7 @@
                 group_tile(LANES, channels), group_tile(8, channels),
                 whole((width, 2 * channels)), whole((states, width)), whole((width, LANES)),
                 whole((8, LANES)), whole((8, channels)), whole((8, states)), whole((1, width)),
+                whole((1, channels)), whole((1, channels)),
             ],
             out_specs=out_specs,
             out_shape=out_shape,
@@ -972,7 +1022,7 @@
                 pltpu.VMEM((LANES, channels), F32),
                 pltpu.VMEM((channels, width), F32), pltpu.VMEM((states, width), F32),
                 pltpu.VMEM((EDGE, width), F32), pltpu.VMEM((8, channels), F32),
-                pltpu.VMEM((8, states), F32),
+                pltpu.VMEM((8, states), F32), pltpu.VMEM((rows, EDGE, width), F32),
             ],
             compiler_params=PARAMS,
             name="backward",
@@ -980,60 +1030,46 @@
         )(
             *lead, *carried, me, tokens, halo, marked, normed, xpre, xpre, halo_x, spre, spre,
             halo_s, xact, bc, yin, dy, back, step, cum, raw, run_all, entry_states, entering,
-            fades, win, ws, wst, hp, ci, cs, gain_in,
+            fades, win, ws, wst, hp, ci, cs, gain_in, grad_gain_out, grad_skip,
         )
 
     first = groups // 2
     if first:
         outs = backward_call(True, False, first, groups - first, [])
-        outs, branch_near = ordered(outs, branch_near)
-        branch_far = send_far(branch, branch_near, "head")
+        outs, early = ordered(outs, early)
+        early = gather_sum(early)
         late_parts, carried = outs[:head_devices], outs[head_devices:]
         late_near = send_near(late_parts, "head")
         outs = backward_call(False, True, 0, first, carried)
-        outs, branch_far, late_near = ordered(outs, branch_far, late_near)
+        outs, branch_near, late_near = ordered(outs, branch_near, late_near)
     else:
         outs = backward_call(True, True, 0, groups, [])
-        branch_far = send_far(branch, branch_near, "head")
+        early = gather_sum(early)
     gtok, packed = outs[:head_devices], outs[head_devices]
-    edge_parts = outs[head_devices + 1 : 2 * head_devices + 1]
-    state_parts = outs[2 * head_devices + 1 :]
+    state_parts = outs[head_devices + 1 :]
     state_pieces = [
         lax.ppermute(state_parts[d], "head", ring("head", -d)) for d in range(1, head_devices)
     ]
-    edge_near = send_near(edge_parts, "head")
-    edge_far = send_far(edge_parts, edge_near, "head")
-    state_total = state_parts[0].astype(F32)
-    for piece in state_pieces:
-        state_total = state_total + piece.astype(F32)
-    edge = add_up(edge_parts, edge_near, edge_far)
     gtok_near = send_near(gtok, "head")
     if first:
         late_far = send_far(late_parts, late_near, "head")
-    output = rounded(own_tokens + add_up(branch, branch_near, branch_far))
-    gain_row = (edge[rows - 1, 0] + edge[rows - 1, 1])[None]
-    gain_high = gain_row.astype(BF16).astype(F32)
-    gain_rows = jnp.pad(
-        jnp.concatenate([gain_high, gain_row - gain_high]),
-        ((0, EDGE - 2), (0, width - own_width)),
-    )
-    taps = state_total[2 * own_state : 2 * own_state + 8] + state_total[2 * own_state + 8 :]
-    taps_high = taps.astype(BF16).astype(F32)
-    late = jnp.concatenate(
-        [
-            packed, rounded(state_total[: 2 * own_state]), rounded(taps_high),
-            rounded(taps - taps_high), rounded(gain_rows),
-            jnp.zeros((chunk * seq_count - late_rows, width), BF16),
-        ],
-        axis=0,
-    )
+    late, edge = pl.pallas_call(
+        functools.partial(merge_kernel, own_width),
+        out_shape=[
+            sds((chunk * seq_count, width), BF16), sds((rows, EDGE, own_width)),
+        ],
+        compiler_params=pltpu.CompilerParams(vmem_limit_bytes=62 * 2**20),
+        cost_estimate=cost(2),
+        name="merge",
+    )(packed, state_parts[0], *state_pieces)
+    late, gtok_near[0] = ordered(late, gtok_near[0])
     parts = lax.all_to_all(late.reshape(seq_count, chunk, -1), "seq", 0, 0, tiled=True)
+    gtok_far = send_far(gtok, gtok_near, "head")
     parts, gtok_near = ordered(parts, gtok_near)
-    gtok_far = send_far(gtok, gtok_near, "head")
+    output = rounded(own_tokens + add_up(branch, branch_near, []))
     from_next = shifted(edge, "seq", -1)[:, EDGE - K + 1 :]
-    late = lax.all_gather(
-        rounded(jnp.sum(parts.astype(F32), axis=0)), "seq", axis=0, tiled=True
-    )
+    late = gather_sum(parts)
+    late, gtok_far = ordered(late, gtok_far)
     token_sums = [add_up(gtok, gtok_near, gtok_far)]
     if first:
         token_sums.append(add_up(late_parts, late_near, late_far))
@@ -1046,20 +1082,20 @@
     outs = pl.pallas_call(
         functools.partial(unpack_kernel, own_width, head_count),
         out_shape=[
-            sds((1, own_width)), sds((width, 2, channels)), sds((width, 2, own_state)),
-            sds((width, head_count)), sds((K, channels)), sds((1, channels)),
-            sds((K, 2, own_state)), sds((2, own_state)), sds((1, head_count)),
-            sds((1, head_count)), sds((1, head_count)), sds((1, channels)),
+            sds((own_width,)), sds((width, 2, channels)), sds((2, own_state, width)),
+            sds((head_count, width)), sds((K, channels)), sds((channels,)),
+            sds((K, 2, own_state)), sds((2, own_state)), sds((head_count,)),
+            sds((head_count,)), sds((head_count,)), sds((channels,)),
             sds((channels, width)),
         ],
         compiler_params=pltpu.CompilerParams(vmem_limit_bytes=62 * 2**20),
         cost_estimate=cost(4),
         name="unpack",
     )(late, early)
-    one_row = (0, 5, 8, 9, 10, 11)
-    return (output, grad_tokens) + tuple(
-        out[0] if place in one_row else out for place, out in enumerate(outs)
-    )
+    outs = list(outs)
+    outs[2] = outs[2].transpose(2, 0, 1)
+    outs[3] = outs[3].T
+    return (output, grad_tokens) + tuple(outs)
 
 
 def solution(mesh):

time: 251 us -> 220 us (0.88)
  waiting for transfers between devices: 59.7 us -> 30.6 us
  starting transfers between devices: 47 us -> 50.7 us
  local copies, waits for them, and re-layouts: 18.9 us -> 15.3 us
  other arithmetic: 17.7 us -> 15.1 us
    psum x1 -> x0, waiting for transfers between devices: 16.9 us -> none  [on_device(): early = lax.psum(early, 'seq')]
    ppermute x8, waiting for transfers between devices: 17.2 us -> 2.81 us  [shifted(): lax.ppermute(block, axis, [(i - distance, i) for i in devices if i - dist...]
    ppermute x14 -> x11, waiting for transfers between devices: 20.6 us -> 8.13 us  [crossed(): lax.ppermute(block, axis, [(i, i ^ mask) for i in range(lax.axis_size(axi...]
    all_to_all x1, waiting for transfers between devices: 0.01 us -> 8.42 us  [on_device(): lax.all_to_all(late.reshape(seq_count, chunk, -1), 'seq', 0, 0, tiled=True)]
    all_to_all x0 -> x1, starting transfers between devices: none -> 6.01 us  [on_device(): lax.all_to_all(early.reshape(seq_count, -1, width), 'seq', 0, 0, tiled=True)]
    ppermute x14 -> x11, starting transfers between devices: 18.1 us -> 12.9 us  [crossed(): lax.ppermute(block, axis, [(i, i ^ mask) for i in range(lax.axis_size(axi...]
    ppermute x3, waiting for transfers between devices: 0.01 us -> 4.85 us  [on_device(): lax.ppermute(state_parts[d], 'head', ring('head', -d))]
    unnamed x95 -> x67, local copies, waits for them, and re-layouts: 13.9 us -> 9.67 us
  transfers between devices with their start and end apart: 33 -> 31, of which waited for: 12 -> 11; matrix products, arithmetic and copies ran while one was open for 11% -> 10% of each run, Pallas kernels for 21% -> 22%
where the time goes in v3:
time: 220 us; the launch traced here: 219 us
  Pallas kernels  78.8 us (36%)
  starting transfers between devices  50.7 us (23%)
  waiting for transfers between devices  30.6 us (14%)
  local copies, waits for them, and re-layouts  15.3 us (7%)
  other arithmetic  15.1 us (7%)
  between operations  14.5 us (7%)
  blocking collectives  10.5 us (5%)
  matrix products  3.23 us (1%)
    pallas_call x2, Pallas kernels, backward_call(): pl.pallas_call(functools.partial(backward_kernel, start_call, end_call, l...  31.3 us
    ppermute x8, starting transfers between devices, shifted(): lax.ppermute(block, axis, [(i - distance, i) for i in devices if i - dist...  13.5 us
    ppermute x11, starting transfers between devices, crossed(): lax.ppermute(block, axis, [(i, i ^ mask) for i in range(lax.axis_size(axi...  12.9 us
    pallas_call x1, Pallas kernels, on_device(): pl.pallas_call(functools.partial(forward_kernel, len(found)), grid=grid,...  11.1 us
    all_gather x1, blocking collectives, gather_sum(): return lax.all_gather(total, 'seq', axis=0, tiled=True)  10.5 us
    unnamed x67, local copies, waits for them, and re-layouts  9.67 us
    pallas_call x1, Pallas kernels, on_device(): pl.pallas_call(functools.partial(out_kernel, head_devices), grid=grid, in...  8.92 us
    all_to_all x1, waiting for transfers between devices, on_device(): lax.all_to_all(late.reshape(seq_count, chunk, -1), 'seq', 0, 0, tiled=True)  8.42 us
  transfers between devices with their start and end apart: 31, of which 11 were waited for; matrix products, arithmetic and copies ran while one was open for 10% of the time, Pallas kernels for 22%

profile of v3, /device:TPU:0, one launch (start us, length us, event | category | flops | bytes accessed | tf_op | source)
XLA Modules:
  0.0 218.8 jit_solution(18326319230862432503)
XLA Ops:
  9.9 3.1 %collective-permute-start = (bf16[64,896]{1,0:T(8,128)(2,1)S(1)}, bf16[64,896]{1,0:T(8,128)(2,1)S(1)}, u32[]{:S(2)}, u32[]{:S(2)}) collective-permute-start(bf16[64,896]{1,0:T(8,128)(2,1)S(1)} %bitcast.32), channel_id=1, source_target_pairs={{0,1},{1,2},{2,3},{3,0},{4,5},{5,6},{6,7},{7,4},{8,9},{9,10},{10,1... | collective-permute-start | bytes 344072 | tf_op jit(solution)/shard_map/ppermute | solution.py:811
  12.9 2.6 %collective-permute-start.1 = (bf16[64,896]{1,0:T(8,128)(2,1)S(1)}, bf16[64,896]{1,0:T(8,128)(2,1)S(1)}, u32[]{:S(2)}, u32[]{:S(2)}) collective-permute-start(bf16[64,896]{1,0:T(8,128)(2,1)S(1)} %bitcast.33), channel_id=1, source_target_pairs={{0,2},{1,3},{2,0},{3,1},{4,6},{5,7},{6,4},{7,5},{8,10},{9,11},{10,... | collective-permute-start | bytes 344072 | tf_op jit(solution)/shard_map/ppermute | solution.py:811
  19.7 2.5 %copy.36 = bf16[96,8,2,384]{3,1,2,0:T(8,128)(2,1)} copy(bf16[96,8,2,384]{3,2,1,0:T(2,128)(2,1)} %bitcast.24) | data formatting | bytes 2359296
  24.3 6.2 %project.1 = (bf16[1,1024,768]{2,1,0:T(8,128)(2,1)}, bf16[1,1024,384]{2,1,0:T(8,128)(2,1)}, f32[1,1024,384]{2,1,0:T(8,128)}, f32[1,1024,128]{2,1,0:T(8,128)}, f3...) custom-call(bf16[1,1024,768]{2,1,0:T(8,128)(2,1)} %refs_7_.1, f32[1,768]{1,0:T(1,128)} %broadcast_in_dim.33.gain.refs_11_.refs_33_.refs_35_, ...), custom_call_target="tpu_custom_call" | custom-call | flops 6000000000 | bytes 600000 | tf_op jit(solution)/shard_map/project/pallas_call | solution.py:831
  33.1 11.1 %forward.1 = (f32[1,1024,384]{2,1,0:T(8,128)}, bf16[1,1024,384]{2,1,0:T(8,128)(2,1)}, bf16[1,1024,256]{2,1,0:T(8,128)(2,1)}, bf16[1,1024,256]{2,1,0:T(8,128)(2,1...) custom-call(bf16[64,896]{1,0:T(8,128)(2,1)} %bitcast.35, ...), custom_call_target="tpu_custom_call" | custom-call | flops 10000000000 | bytes 1000000 | tf_op jit(solution)/shard_map/forward/pallas_call | solution.py:852
  44.2 2.3 %collective-permute-start.4 = (f32[1,136,384]{2,1,0:T(8,128)}, f32[1,136,384]{2,1,0:T(8,128)S(1)}, u32[]{:S(2)}, u32[]{:S(2)}) collective-permute-start(f32[1,136,384]{2,1,0:T(8,128)} %get-tuple-element.127), channel_id=1, source_target_pairs={{0,4},{4,0},{8,12},{12,8},{16,20},{20,16},{24,28},{28,24},{1,5},{5... | collective-permute-start | bytes 626696 | tf_op jit(solution)/shard_map/ppermute | solution.py:701
  49.5 3.4 %collective-permute-start.5 = (f32[1,136,384]{2,1,0:T(8,128)S(1)}, f32[1,136,384]{2,1,0:T(8,128)S(1)}, u32[]{:S(2)}, u32[]{:S(2)}) collective-permute-start(f32[1,136,384]{2,1,0:T(8,128)S(1)} %pad_maximum_fusion), channel_id=1, source_target_pairs={{0,8},{4,12},{8,16},{12,20},{16,24},{20,28},{1,9},{5,13},{9,17},{1... | collective-permute-start | bytes 626696 | tf_op jit(solution)/shard_map/ppermute | solution.py:697
  56.4 3.2 %fusion.2.refs_8_.refs_6_ = f32[1,1024,384]{2,1,0:T(8,128)} fusion(bf16[384,768]{1,0:T(8,128)(2,1)} %wout.1, bf16[1,1024,768]{2,1,0:T(8,128)(2,1)S(1)} %copy-done), kind=kOutput, calls=%fused_computation.2 | convolution fusion | flops 603979776 | bytes 3735552 | tf_op jit(solution)/shard_map/rsd,cd->rsc/dot_general | solution.py:884
  60.4 2.8 %collective-permute-done.6.refs_2_ = f32[1,136,384]{2,1,0:T(8,128)S(1)} collective-permute-done((f32[1,136,384]{2,1,0:T(8,128)S(1)}, f32[1,136,384]{2,1,0:T(8,128)S(1)}, u32[]{:S(2)}, u32[]{:S(2)}) %collective-permute-start.6) | collective-permute-done | bytes 208928 | tf_op jit(solution)/shard_map/ppermute | solution.py:697
  64.6 7.3 %mix.1 = (f32[1,1024,384]{2,1,0:T(8,128)}, f32[1,4,8,256]{3,2,1,0:T(8,128)}, f32[1,4,128,384]{3,2,1,0:T(8,128)}) custom-call(f32[1,136,384]{2,1,0:T(8,128)} %broadcast_select_fusion.1.refs_0_, f32[1,136,384]{2,1,0:T(8,128)} %copy-done.19, f32[1,136,384]{2,1,0:T(8,128)} %copy-done.20, f32[1,136,384]{2,1,0:T(8,128)} %copy-done.21, ...), custom_call_target="tpu_custom_call" | custom-call | flops 6000000000 | bytes 600000 | tf_op jit(solution)/shard_map/mix/pallas_call | solution.py:885
  76.1 2.2 %collective-permute-done.8.refs_1_ = f32[1,4,8,256]{3,2,1,0:T(8,128)S(1)} collective-permute-done((f32[1,4,8,256]{3,2,1,0:T(8,128)}, f32[1,4,8,256]{3,2,1,0:T(8,128)S(1)}, u32[]{:S(2)}, u32[]{:S(2)}) %collective-permute-start.8) | collective-permute-done | bytes 32800 | tf_op jit(solution)/shard_map/ppermute | solution.py:904
  80.0 7.5 %gate.1 = (f32[1,1024,384]{2,1,0:T(8,128)}, bf16[1,1024,384]{2,1,0:T(8,128)(2,1)}, bf16[1,1024,384]{2,1,0:T(8,128)(2,1)}, f32[1,4,128,384]{3,2,1,0:T(8,128)}, f3...) custom-call(f32[1,4,8,256]{3,2,1,0:T(8,128)} %get-tuple-element.136.refs_0_, ...), custom_call_target="tpu_custom_call" | custom-call | flops 6000000000 | bytes 600000 | tf_op jit(solution)/shard_map/gate/pallas_call | solution.py:906
  94.8 8.9 %out.1 = (f32[1,1024,768]{2,1,0:T(8,128)}, bf16[768,768]{1,0:T(8,128)(2,1)}, bf16[1,1024,192]{2,1,0:T(8,128)(2,1)}, bf16[1,1024,192]{2,1,0:T(8,128)(2,1)}, bf16[...) custom-call(s32[1]{0:T(128)} %bitcast.me.refs_4_.refs_6_, bf16[1,1024,384]{2,1,0:T(8,128)(2,1)} %get-tuple-element.140.normed_out, ...), custom_call_target="tpu_custom_call" | custom-call | flops 8000000000 | bytes 800000 | tf_op jit(solution)/shard_map/out/pallas_call | solution.py:932
  109.8 6.0 %all-to-all-start = ((bf16[8,96,768]{2,1,0:T(8,128)(2,1)}), bf16[8,96,768]{2,1,0:T(8,128)(2,1)S(1)}, u32[]{:S(2)}, u32[]{:S(2)}) async-start(bf16[8,96,768]{2,1,0:T(8,128)(2,1)} %bitcast.30), calls=%async_computation | async-start | bytes 2359296 | tf_op jit(solution)/shard_map/all_to_all | solution.py:952
  116.0 15.2 %backward.2 = (bf16[1,512,192]{2,1,0:T(8,128)(2,1)}, bf16[1,512,192]{2,1,0:T(8,128)(2,1)}, bf16[1,512,192]{2,1,0:T(8,128)(2,1)}, bf16[1,512,192]{2,1,0:T(8,128)(...) custom-call(f32[1,136,384]{2,1,0:T(8,128)} %broadcast_select_fusion., ...), custom_call_target="tpu_custom_call" | custom-call | flops 15000000512 | bytes 1500000 | tf_op jit(solution)/shard_map/backward/pallas_call | solution.py:999
  135.5 16.1 %backward.3 = (bf16[1,512,192]{2,1,0:T(8,128)(2,1)}, bf16[1,512,192]{2,1,0:T(8,128)(2,1)}, bf16[1,512,192]{2,1,0:T(8,128)(2,1)}, bf16[1,512,192]{2,1,0:T(8,128)(...) custom-call(f32[1,128,384]{2,1,0:T(8,128)} %get-tuple-element.173.re, ...), custom_call_target="tpu_custom_call" | custom-call | flops 15000000512 | bytes 1500000 | tf_op jit(solution)/shard_map/backward/pallas_call | solution.py:999
  155.9 2.3 %collective-permute-start.23 = (bf16[1,512,192]{2,1,0:T(8,128)(2,1)}, bf16[1,512,192]{2,1,0:T(8,128)(2,1)S(1)}, u32[]{:S(2)}, u32[]{:S(2)}) collective-permute-start(bf16[1,512,192]{2,1,0:T(8,128)(2,1)} %get-tuple-element.203), channel_id=1, source_target_pairs={{0,1},{1,0},{2,3},{3,2},{4,5},{5,4},{6,7},{7,6},{8,9},{9,8},{10,11... | collective-permute-start | bytes 589832 | tf_op jit(solution)/shard_map/ppermute | solution.py:701
  161.6 4.8 %collective-permute-done.21.refs_2_ = bf16[80,768]{1,0:T(8,128)(2,1)S(1)} collective-permute-done((bf16[80,768]{1,0:T(8,128)(2,1)}, bf16[80,768]{1,0:T(8,128)(2,1)S(1)}, u32[]{:S(2)}, u32[]{:S(2)}) %collective-permute-start.21) | collective-permute-done | bytes 122912 | tf_op jit(solution)/shard_map/ppermute | solution.py:1051
  167.1 2.2 %merge.1 = (bf16[512,768]{1,0:T(8,128)(2,1)}, f32[1,16,192]{2,1,0:T(8,128)}) custom-call(bf16[416,768]{1,0:T(8,128)(2,1)} %get-tuple-element.197.packed, bf16[80,768]{1,0:T(8,128)(2,1)} %get-tuple-element.198.refs_0_, bf16[80,768]{1,0:T(8,128)(2,1)} %copy-done.22, bf16[80,768]{1,0:T(8,128)(2,1)} %copy-done.23, bf16[80,768]{1,0:T(8,128)(2,1)} %collective-permute-done.22.refs_3_), custom_call_target="tpu_custom_call" | custom-call | flops 2000000000 | bytes 200000 | tf_op jit(solution)/shard_map/merge/pallas_call | solution.py:1056
  170.8 5.3 %collective-permute-done.23 = bf16[1,512,192]{2,1,0:T(8,128)(2,1)S(1)} collective-permute-done((bf16[1,512,192]{2,1,0:T(8,128)(2,1)}, bf16[1,512,192]{2,1,0:T(8,128)(2,1)S(1)}, u32[]{:S(2)}, u32[]{:S(2)}) %collective-permute-start.23) | collective-permute-done | bytes 196640 | tf_op jit(solution)/shard_map/ppermute | solution.py:701
  176.1 5.7 %all-to-all-start.1 = ((bf16[8,64,768]{2,1,0:T(8,128)(2,1)}), bf16[8,64,768]{2,1,0:T(8,128)(2,1)S(1)}, u32[]{:S(2)}, u32[]{:S(2)}) async-start(bf16[8,64,768]{2,1,0:T(8,128)(2,1)} %bitcast.31), calls=%async_computation.1 | async-start | bytes 1572864 | tf_op jit(solution)/shard_map/all_to_all | solution.py:1066
  186.0 8.4 %all-to-all-done.1 = bf16[8,64,768]{2,1,0:T(8,128)(2,1)S(1)} async-done(((bf16[8,64,768]{2,1,0:T(8,128)(2,1)}), bf16[8,64,768]{2,1,0:T(8,128)(2,1)S(1)}, u32[]{:S(2)}, u32[]{:S(2)}) %all-to-all-start.1) | async-done | bytes 786464 | tf_op jit(solution)/shard_map/all_to_all | solution.py:1066
  194.5 10.5 %all_gather.6.late = bf16[512,768]{1,0:T(8,128)(2,1)} all-gather(bf16[64,768]{1,0:T(8,128)(2,1)S(1)} %reduce_sum.24), channel_id=1, replica_groups=mesh['seq'=8,'head'=4] {'seq'}, dimensions={0}, use_global_device_ids=true | all-gather | bytes 884736 | tf_op jit(solution)/shard_map/all_gather | solution.py:754
  207.7 4.2 %unpack.1 = (f32[192]{0:T(256)}, f32[768,2,384]{2,1,0:T(2,128)}, f32[2,32,768]{2,1,0:T(8,128)}, f32[6,768]{1,0:T(8,128)}, f32[4,384]{1,0:T(4,128)}, /*index=5*/f...) custom-call(bf16[512,768]{1,0:T(8,128)(2,1)} %all_gather.6.late, ...), custom_call_target="tpu_custom_call" | custom-call | flops 4000000000 | bytes 400000 | tf_op jit(solution)/shard_map/unpack/pallas_call | solution.py:1082
  (156 shorter events, 60.1 us)
Async XLA Ops:
  9.9 22.0 %collective-permute-start = (bf16[64,896]{1,0:T(8,128)(2,1)S(1)}, bf16[64,896]{1,0:T(8,128)(2,1)S(1)}, u32[]{:S(2)}, u32[]{:S(2)}) collective-permute-start(bf16[64,896]{1,0:T(8,128)(2,1)S(1)} %bitcast.32), channel_id=1, source_target_pairs={{0,1},{1,2},{2,3},{3,0},{4,5},{5,6},{6,7},{7,4},{8,9},{9,10},{10,1... | collective-permute-start | bytes 344072 | tf_op jit(solution)/shard_map/ppermute | solution.py:811
  12.9 18.9 %collective-permute-start.1 = (bf16[64,896]{1,0:T(8,128)(2,1)S(1)}, bf16[64,896]{1,0:T(8,128)(2,1)S(1)}, u32[]{:S(2)}, u32[]{:S(2)}) collective-permute-start(bf16[64,896]{1,0:T(8,128)(2,1)S(1)} %bitcast.33), channel_id=1, source_target_pairs={{0,2},{1,3},{2,0},{3,1},{4,6},{5,7},{6,4},{7,5},{8,10},{9,11},{10,... | collective-permute-start | bytes 344072 | tf_op jit(solution)/shard_map/ppermute | solution.py:811
  15.5 16.4 %collective-permute-start.2 = (bf16[64,896]{1,0:T(8,128)(2,1)S(1)}, bf16[64,896]{1,0:T(8,128)(2,1)S(1)}, u32[]{:S(2)}, u32[]{:S(2)}) collective-permute-start(bf16[64,896]{1,0:T(8,128)(2,1)S(1)} %bitcast.34), channel_id=1, source_target_pairs={{0,3},{1,0},{2,1},{3,2},{4,7},{5,4},{6,5},{7,6},{8,11},{9,8},{10,9... | collective-permute-start | bytes 344072 | tf_op jit(solution)/shard_map/ppermute | solution.py:811
  18.4 13.4 %collective-permute-start.3 = (bf16[1,16,896]{2,1,0:T(8,128)(2,1)S(1)}, bf16[1,16,896]{2,1,0:T(8,128)(2,1)S(1)}, u32[]{:S(2)}, u32[]{:S(2)}) collective-permute-start(bf16[1,16,896]{2,1,0:T(8,128)(2,1)S(1)} %pad_maximum_fusion.2), channel_id=1, source_target_pairs={{0,4},{4,8},{8,12},{12,16},{16,20},{20,24},{24,28},{1,5},{5,9},{9,... | collective-permute-start | bytes 86024 | tf_op jit(solution)/shard_map/ppermute | solution.py:697
  49.5 11.0 %collective-permute-start.5 = (f32[1,136,384]{2,1,0:T(8,128)S(1)}, f32[1,136,384]{2,1,0:T(8,128)S(1)}, u32[]{:S(2)}, u32[]{:S(2)}) collective-permute-start(f32[1,136,384]{2,1,0:T(8,128)S(1)} %pad_maximum_fusion), channel_id=1, source_target_pairs={{0,8},{4,12},{8,16},{12,20},{16,24},{20,28},{1,9},{5,13},{9,17},{1... | collective-permute-start | bytes 626696 | tf_op jit(solution)/shard_map/ppermute | solution.py:697
  52.9 10.3 %collective-permute-start.6 = (f32[1,136,384]{2,1,0:T(8,128)S(1)}, f32[1,136,384]{2,1,0:T(8,128)S(1)}, u32[]{:S(2)}, u32[]{:S(2)}) collective-permute-start(f32[1,136,384]{2,1,0:T(8,128)S(1)} %pad_maximum_fusion), channel_id=1, source_target_pairs={{0,16},{4,20},{8,24},{12,28},{1,17},{5,21},{9,25},{13,29},{2,18},{... | collective-permute-start | bytes 626696 | tf_op jit(solution)/shard_map/ppermute | solution.py:697
  90.9 16.1 %collective-permute-start.12 = (f32[1,136,384]{2,1,0:T(8,128)S(1)}, f32[1,136,384]{2,1,0:T(8,128)S(1)}, u32[]{:S(2)}, u32[]{:S(2)}) collective-permute-start(f32[1,136,384]{2,1,0:T(8,128)S(1)} %pad_maximum_fusion.1), channel_id=1, source_target_pairs={{8,0},{12,4},{16,8},{20,12},{24,16},{28,20},{9,1},{13,5},{17,9},{2... | collective-permute-start | bytes 626696 | tf_op jit(solution)/shard_map/ppermute | solution.py:697
  92.2 16.8 %collective-permute-start.13 = (f32[1,136,384]{2,1,0:T(8,128)S(1)}, f32[1,136,384]{2,1,0:T(8,128)S(1)}, u32[]{:S(2)}, u32[]{:S(2)}) collective-permute-start(f32[1,136,384]{2,1,0:T(8,128)S(1)} %pad_maximum_fusion.1), channel_id=1, source_target_pairs={{16,0},{20,4},{24,8},{28,12},{17,1},{21,5},{25,9},{29,13},{18,2},{... | collective-permute-start | bytes 626696 | tf_op jit(solution)/shard_map/ppermute | solution.py:697
  93.5 15.5 %collective-permute-start.14 = (f32[1,136,384]{2,1,0:T(8,128)S(1)}, f32[1,136,384]{2,1,0:T(8,128)S(1)}, u32[]{:S(2)}, u32[]{:S(2)}) collective-permute-start(f32[1,136,384]{2,1,0:T(8,128)S(1)} %pad_maximum_fusion.1), channel_id=1, source_target_pairs={{24,0},{28,4},{25,1},{29,5},{26,2},{30,6},{27,3},{31,7}} | collective-permute-start | bytes 626696 | tf_op jit(solution)/shard_map/ppermute | solution.py:697
  103.7 47.8 %collective-permute-start.15 = (bf16[1,1024,192]{2,1,0:T(8,128)(2,1)}, bf16[1,1024,192]{2,1,0:T(8,128)(2,1)S(1)}, u32[]{:S(2)}, u32[]{:S(2)}) collective-permute-start(bf16[1,1024,192]{2,1,0:T(8,128)(2,1)} %get-tuple-element.188), channel_id=1, source_target_pairs={{0,1},{1,0},{2,3},{3,2},{4,5},{5,4},{6,7},{7,6},{8,9},{9,8},{10,11... | collective-permute-start | bytes 1179656 | tf_op jit(solution)/shard_map/ppermute | solution.py:701
  104.2 47.4 %collective-permute-start.16 = (bf16[1,1024,192]{2,1,0:T(8,128)(2,1)}, bf16[1,1024,192]{2,1,0:T(8,128)(2,1)}, u32[]{:S(2)}, u32[]{:S(2)}) collective-permute-start(bf16[1,1024,192]{2,1,0:T(8,128)(2,1)} %get-tuple-element.189), channel_id=1, source_target_pairs={{0,2},{1,3},{2,0},{3,1},{4,6},{5,7},{6,4},{7,5},{8,10},{9,11},{10,... | collective-permute-start | bytes 1179656 | tf_op jit(solution)/shard_map/ppermute | solution.py:701
  107.1 44.6 %collective-permute-start.17 = (bf16[1,1024,192]{2,1,0:T(8,128)(2,1)}, bf16[1,1024,192]{2,1,0:T(8,128)(2,1)}, u32[]{:S(2)}, u32[]{:S(2)}) collective-permute-start(bf16[1,1024,192]{2,1,0:T(8,128)(2,1)} %get-tuple-element.190), channel_id=1, source_target_pairs={{0,3},{1,2},{2,1},{3,0},{4,7},{5,6},{6,5},{7,4},{8,11},{9,10},{10,... | collective-permute-start | bytes 1179656 | tf_op jit(solution)/shard_map/ppermute | solution.py:701
  109.8 22.8 %all-to-all-start = ((bf16[8,96,768]{2,1,0:T(8,128)(2,1)}), bf16[8,96,768]{2,1,0:T(8,128)(2,1)S(1)}, u32[]{:S(2)}, u32[]{:S(2)}) async-start(bf16[8,96,768]{2,1,0:T(8,128)(2,1)} %bitcast.30), calls=%async_computation | async-start | bytes 2359296 | tf_op jit(solution)/shard_map/all_to_all | solution.py:952
  115.8 91.9 %all-gather.2.cloned.1.call-start = ((), (), s32[]{:S(2)}) async-start(), calls=%async_computation.2 | async-start | bytes 1327104 | tf_op jit(solution)/shard_map/all_gather | solution.py:754
  132.6 19.0 %collective-permute-start.18 = (bf16[1,512,192]{2,1,0:T(8,128)(2,1)}, bf16[1,512,192]{2,1,0:T(8,128)(2,1)}, u32[]{:S(2)}, u32[]{:S(2)}) collective-permute-start(bf16[1,512,192]{2,1,0:T(8,128)(2,1)} %get-tuple-element.191), channel_id=1, source_target_pairs={{0,1},{1,0},{2,3},{3,2},{4,5},{5,4},{6,7},{7,6},{8,9},{9,8},{10,11... | collective-permute-start | bytes 589832 | tf_op jit(solution)/shard_map/ppermute | solution.py:701
  132.6 20.3 %collective-permute-start.19 = (bf16[1,512,192]{2,1,0:T(8,128)(2,1)}, bf16[1,512,192]{2,1,0:T(8,128)(2,1)S(1)}, u32[]{:S(2)}, u32[]{:S(2)}) collective-permute-start(bf16[1,512,192]{2,1,0:T(8,128)(2,1)} %get-tuple-element.192), channel_id=1, source_target_pairs={{0,1},{1,0},{2,3},{3,2},{4,5},{5,4},{6,7},{7,6},{8,9},{9,8},{10,11... | collective-permute-start | bytes 589832 | tf_op jit(solution)/shard_map/ppermute | solution.py:701
  154.7 11.7 %collective-permute-start.21 = (bf16[80,768]{1,0:T(8,128)(2,1)}, bf16[80,768]{1,0:T(8,128)(2,1)S(1)}, u32[]{:S(2)}, u32[]{:S(2)}) collective-permute-start(bf16[80,768]{1,0:T(8,128)(2,1)} %get-tuple-element.200), channel_id=1, source_target_pairs={{0,2},{1,3},{2,0},{3,1},{4,6},{5,7},{6,4},{7,5},{8,10},{9,11},{10,... | collective-permute-start | bytes 368648 | tf_op jit(solution)/shard_map/ppermute | solution.py:1051
  155.0 11.5 %collective-permute-start.22 = (bf16[80,768]{1,0:T(8,128)(2,1)}, bf16[80,768]{1,0:T(8,128)(2,1)}, u32[]{:S(2)}, u32[]{:S(2)}) collective-permute-start(bf16[80,768]{1,0:T(8,128)(2,1)} %get-tuple-element.201), channel_id=1, source_target_pairs={{0,1},{1,2},{2,3},{3,0},{4,5},{5,6},{6,7},{7,4},{8,9},{9,10},{10,1... | collective-permute-start | bytes 368648 | tf_op jit(solution)/shard_map/ppermute | solution.py:1051
  155.9 20.2 %collective-permute-start.23 = (bf16[1,512,192]{2,1,0:T(8,128)(2,1)}, bf16[1,512,192]{2,1,0:T(8,128)(2,1)S(1)}, u32[]{:S(2)}, u32[]{:S(2)}) collective-permute-start(bf16[1,512,192]{2,1,0:T(8,128)(2,1)} %get-tuple-element.203), channel_id=1, source_target_pairs={{0,1},{1,0},{2,3},{3,2},{4,5},{5,4},{6,7},{7,6},{8,9},{9,8},{10,11... | collective-permute-start | bytes 589832 | tf_op jit(solution)/shard_map/ppermute | solution.py:701
  158.2 27.8 %collective-permute-start.24 = (bf16[1,512,192]{2,1,0:T(8,128)(2,1)}, bf16[1,512,192]{2,1,0:T(8,128)(2,1)S(1)}, u32[]{:S(2)}, u32[]{:S(2)}) collective-permute-start(bf16[1,512,192]{2,1,0:T(8,128)(2,1)} %get-tuple-element.206), channel_id=1, source_target_pairs={{0,1},{1,0},{2,3},{3,2},{4,5},{5,4},{6,7},{7,6},{8,9},{9,8},{10,11... | collective-permute-start | bytes 589832 | tf_op jit(solution)/shard_map/ppermute | solution.py:701
  160.0 24.9 %collective-permute-start.26 = (bf16[1,512,192]{2,1,0:T(8,128)(2,1)}, bf16[1,512,192]{2,1,0:T(8,128)(2,1)}, u32[]{:S(2)}, u32[]{:S(2)}) collective-permute-start(bf16[1,512,192]{2,1,0:T(8,128)(2,1)} %add_convert_fusion.1), channel_id=1, source_target_pairs={{0,2},{1,3},{2,0},{3,1},{4,6},{5,7},{6,4},{7,5},{8,10},{9,11},{10,... | collective-permute-start | bytes 589832 | tf_op jit(solution)/shard_map/ppermute | solution.py:701
  169.4 15.4 %collective-permute-start.27 = (f32[1,16,192]{2,1,0:T(8,128)}, f32[1,16,192]{2,1,0:T(8,128)S(1)}, u32[]{:S(2)}, u32[]{:S(2)}) collective-permute-start(f32[1,16,192]{2,1,0:T(8,128)} %get-tuple-element.215), channel_id=1, source_target_pairs={{4,0},{8,4},{12,8},{16,12},{20,16},{24,20},{28,24},{5,1},{9,5},{13... | collective-permute-start | bytes 36872 | tf_op jit(solution)/shard_map/ppermute | solution.py:697
  176.1 18.3 %all-to-all-start.1 = ((bf16[8,64,768]{2,1,0:T(8,128)(2,1)}), bf16[8,64,768]{2,1,0:T(8,128)(2,1)S(1)}, u32[]{:S(2)}, u32[]{:S(2)}) async-start(bf16[8,64,768]{2,1,0:T(8,128)(2,1)} %bitcast.31), calls=%async_computation.1 | async-start | bytes 1572864 | tf_op jit(solution)/shard_map/all_to_all | solution.py:1066
  184.8 20.2 %collective-permute-start.25 = (bf16[1,512,192]{2,1,0:T(8,128)(2,1)S(1)}, bf16[1,512,192]{2,1,0:T(8,128)(2,1)S(1)}, u32[]{:S(2)}, u32[]{:S(2)}) collective-permute-start(bf16[1,512,192]{2,1,0:T(8,128)(2,1)S(1)} %add_convert_fusion.2), channel_id=1, source_target_pairs={{0,2},{1,3},{2,0},{3,1},{4,6},{5,7},{6,4},{7,5},{8,10},{9,11},{10,... | collective-permute-start | bytes 589832 | tf_op jit(solution)/shard_map/ppermute | solution.py:701
  (38 other events, 270.0 us)
Sparse Core Ops, SparseCore 0:
  135.6 22.6 all-gather.1

commit v4 on v3

--- a/solution.py
+++ b/solution.py
@@ -116,6 +116,53 @@
         yield start, width, [start // WIDTH + i for i in range(width // WIDTH)]
 
 
+def pair_kernel(later, own, other, pair, near):
+    flag = later[0] == 1
+    mine, theirs = own[...], other[...]
+    first, second = jnp.where(flag, theirs, mine), jnp.where(flag, mine, theirs)
+    fade = second[:, LANES : LANES + 1]
+    pair[:, :LANES] = fade * first[:, :LANES] + second[:, :LANES]
+    pair[:, LANES:] = first[:, LANES:] * second[:, LANES:]
+    neutral = (iota(mine.shape, 1) >= LANES).astype(F32)
+    near[...] = jnp.where(flag, theirs, neutral)
+
+
+def prepare_kernel(
+    tok, starts, state, conv, conv_bias, step, step_bias, decay, skip, conv_x, conv_x_bias,
+    gain_in, gain_out, tail, message, norm_in, norm_out, hp, ci, wst, marked, turn,
+):
+    rows, length = starts.shape
+    width = tok.shape[-1]
+    own = state.shape[1]
+    heads = step.shape[0]
+    tail[:, :, :width] = tok[...]
+    for line in range(rows):
+        for group in range(length // GROUP):
+            part = starts[line : line + 1, group * GROUP : (group + 1) * GROUP].astype(F32)
+            marked[line, group] = jnp.broadcast_to(part, (8, GROUP))
+        last = starts[line : line + 1, length - LANES :].astype(F32)
+        column = jnp.broadcast_to(last, (LANES, LANES)).T
+        tail[line, :, width:] = rounded(column[LANES - EDGE :])
+    message[:, width:] = jnp.zeros((2 * own, LANES), BF16)
+    taps = conv[...].astype(F32)
+    for kind in range(2):
+        message[kind * own : (kind + 1) * own, :width] = state[kind]
+        turn[...] = jnp.zeros_like(turn)
+        turn[:K, :own] = taps[:, kind, :]
+        turn[K : K + 1, :own] = conv_bias[kind : kind + 1, :].astype(F32)
+        message[kind * own : (kind + 1) * own, width:] = rounded(turn[...].T[:own])
+    norm_in[...] = gain_in[...].reshape(1, -1)
+    norm_out[...] = gain_out[...].reshape(1, -1)
+    hp[...] = jnp.zeros_like(hp)
+    for line, vector in enumerate((step_bias, decay, skip)):
+        hp[line : line + 1, :heads] = vector[...].reshape(1, -1)
+    ci[...] = jnp.zeros_like(ci)
+    ci[:K, :] = conv_x[...].astype(F32)
+    ci[K : K + 1, :] = conv_x_bias[...].astype(F32).reshape(1, -1)
+    wst[...] = jnp.zeros_like(wst)
+    wst[:heads, :] = step[...]
+
+
 def project_kernel(tok, gain, win, wst, hp, normed, xpre, gate, spre, step, cum):
     channels = xpre.shape[-1]
     tokens = tok[...].astype(F32)
@@ -124,7 +171,7 @@
     product = dot(row, win[...])
     xpre[...] = rounded(product[:, :channels])
     gate[...] = product[:, channels:]
-    raw = dot(row, wst[...]) + hp[0:1, :]
+    raw = dot_nt(row, wst[...]) + hp[0:1, :]
     sizes = jax.nn.softplus(raw)
     spre[...] = raw
     step[...] = sizes
@@ -339,15 +386,17 @@
         ref[...] = block
 
 
-def out_kernel(parts, me, normed_out, cot, dgate, normed, wout, win, back, grads, *rest):
-    channels = wout.shape[0]
-    branch, total = rest[:parts], rest[parts]
+def branch_kernel(me, normed_out, wout, *branch):
+    store_parts(branch, dot(normed_out[...], wout[...]), me[0])
+
+
+def out_kernel(normed_out, cot, dgate, normed, grads, total):
+    channels = normed_out.shape[1]
 
     @pl.when((pl.program_id(1) == 0) & (pl.program_id(0) == 0))
     def _():
         total[...] = jnp.zeros_like(total)
 
-    store_parts(branch, dot(normed_out[...], wout[...]), me[0])
     total[:channels, :] += dot_tn(normed_out[...], cot[...])
     total[channels : 2 * channels, :] += dot_tn(dgate[...], normed[...])
 
@@ -357,8 +406,6 @@
     )
     def _():
         grads[...] = rounded(total[...])
-
-    back[...] = dot_nt(dgate[...], win[:, channels:])
 
 
 def token_grad(tokens, gain, down):
@@ -535,8 +582,8 @@
     grad_x[...] += dot_tn(main_x, row)
     grad_s[...] += dot_tn(main_s, row)
     grad_normed = (
-        back[...] + dot_nt(main_x, win[:, :channels]) + dot(main_s, ws[...])
-        + dot_nt(grad_raw, wst[...])
+        dot_nt(jnp.concatenate([main_x, back[...]], axis=1), win[...]) + dot(main_s, ws[...])
+        + dot(grad_raw, wst[...])
     )
     grad, gain_part = token_grad(tok[...].astype(F32), gain[...], grad_normed)
     grad_misc[0:8, :] += dot_tn(grad_raw, row)[:8]
@@ -736,14 +783,15 @@
     core = lax.axis_index("seq") % 2
     later = core == (0 if reverse else 1)
     other = crossed(message, "seq", 1)
-    fade, other_fade = message[:, LANES:], other[:, LANES:]
-    state, other_state = message[:, :LANES], other[:, :LANES]
-    pair = jnp.where(
-        later, fade[:, :1] * other_state + state, other_fade[:, :1] * state + other_state
-    )
-    pair = jnp.concatenate([pair, fade * other_fade], axis=1)
-    neutral = (lax.broadcasted_iota(jnp.int32, message.shape, 1) >= LANES).astype(F32)
-    near = jnp.where(later, other, neutral)
+    pair, near = pl.pallas_call(
+        pair_kernel,
+        in_specs=[pl.BlockSpec(memory_space=pltpu.SMEM)]
+        + [pl.BlockSpec(memory_space=pltpu.VMEM)] * 2,
+        out_shape=[jax.ShapeDtypeStruct(message.shape, F32)] * 2,
+        compiler_params=pltpu.CompilerParams(vmem_limit_bytes=62 * 2**20),
+        cost_estimate=cost(1),
+        name="pair",
+    )(later.astype(jnp.int32).reshape(1), message, other)
     sign = -2 if reverse else 2
     pair, beside = ordered(pair, beside)
     return beside, [near] + [shifted(pair, "seq", sign * d) for d in range(1, count // 2)]
@@ -792,38 +840,33 @@
 
     scalar = pl.BlockSpec(memory_space=pltpu.SMEM)
     halo_width = width + LANES
-    tail = jnp.concatenate(
-        [
-            tokens[:, length - EDGE :],
-            jnp.broadcast_to(starts[:, length - EDGE :, None], (rows, EDGE, LANES)).astype(BF16),
-        ],
-        axis=2,
+    tail, state_own, gain_in, gain_out, hp, ci, wst, marked = pl.pallas_call(
+        prepare_kernel,
+        grid=(1,),
+        in_specs=[
+            pl.BlockSpec((rows, EDGE, width), lambda i: (0, length // EDGE - 1, 0)),
+        ] + [pl.BlockSpec(memory_space=pltpu.VMEM)] * 12,
+        out_specs=[pl.BlockSpec(memory_space=pltpu.VMEM)] * 8,
+        out_shape=[
+            sds((rows, EDGE, halo_width), BF16), sds((2 * own_state, halo_width), BF16),
+            sds((1, width)), sds((1, channels)), sds((8, LANES)), sds((8, channels)),
+            sds((LANES, width), BF16), sds((rows, groups, 8, GROUP)),
+        ],
+        scratch_shapes=[pltpu.VMEM((LANES, LANES), F32)],
+        compiler_params=pltpu.CompilerParams(vmem_limit_bytes=62 * 2**20),
+        cost_estimate=cost(2),
+        name="prepare",
+    )(
+        tokens, starts, state_weight.transpose(1, 2, 0), conv_state, conv_state_bias,
+        step_weight.T, step_bias, decay_log, skip_gain, conv_inner, conv_inner_bias,
+        norm_in_gain, norm_out_gain,
     )
     halo = shifted(tail, "seq", 1)
-    state_own = jnp.concatenate(
-        [
-            state_weight, conv_state, conv_state_bias[None],
-            jnp.zeros((LANES - K - 1, 2, own_state), BF16),
-        ],
-        axis=0,
-    ).transpose(1, 2, 0).reshape(2 * own_state, width + LANES)
     found = [state_own] + [
         lax.ppermute(state_own, "head", ring("head", d)) for d in range(1, head_devices)
     ]
 
-    gain_in = norm_in_gain[None]
-    gain_out = norm_out_gain[None]
     win = inner_weight.reshape(width, 2 * channels)
-    wst = jnp.pad(step_weight, ((0, 0), (0, LANES - head_count)))
-    hp = jnp.pad(
-        jnp.stack([step_bias, decay_log, skip_gain]), ((0, 5), (0, LANES - head_count))
-    )
-    ci = jnp.pad(
-        jnp.concatenate([conv_inner, conv_inner_bias[None]], axis=0).astype(F32), ((0, 3), (0, 0))
-    )
-    marked = jnp.broadcast_to(
-        starts.astype(F32).reshape(rows, groups, 1, GROUP), (rows, groups, 8, GROUP)
-    )
 
     def act(cols, dtype=F32):
         return sds((rows, length, cols), dtype)
@@ -833,7 +876,7 @@
         grid=grid,
         in_specs=[
             block(width), whole((1, width)), whole((width, 2 * channels)),
-            whole((width, LANES)), whole((8, LANES)),
+            whole((LANES, width)), whole((8, LANES)),
         ],
         out_specs=[
             block(width), block(channels), block(channels), block(LANES), block(LANES),
@@ -928,29 +971,34 @@
         cost_estimate=cost(6),
     )(*sums_all, mixer, gate, dn, xact, bc, cum, marked, gain_out, hp, fades)
 
+    branch = pl.pallas_call(
+        branch_kernel,
+        grid=grid,
+        in_specs=[scalar, block(channels), whole((channels, width))],
+        out_specs=[block(own_width)] * head_devices,
+        out_shape=[act(own_width, BF16)] * head_devices,
+        compiler_params=PARAMS,
+        cost_estimate=cost(3),
+        name="branch",
+    )(me, normed_out, out_weight)
+    branch_near = send_all(branch, "head")
     normed_out, returned = chained(back_message, True, normed_out)
-    back, early, *branch = pl.pallas_call(
-        functools.partial(out_kernel, head_devices),
+    early = pl.pallas_call(
+        out_kernel,
         grid=grid,
-        in_specs=[
-            scalar, block(channels), block(width), block(channels), block(width),
-            whole((channels, width)), whole((width, 2 * channels)),
-        ],
-        out_specs=[block(width), whole((2 * channels, width))]
-        + [block(own_width)] * head_devices,
-        out_shape=[act(width), sds((2 * channels, width), BF16)]
-        + [act(own_width, BF16)] * head_devices,
+        in_specs=[block(channels), block(width), block(channels), block(width)],
+        out_specs=whole((2 * channels, width)),
+        out_shape=sds((2 * channels, width), BF16),
         scratch_shapes=[pltpu.VMEM((2 * channels, width), F32)],
         compiler_params=PARAMS,
+        cost_estimate=cost(5),
         name="out",
-        cost_estimate=cost(8),
-    )(me, normed_out, cotangent, dgate, normed, out_weight, win)
+    )(normed_out, cotangent, dgate, normed)
 
     column = lax.axis_index("head") * own_width
     own_tokens = lax.dynamic_slice_in_dim(tokens, column, own_width, 2).astype(F32)
-    early, returned = ordered(early, returned)
+
     early = lax.all_to_all(early.reshape(seq_count, -1, width), "seq", 0, 0, tiled=True)
-    branch_near = send_all(branch, "head")
 
     late_rows = channels + 3 * EDGE + 2 * own_state + EDGE
     chunk = -(-late_rows // (seq_count * EDGE)) * EDGE
@@ -1005,10 +1053,10 @@
                 scalar, tile(width), per_row(EDGE, halo_width), group_tile(8, GROUP), tile(width),
                 tile(channels), before(channels), per_row(EDGE, channels), tile(states),
                 before(states), per_row(EDGE, states), tile(channels), tile(states),
-                tile(channels), tile(channels), tile(width), tile(LANES), tile(LANES),
+                tile(channels), tile(channels), tile(channels), tile(LANES), tile(LANES),
                 tile(LANES), tile(LANES), group_tile(LANES, channels),
                 group_tile(LANES, channels), group_tile(8, channels),
-                whole((width, 2 * channels)), whole((states, width)), whole((width, LANES)),
+                whole((width, 2 * channels)), whole((states, width)), whole((LANES, width)),
                 whole((8, LANES)), whole((8, channels)), whole((8, states)), whole((1, width)),
                 whole((1, channels)), whole((1, channels)),
             ],
@@ -1029,7 +1077,7 @@
             cost_estimate=cost(15),
         )(
             *lead, *carried, me, tokens, halo, marked, normed, xpre, xpre, halo_x, spre, spre,
-            halo_s, xact, bc, yin, dy, back, step, cum, raw, run_all, entry_states, entering,
+            halo_s, xact, bc, yin, dy, dgate, step, cum, raw, run_all, entry_states, entering,
             fades, win, ws, wst, hp, ci, cs, gain_in, grad_gain_out, grad_skip,
         )
 

time: 220 us -> 209 us (0.950)
  other arithmetic: 15.1 us -> 7.19 us
  local copies, waits for them, and re-layouts: 15.3 us -> 7.41 us
  Pallas kernels: 78.8 us -> 86 us
  waiting for transfers between devices: 30.6 us -> 28 us
    pallas_call x1 -> x5, Pallas kernels: 8.92 us -> 16.1 us  [the longest x1 5.48 us: on_device(): pl.pallas_call(out_kernel, grid=grid, in_specs=[block(channels), block(wi...]
    select_n x4 -> x0, other arithmetic: 3.48 us -> none  [the longest x2 1.93 us: chained(): jnp.where(later, fade[:, :1] * other_state + state, other_fade[:, :1] * s...]
    broadcast_in_dim x8 -> x0, local copies, waits for them, and re-layouts: 2.61 us -> none  [the longest x1 0.76 us: on_device(): conv_state_bias[None]]
    unnamed x67 -> x45, local copies, waits for them, and re-layouts: 9.67 us -> 7.41 us
    slice x5 -> x0, local copies, waits for them, and re-layouts: 2.23 us -> none  [the longest x2 1.45 us: chained(): fade[:, :1] * other_state + state]
  transfers between devices with their start and end apart: 31 -> 31, of which waited for: 11 -> 8; matrix products, arithmetic and copies ran while one was open for 10% -> 7% of each run, Pallas kernels for 22% -> 25%
where the time goes in v4:
time: 209 us; the launch traced here: 208 us
  Pallas kernels  86 us (41%)
  starting transfers between devices  51.1 us (24%)
  waiting for transfers between devices  28 us (13%)
  between operations  14.4 us (7%)
  blocking collectives  10.5 us (5%)
  local copies, waits for them, and re-layouts  7.41 us (4%)
  other arithmetic  7.19 us (3%)
  matrix products  3.24 us (2%)
    pallas_call x2, Pallas kernels, backward_call(): pl.pallas_call(functools.partial(backward_kernel, start_call, end_call, l...  31.5 us
    ppermute x8, starting transfers between devices, shifted(): lax.ppermute(block, axis, [(i - distance, i) for i in devices if i - dist...  14.1 us
    ppermute x11, starting transfers between devices, crossed(): lax.ppermute(block, axis, [(i, i ^ mask) for i in range(lax.axis_size(axi...  13.5 us
    pallas_call x1, Pallas kernels, on_device(): pl.pallas_call(functools.partial(forward_kernel, len(found)), grid=grid,...  11 us
    all_gather x1, blocking collectives, gather_sum(): return lax.all_gather(total, 'seq', axis=0, tiled=True)  10.5 us
    all_to_all x1, waiting for transfers between devices, on_device(): lax.all_to_all(late.reshape(seq_count, chunk, -1), 'seq', 0, 0, tiled=True)  8.38 us
    pallas_call x1, Pallas kernels, on_device(): pl.pallas_call(functools.partial(gate_kernel, len(sums_all)), grid=grid,...  7.44 us
    unnamed x45, local copies, waits for them, and re-layouts  7.41 us
  transfers between devices with their start and end apart: 31, of which 8 were waited for; matrix products, arithmetic and copies ran while one was open for 7% of the time, Pallas kernels for 25%

profile of v4, /device:TPU:0, one launch (start us, length us, event | category | flops | bytes accessed | tf_op | source)
XLA Modules:
  0.0 207.8 jit_solution(17583615644735511920)
XLA Ops:
  9.1 3.1 %collective-permute-start = (bf16[64,896]{1,0:T(8,128)(2,1)}, bf16[64,896]{1,0:T(8,128)(2,1)S(1)}, u32[]{:S(2)}, u32[]{:S(2)}) collective-permute-start(bf16[64,896]{1,0:T(8,128)(2,1)} %get-tuple-element.128.refs_0_), channel_id=1, source_target_pairs={{0,1},{1,2},{2,3},{3,0},{4,5},{5,6},{6,7},{7,4},{8,9},{9,10},{10,1... | collective-permute-start | bytes 344072 | tf_op jit(solution)/shard_map/ppermute | solution.py:866
  12.2 2.6 %collective-permute-start.1 = (bf16[64,896]{1,0:T(8,128)(2,1)}, bf16[64,896]{1,0:T(8,128)(2,1)S(1)}, u32[]{:S(2)}, u32[]{:S(2)}) collective-permute-start(bf16[64,896]{1,0:T(8,128)(2,1)} %get-tuple-element.128.refs_0_), channel_id=1, source_target_pairs={{0,2},{1,3},{2,0},{3,1},{4,6},{5,7},{6,4},{7,5},{8,10},{9,11},{10,... | collective-permute-start | bytes 344072 | tf_op jit(solution)/shard_map/ppermute | solution.py:866
  18.7 6.2 %project.1 = (bf16[1,1024,768]{2,1,0:T(8,128)(2,1)}, bf16[1,1024,384]{2,1,0:T(8,128)(2,1)}, f32[1,1024,384]{2,1,0:T(8,128)}, f32[1,1024,128]{2,1,0:T(8,128)}, f3...) custom-call(bf16[1,1024,768]{2,1,0:T(8,128)(2,1)} %refs_7_.1, ...), custom_call_target="tpu_custom_call" | custom-call | flops 6000000000 | bytes 600000 | tf_op jit(solution)/shard_map/project/pallas_call | solution.py:874
  25.6 11.0 %forward.1 = (f32[1,1024,384]{2,1,0:T(8,128)}, bf16[1,1024,384]{2,1,0:T(8,128)(2,1)}, bf16[1,1024,256]{2,1,0:T(8,128)(2,1)}, bf16[1,1024,256]{2,1,0:T(8,128)(2,1...) custom-call(bf16[64,896]{1,0:T(8,128)(2,1)} %get-tuple-element.128.r, ...), custom_call_target="tpu_custom_call" | custom-call | flops 10000000000 | bytes 1000000 | tf_op jit(solution)/shard_map/forward/pallas_call | solution.py:895
  36.6 2.3 %collective-permute-start.4 = (f32[1,136,384]{2,1,0:T(8,128)}, f32[1,136,384]{2,1,0:T(8,128)S(1)}, u32[]{:S(2)}, u32[]{:S(2)}) collective-permute-start(f32[1,136,384]{2,1,0:T(8,128)} %get-tuple-element.139.own), channel_id=1, source_target_pairs={{0,4},{4,0},{8,12},{12,8},{16,20},{20,16},{24,28},{28,24},{1,5},{5... | collective-permute-start | bytes 626696 | tf_op jit(solution)/shard_map/ppermute | solution.py:748
  42.8 3.4 %collective-permute-start.5 = (f32[1,136,384]{2,1,0:T(8,128)}, f32[1,136,384]{2,1,0:T(8,128)S(1)}, u32[]{:S(2)}, u32[]{:S(2)}) collective-permute-start(f32[1,136,384]{2,1,0:T(8,128)} %get-tuple-element.142), channel_id=1, source_target_pairs={{0,8},{4,12},{8,16},{12,20},{16,24},{20,28},{1,9},{5,13},{9,17},{1... | collective-permute-start | bytes 626696 | tf_op jit(solution)/shard_map/ppermute | solution.py:744
  50.4 3.2 %fusion.2.refs_8_.refs_6_ = f32[1,1024,384]{2,1,0:T(8,128)} fusion(bf16[384,768]{1,0:T(8,128)(2,1)} %wout.1, bf16[1,1024,768]{2,1,0:T(8,128)(2,1)S(1)} %copy-done), kind=kOutput, calls=%fused_computation.2 | convolution fusion | flops 603979776 | bytes 3735552 | tf_op jit(solution)/shard_map/rsd,cd->rsc/dot_general | solution.py:927
  53.6 3.2 %collective-permute-done.6.refs_2_ = f32[1,136,384]{2,1,0:T(8,128)S(1)} collective-permute-done((f32[1,136,384]{2,1,0:T(8,128)}, f32[1,136,384]{2,1,0:T(8,128)S(1)}, u32[]{:S(2)}, u32[]{:S(2)}) %collective-permute-start.6) | collective-permute-done | bytes 208928 | tf_op jit(solution)/shard_map/ppermute | solution.py:744
  57.5 7.3 %mix.1 = (f32[1,1024,384]{2,1,0:T(8,128)}, f32[1,4,8,256]{3,2,1,0:T(8,128)}, f32[1,4,128,384]{3,2,1,0:T(8,128)}) custom-call(f32[1,136,384]{2,1,0:T(8,128)} %get-tuple-element.140.refs_0_, f32[1,136,384]{2,1,0:T(8,128)} %copy-done.9, f32[1,136,384]{2,1,0:T(8,128)} %copy-done.10, f32[1,136,384]{2,1,0:T(8,128)} %collective-permute-done.7.refs_3_, ...), custom_call_target="tpu_custom_call" | custom-call | flops 6000000000 | bytes 600000 | tf_op jit(solution)/shard_map/mix/pallas_call | solution.py:928
  69.0 2.2 %collective-permute-done.8.refs_1_ = f32[1,4,8,256]{3,2,1,0:T(8,128)S(1)} collective-permute-done((f32[1,4,8,256]{3,2,1,0:T(8,128)}, f32[1,4,8,256]{3,2,1,0:T(8,128)S(1)}, u32[]{:S(2)}, u32[]{:S(2)}) %collective-permute-start.8) | collective-permute-done | bytes 32800 | tf_op jit(solution)/shard_map/ppermute | solution.py:947
  72.9 7.4 %gate.1 = (f32[1,1024,384]{2,1,0:T(8,128)}, bf16[1,1024,384]{2,1,0:T(8,128)(2,1)}, bf16[1,1024,384]{2,1,0:T(8,128)(2,1)}, f32[1,4,128,384]{3,2,1,0:T(8,128)}, f3...) custom-call(f32[1,4,8,256]{3,2,1,0:T(8,128)} %get-tuple-element.151.refs_0_, ...), custom_call_target="tpu_custom_call" | custom-call | flops 6000000000 | bytes 600000 | tf_op jit(solution)/shard_map/gate/pallas_call | solution.py:949
  80.4 4.9 %branch.1 = (bf16[1,1024,192]{2,1,0:T(8,128)(2,1)}, bf16[1,1024,192]{2,1,0:T(8,128)(2,1)}, bf16[1,1024,192]{2,1,0:T(8,128)(2,1)}, bf16[1,1024,192]{2,1,0:T(8,128)(2,1)}) custom-call(s32[1]{0:T(128)} %bitcast.me.refs_4_.refs_6_, bf16[1,1024,384]{2,1,0:T(8,128)(2,1)} %get-tuple-element.182.normed_out, bf16[384,768]{1,0:T(8,128)(2,1)} %wout.1), custom_call_target="tpu_custom_call" | custom-call | flops 3000000000 | bytes 300000 | tf_op jit(solution)/shard_map/branch/pallas_call | solution.py:974
  94.2 5.5 %out.1 = bf16[768,768]{1,0:T(8,128)(2,1)} custom-call(bf16[1,1024,384]{2,1,0:T(8,128)(2,1)} %get-tuple-element.182.normed_out, bf16[1,1024,768]{2,1,0:T(8,128)(2,1)} %cot.1, bf16[1,1024,384]{2,1,0:T(8,128)(2,1)} %get-tuple-element.163.refs_19_.dgate.refs_21_, bf16[1,1024,768]{2,1,0:T(8,128)(2,1)} %get-tuple-element.133.refs_5_.refs_8_.normed.refs_10_), custom_call_target="tpu_custom_call" | custom-call | flops 5000000000 | bytes 500000 | tf_op jit(solution)/shard_map/out/pallas_call | solution.py:986
  99.7 7.3 %all-to-all-start = ((bf16[8,96,768]{2,1,0:T(8,128)(2,1)}), bf16[8,96,768]{2,1,0:T(8,128)(2,1)S(1)}, u32[]{:S(2)}, u32[]{:S(2)}) async-start(bf16[8,96,768]{2,1,0:T(8,128)(2,1)} %bitcast.24), calls=%async_computation | async-start | bytes 2359296 | tf_op jit(solution)/shard_map/all_to_all | solution.py:1001
  109.3 15.2 %backward.2 = (bf16[1,512,192]{2,1,0:T(8,128)(2,1)}, bf16[1,512,192]{2,1,0:T(8,128)(2,1)}, bf16[1,512,192]{2,1,0:T(8,128)(2,1)}, bf16[1,512,192]{2,1,0:T(8,128)(...) custom-call(f32[1,136,384]{2,1,0:T(8,128)} %get-tuple-element.156.re, ...), custom_call_target="tpu_custom_call" | custom-call | flops 15000000512 | bytes 1500000 | tf_op jit(solution)/shard_map/backward/pallas_call | solution.py:1047
  127.5 16.3 %backward.3 = (bf16[1,512,192]{2,1,0:T(8,128)(2,1)}, bf16[1,512,192]{2,1,0:T(8,128)(2,1)}, bf16[1,512,192]{2,1,0:T(8,128)(2,1)}, bf16[1,512,192]{2,1,0:T(8,128)(...) custom-call(f32[1,128,384]{2,1,0:T(8,128)} %get-tuple-element.183.re, ...), custom_call_target="tpu_custom_call" | custom-call | flops 15000000512 | bytes 1500000 | tf_op jit(solution)/shard_map/backward/pallas_call | solution.py:1047
  146.4 2.8 %collective-permute-start.23 = (bf16[1,512,192]{2,1,0:T(8,128)(2,1)}, bf16[1,512,192]{2,1,0:T(8,128)(2,1)S(1)}, u32[]{:S(2)}, u32[]{:S(2)}) collective-permute-start(bf16[1,512,192]{2,1,0:T(8,128)(2,1)} %get-tuple-element.213), channel_id=1, source_target_pairs={{0,1},{1,0},{2,3},{3,2},{4,5},{5,4},{6,7},{7,6},{8,9},{9,8},{10,11... | collective-permute-start | bytes 589832 | tf_op jit(solution)/shard_map/ppermute | solution.py:748
  152.6 4.5 %collective-permute-done.21.refs_2_ = bf16[80,768]{1,0:T(8,128)(2,1)S(1)} collective-permute-done((bf16[80,768]{1,0:T(8,128)(2,1)}, bf16[80,768]{1,0:T(8,128)(2,1)S(1)}, u32[]{:S(2)}, u32[]{:S(2)}) %collective-permute-start.21) | collective-permute-done | bytes 122912 | tf_op jit(solution)/shard_map/ppermute | solution.py:1099
  157.7 2.2 %merge.1 = (bf16[512,768]{1,0:T(8,128)(2,1)}, f32[1,16,192]{2,1,0:T(8,128)}) custom-call(bf16[416,768]{1,0:T(8,128)(2,1)} %get-tuple-element.207.packed, bf16[80,768]{1,0:T(8,128)(2,1)} %get-tuple-element.208.refs_0_, bf16[80,768]{1,0:T(8,128)(2,1)} %copy-done.12, bf16[80,768]{1,0:T(8,128)(2,1)} %copy-done.13, bf16[80,768]{1,0:T(8,128)(2,1)} %collective-permute-done.22.refs_3_), custom_call_target="tpu_custom_call" | custom-call | flops 2000000000 | bytes 200000 | tf_op jit(solution)/shard_map/merge/pallas_call | solution.py:1104
  161.3 5.5 %collective-permute-done.23 = bf16[1,512,192]{2,1,0:T(8,128)(2,1)S(1)} collective-permute-done((bf16[1,512,192]{2,1,0:T(8,128)(2,1)}, bf16[1,512,192]{2,1,0:T(8,128)(2,1)S(1)}, u32[]{:S(2)}, u32[]{:S(2)}) %collective-permute-start.23) | collective-permute-done | bytes 196640 | tf_op jit(solution)/shard_map/ppermute | solution.py:748
  166.9 3.9 %all-to-all-start.1 = ((bf16[8,64,768]{2,1,0:T(8,128)(2,1)}), bf16[8,64,768]{2,1,0:T(8,128)(2,1)S(1)}, u32[]{:S(2)}, u32[]{:S(2)}) async-start(bf16[8,64,768]{2,1,0:T(8,128)(2,1)} %bitcast.25), calls=%async_computation.1 | async-start | bytes 1572864 | tf_op jit(solution)/shard_map/all_to_all | solution.py:1114
  175.0 8.4 %all-to-all-done.1 = bf16[8,64,768]{2,1,0:T(8,128)(2,1)S(1)} async-done(((bf16[8,64,768]{2,1,0:T(8,128)(2,1)}), bf16[8,64,768]{2,1,0:T(8,128)(2,1)S(1)}, u32[]{:S(2)}, u32[]{:S(2)}) %all-to-all-start.1) | async-done | bytes 786464 | tf_op jit(solution)/shard_map/all_to_all | solution.py:1114
  183.5 10.5 %all_gather.6.late = bf16[512,768]{1,0:T(8,128)(2,1)} all-gather(bf16[64,768]{1,0:T(8,128)(2,1)S(1)} %reduce_sum.24), channel_id=1, replica_groups=mesh['seq'=8,'head'=4] {'seq'}, dimensions={0}, use_global_device_ids=true | all-gather | bytes 884736 | tf_op jit(solution)/shard_map/all_gather | solution.py:802
  196.7 4.2 %unpack.1 = (f32[192]{0:T(256)}, f32[768,2,384]{2,1,0:T(2,128)}, f32[2,32,768]{2,1,0:T(8,128)}, f32[6,768]{1,0:T(8,128)}, f32[4,384]{1,0:T(4,128)}, /*index=5*/f...) custom-call(bf16[512,768]{1,0:T(8,128)(2,1)} %all_gather.6.late, ...), custom_call_target="tpu_custom_call" | custom-call | flops 4000000000 | bytes 400000 | tf_op jit(solution)/shard_map/unpack/pallas_call | solution.py:1130
  (108 shorter events, 50.1 us)
Async XLA Ops:
  9.1 15.8 %collective-permute-start = (bf16[64,896]{1,0:T(8,128)(2,1)}, bf16[64,896]{1,0:T(8,128)(2,1)S(1)}, u32[]{:S(2)}, u32[]{:S(2)}) collective-permute-start(bf16[64,896]{1,0:T(8,128)(2,1)} %get-tuple-element.128.refs_0_), channel_id=1, source_target_pairs={{0,1},{1,2},{2,3},{3,0},{4,5},{5,6},{6,7},{7,4},{8,9},{9,10},{10,1... | collective-permute-start | bytes 344072 | tf_op jit(solution)/shard_map/ppermute | solution.py:866
  12.2 12.7 %collective-permute-start.1 = (bf16[64,896]{1,0:T(8,128)(2,1)}, bf16[64,896]{1,0:T(8,128)(2,1)S(1)}, u32[]{:S(2)}, u32[]{:S(2)}) collective-permute-start(bf16[64,896]{1,0:T(8,128)(2,1)} %get-tuple-element.128.refs_0_), channel_id=1, source_target_pairs={{0,2},{1,3},{2,0},{3,1},{4,6},{5,7},{6,4},{7,5},{8,10},{9,11},{10,... | collective-permute-start | bytes 344072 | tf_op jit(solution)/shard_map/ppermute | solution.py:866
  14.8 10.1 %collective-permute-start.2 = (bf16[64,896]{1,0:T(8,128)(2,1)}, bf16[64,896]{1,0:T(8,128)(2,1)S(1)}, u32[]{:S(2)}, u32[]{:S(2)}) collective-permute-start(bf16[64,896]{1,0:T(8,128)(2,1)} %get-tuple-element.128.refs_0_), channel_id=1, source_target_pairs={{0,3},{1,0},{2,1},{3,2},{4,7},{5,4},{6,5},{7,6},{8,11},{9,8},{10,9... | collective-permute-start | bytes 344072 | tf_op jit(solution)/shard_map/ppermute | solution.py:866
  16.1 8.7 %collective-permute-start.3 = (bf16[1,16,896]{2,1,0:T(8,128)(2,1)}, bf16[1,16,896]{2,1,0:T(8,128)(2,1)S(1)}, u32[]{:S(2)}, u32[]{:S(2)}) collective-permute-start(bf16[1,16,896]{2,1,0:T(8,128)(2,1)} %get-tuple-element.137), channel_id=1, source_target_pairs={{0,4},{4,8},{8,12},{12,16},{16,20},{20,24},{24,28},{1,5},{5,9},{9,... | collective-permute-start | bytes 86024 | tf_op jit(solution)/shard_map/ppermute | solution.py:744
  42.8 10.8 %collective-permute-start.5 = (f32[1,136,384]{2,1,0:T(8,128)}, f32[1,136,384]{2,1,0:T(8,128)S(1)}, u32[]{:S(2)}, u32[]{:S(2)}) collective-permute-start(f32[1,136,384]{2,1,0:T(8,128)} %get-tuple-element.142), channel_id=1, source_target_pairs={{0,8},{4,12},{8,16},{12,20},{16,24},{20,28},{1,9},{5,13},{9,17},{1... | collective-permute-start | bytes 626696 | tf_op jit(solution)/shard_map/ppermute | solution.py:744
  46.2 10.6 %collective-permute-start.6 = (f32[1,136,384]{2,1,0:T(8,128)}, f32[1,136,384]{2,1,0:T(8,128)S(1)}, u32[]{:S(2)}, u32[]{:S(2)}) collective-permute-start(f32[1,136,384]{2,1,0:T(8,128)} %get-tuple-element.142), channel_id=1, source_target_pairs={{0,16},{4,20},{8,24},{12,28},{1,17},{5,21},{9,25},{13,29},{2,18},{... | collective-permute-start | bytes 626696 | tf_op jit(solution)/shard_map/ppermute | solution.py:744
  85.4 58.4 %collective-permute-start.15 = (bf16[1,1024,192]{2,1,0:T(8,128)(2,1)}, bf16[1,1024,192]{2,1,0:T(8,128)(2,1)S(1)}, u32[]{:S(2)}, u32[]{:S(2)}) collective-permute-start(bf16[1,1024,192]{2,1,0:T(8,128)(2,1)} %get-tuple-element.198), channel_id=1, source_target_pairs={{0,1},{1,0},{2,3},{3,2},{4,5},{5,4},{6,7},{7,6},{8,9},{9,8},{10,11... | collective-permute-start | bytes 1179656 | tf_op jit(solution)/shard_map/ppermute | solution.py:748
  85.7 58.1 %collective-permute-start.16 = (bf16[1,1024,192]{2,1,0:T(8,128)(2,1)}, bf16[1,1024,192]{2,1,0:T(8,128)(2,1)}, u32[]{:S(2)}, u32[]{:S(2)}) collective-permute-start(bf16[1,1024,192]{2,1,0:T(8,128)(2,1)} %get-tuple-element.199), channel_id=1, source_target_pairs={{0,2},{1,3},{2,0},{3,1},{4,6},{5,7},{6,4},{7,5},{8,10},{9,11},{10,... | collective-permute-start | bytes 1179656 | tf_op jit(solution)/shard_map/ppermute | solution.py:748
  90.4 16.9 %collective-permute-start.12 = (f32[1,136,384]{2,1,0:T(8,128)}, f32[1,136,384]{2,1,0:T(8,128)S(1)}, u32[]{:S(2)}, u32[]{:S(2)}) collective-permute-start(f32[1,136,384]{2,1,0:T(8,128)} %get-tuple-element.158), channel_id=1, source_target_pairs={{8,0},{12,4},{16,8},{20,12},{24,16},{28,20},{9,1},{13,5},{17,9},{2... | collective-permute-start | bytes 626696 | tf_op jit(solution)/shard_map/ppermute | solution.py:744
  91.6 17.6 %collective-permute-start.13 = (f32[1,136,384]{2,1,0:T(8,128)}, f32[1,136,384]{2,1,0:T(8,128)}, u32[]{:S(2)}, u32[]{:S(2)}) collective-permute-start(f32[1,136,384]{2,1,0:T(8,128)} %get-tuple-element.158), channel_id=1, source_target_pairs={{16,0},{20,4},{24,8},{28,12},{17,1},{21,5},{25,9},{29,13},{18,2},{... | collective-permute-start | bytes 626696 | tf_op jit(solution)/shard_map/ppermute | solution.py:744
  92.9 16.3 %collective-permute-start.14 = (f32[1,136,384]{2,1,0:T(8,128)}, f32[1,136,384]{2,1,0:T(8,128)}, u32[]{:S(2)}, u32[]{:S(2)}) collective-permute-start(f32[1,136,384]{2,1,0:T(8,128)} %get-tuple-element.158), channel_id=1, source_target_pairs={{24,0},{28,4},{25,1},{29,5},{26,2},{30,6},{27,3},{31,7}} | collective-permute-start | bytes 626696 | tf_op jit(solution)/shard_map/ppermute | solution.py:744
  99.7 24.8 %all-to-all-start = ((bf16[8,96,768]{2,1,0:T(8,128)(2,1)}), bf16[8,96,768]{2,1,0:T(8,128)(2,1)S(1)}, u32[]{:S(2)}, u32[]{:S(2)}) async-start(bf16[8,96,768]{2,1,0:T(8,128)(2,1)} %bitcast.24), calls=%async_computation | async-start | bytes 2359296 | tf_op jit(solution)/shard_map/all_to_all | solution.py:1001
  107.0 89.6 %all-gather.2.cloned.1.call-start = ((), (), s32[]{:S(2)}) async-start(), calls=%async_computation.2 | async-start | bytes 1327104 | tf_op jit(solution)/shard_map/all_gather | solution.py:802
  107.3 36.5 %collective-permute-start.17 = (bf16[1,1024,192]{2,1,0:T(8,128)(2,1)}, bf16[1,1024,192]{2,1,0:T(8,128)(2,1)}, u32[]{:S(2)}, u32[]{:S(2)}) collective-permute-start(bf16[1,1024,192]{2,1,0:T(8,128)(2,1)} %get-tuple-element.200), channel_id=1, source_target_pairs={{0,3},{1,2},{2,1},{3,0},{4,7},{5,6},{6,5},{7,4},{8,11},{9,10},{10,... | collective-permute-start | bytes 1179656 | tf_op jit(solution)/shard_map/ppermute | solution.py:748
  124.5 19.3 %collective-permute-start.18 = (bf16[1,512,192]{2,1,0:T(8,128)(2,1)}, bf16[1,512,192]{2,1,0:T(8,128)(2,1)}, u32[]{:S(2)}, u32[]{:S(2)}) collective-permute-start(bf16[1,512,192]{2,1,0:T(8,128)(2,1)} %get-tuple-element.201), channel_id=1, source_target_pairs={{0,1},{1,0},{2,3},{3,2},{4,5},{5,4},{6,7},{7,6},{8,9},{9,8},{10,11... | collective-permute-start | bytes 589832 | tf_op jit(solution)/shard_map/ppermute | solution.py:748
  124.6 19.2 %collective-permute-start.19 = (bf16[1,512,192]{2,1,0:T(8,128)(2,1)}, bf16[1,512,192]{2,1,0:T(8,128)(2,1)S(1)}, u32[]{:S(2)}, u32[]{:S(2)}) collective-permute-start(bf16[1,512,192]{2,1,0:T(8,128)(2,1)} %get-tuple-element.202), channel_id=1, source_target_pairs={{0,1},{1,0},{2,3},{3,2},{4,5},{5,4},{6,7},{7,6},{8,9},{9,8},{10,11... | collective-permute-start | bytes 589832 | tf_op jit(solution)/shard_map/ppermute | solution.py:748
  145.8 11.3 %collective-permute-start.21 = (bf16[80,768]{1,0:T(8,128)(2,1)}, bf16[80,768]{1,0:T(8,128)(2,1)S(1)}, u32[]{:S(2)}, u32[]{:S(2)}) collective-permute-start(bf16[80,768]{1,0:T(8,128)(2,1)} %get-tuple-element.210), channel_id=1, source_target_pairs={{0,2},{1,3},{2,0},{3,1},{4,6},{5,7},{6,4},{7,5},{8,10},{9,11},{10,... | collective-permute-start | bytes 368648 | tf_op jit(solution)/shard_map/ppermute | solution.py:1099
  145.8 11.3 %collective-permute-start.22 = (bf16[80,768]{1,0:T(8,128)(2,1)}, bf16[80,768]{1,0:T(8,128)(2,1)}, u32[]{:S(2)}, u32[]{:S(2)}) collective-permute-start(bf16[80,768]{1,0:T(8,128)(2,1)} %get-tuple-element.211), channel_id=1, source_target_pairs={{0,1},{1,2},{2,3},{3,0},{4,5},{5,6},{6,7},{7,4},{8,9},{9,10},{10,1... | collective-permute-start | bytes 368648 | tf_op jit(solution)/shard_map/ppermute | solution.py:1099
  146.4 20.5 %collective-permute-start.23 = (bf16[1,512,192]{2,1,0:T(8,128)(2,1)}, bf16[1,512,192]{2,1,0:T(8,128)(2,1)S(1)}, u32[]{:S(2)}, u32[]{:S(2)}) collective-permute-start(bf16[1,512,192]{2,1,0:T(8,128)(2,1)} %get-tuple-element.213), channel_id=1, source_target_pairs={{0,1},{1,0},{2,3},{3,2},{4,5},{5,4},{6,7},{7,6},{8,9},{9,8},{10,11... | collective-permute-start | bytes 589832 | tf_op jit(solution)/shard_map/ppermute | solution.py:748
  149.2 25.8 %collective-permute-start.24 = (bf16[1,512,192]{2,1,0:T(8,128)(2,1)}, bf16[1,512,192]{2,1,0:T(8,128)(2,1)S(1)}, u32[]{:S(2)}, u32[]{:S(2)}) collective-permute-start(bf16[1,512,192]{2,1,0:T(8,128)(2,1)} %get-tuple-element.216), channel_id=1, source_target_pairs={{0,1},{1,0},{2,3},{3,2},{4,5},{5,4},{6,7},{7,6},{8,9},{9,8},{10,11... | collective-permute-start | bytes 589832 | tf_op jit(solution)/shard_map/ppermute | solution.py:748
  151.0 23.0 %collective-permute-start.26 = (bf16[1,512,192]{2,1,0:T(8,128)(2,1)}, bf16[1,512,192]{2,1,0:T(8,128)(2,1)}, u32[]{:S(2)}, u32[]{:S(2)}) collective-permute-start(bf16[1,512,192]{2,1,0:T(8,128)(2,1)} %add_convert_fusion.1), channel_id=1, source_target_pairs={{0,2},{1,3},{2,0},{3,1},{4,6},{5,7},{6,4},{7,5},{8,10},{9,11},{10,... | collective-permute-start | bytes 589832 | tf_op jit(solution)/shard_map/ppermute | solution.py:748
  159.9 13.8 %collective-permute-start.27 = (f32[1,16,192]{2,1,0:T(8,128)}, f32[1,16,192]{2,1,0:T(8,128)S(1)}, u32[]{:S(2)}, u32[]{:S(2)}) collective-permute-start(f32[1,16,192]{2,1,0:T(8,128)} %get-tuple-element.225), channel_id=1, source_target_pairs={{4,0},{8,4},{12,8},{16,12},{20,16},{24,20},{28,24},{5,1},{9,5},{13... | collective-permute-start | bytes 36872 | tf_op jit(solution)/shard_map/ppermute | solution.py:744
  166.9 16.5 %all-to-all-start.1 = ((bf16[8,64,768]{2,1,0:T(8,128)(2,1)}), bf16[8,64,768]{2,1,0:T(8,128)(2,1)S(1)}, u32[]{:S(2)}, u32[]{:S(2)}) async-start(bf16[8,64,768]{2,1,0:T(8,128)(2,1)} %bitcast.25), calls=%async_computation.1 | async-start | bytes 1572864 | tf_op jit(solution)/shard_map/all_to_all | solution.py:1114
  173.8 20.2 %collective-permute-start.25 = (bf16[1,512,192]{2,1,0:T(8,128)(2,1)S(1)}, bf16[1,512,192]{2,1,0:T(8,128)(2,1)S(1)}, u32[]{:S(2)}, u32[]{:S(2)}) collective-permute-start(bf16[1,512,192]{2,1,0:T(8,128)(2,1)S(1)} %add_convert_fusion.2), channel_id=1, source_target_pairs={{0,2},{1,3},{2,0},{3,1},{4,6},{5,7},{6,4},{7,5},{8,10},{9,11},{10,... | collective-permute-start | bytes 589832 | tf_op jit(solution)/shard_map/ppermute | solution.py:748
  (28 other events, 140.5 us)
Sparse Core Ops, SparseCore 0:
  127.6 23.8 all-gather.1

commit v5 on v4

--- a/solution.py
+++ b/solution.py
@@ -1081,7 +1081,7 @@
             fades, win, ws, wst, hp, ci, cs, gain_in, grad_gain_out, grad_skip,
         )
 
-    first = groups // 2
+    first = min(1, groups // 2)
     if first:
         outs = backward_call(True, False, first, groups - first, [])
         outs, early = ordered(outs, early)

time: 209 us -> 211 us (level)
    all_to_all x1, waiting for transfers between devices: 8.38 us -> 0.52 us  [on_device(): lax.all_to_all(late.reshape(seq_count, chunk, -1), 'seq', 0, 0, tiled=True)]
    ppermute x11, waiting for transfers between devices: 6.86 us -> 14.3 us  [crossed(): lax.ppermute(block, axis, [(i, i ^ mask) for i in range(lax.axis_size(axi...]
    unnamed x45 -> x53, local copies, waits for them, and re-layouts: 7.41 us -> 8.06 us
  transfers between devices with their start and end apart: 31 -> 31, of which waited for: 8 -> 11; matrix products, arithmetic and copies ran while one was open for 7% -> 7% of each run, Pallas kernels for 25% -> 24%
where the time goes in v5:
time: 211 us; the launch traced here: 210 us
  Pallas kernels  84.6 us (40%)
  starting transfers between devices  51.2 us (24%)
  waiting for transfers between devices  29.4 us (14%)
  between operations  14.4 us (7%)
  blocking collectives  11.3 us (5%)
  local copies, waits for them, and re-layouts  8.06 us (4%)
  other arithmetic  7.63 us (4%)
  matrix products  3.2 us (2%)
    pallas_call x2, Pallas kernels, backward_call(): pl.pallas_call(functools.partial(backward_kernel, start_call, end_call, l...  30.1 us
    ppermute x11, waiting for transfers between devices, crossed(): lax.ppermute(block, axis, [(i, i ^ mask) for i in range(lax.axis_size(axi...  14.3 us
    ppermute x8, starting transfers between devices, shifted(): lax.ppermute(block, axis, [(i - distance, i) for i in devices if i - dist...  14 us
    ppermute x11, starting transfers between devices, crossed(): lax.ppermute(block, axis, [(i, i ^ mask) for i in range(lax.axis_size(axi...  13.8 us
    all_gather x1, blocking collectives, gather_sum(): return lax.all_gather(total, 'seq', axis=0, tiled=True)  11.3 us
    pallas_call x1, Pallas kernels, on_device(): pl.pallas_call(functools.partial(forward_kernel, len(found)), grid=grid,...  11 us
    unnamed x53, local copies, waits for them, and re-layouts  8.06 us
    pallas_call x1, Pallas kernels, on_device(): pl.pallas_call(functools.partial(gate_kernel, len(sums_all)), grid=grid,...  7.46 us
  transfers between devices with their start and end apart: 31, of which 11 were waited for; matrix products, arithmetic and copies ran while one was open for 7% of the time, Pallas kernels for 24%

profile of v5, /device:TPU:0, one launch (start us, length us, event | category | flops | bytes accessed | tf_op | source)
XLA Modules:
  0.0 209.8 jit_solution(18384226136881327029)
XLA Ops:
  9.1 3.1 %collective-permute-start = (bf16[64,896]{1,0:T(8,128)(2,1)}, bf16[64,896]{1,0:T(8,128)(2,1)S(1)}, u32[]{:S(2)}, u32[]{:S(2)}) collective-permute-start(bf16[64,896]{1,0:T(8,128)(2,1)} %get-tuple-element.128.refs_0_), channel_id=1, source_target_pairs={{0,1},{1,2},{2,3},{3,0},{4,5},{5,6},{6,7},{7,4},{8,9},{9,10},{10,1... | collective-permute-start | bytes 344072 | tf_op jit(solution)/shard_map/ppermute | solution.py:866
  12.2 2.6 %collective-permute-start.1 = (bf16[64,896]{1,0:T(8,128)(2,1)}, bf16[64,896]{1,0:T(8,128)(2,1)S(1)}, u32[]{:S(2)}, u32[]{:S(2)}) collective-permute-start(bf16[64,896]{1,0:T(8,128)(2,1)} %get-tuple-element.128.refs_0_), channel_id=1, source_target_pairs={{0,2},{1,3},{2,0},{3,1},{4,6},{5,7},{6,4},{7,5},{8,10},{9,11},{10,... | collective-permute-start | bytes 344072 | tf_op jit(solution)/shard_map/ppermute | solution.py:866
  18.7 6.2 %project.1 = (bf16[1,1024,768]{2,1,0:T(8,128)(2,1)}, bf16[1,1024,384]{2,1,0:T(8,128)(2,1)}, f32[1,1024,384]{2,1,0:T(8,128)}, f32[1,1024,128]{2,1,0:T(8,128)}, f3...) custom-call(bf16[1,1024,768]{2,1,0:T(8,128)(2,1)} %refs_7_.1, ...), custom_call_target="tpu_custom_call" | custom-call | flops 6000000000 | bytes 600000 | tf_op jit(solution)/shard_map/project/pallas_call | solution.py:874
  25.6 11.0 %forward.1 = (f32[1,1024,384]{2,1,0:T(8,128)}, bf16[1,1024,384]{2,1,0:T(8,128)(2,1)}, bf16[1,1024,256]{2,1,0:T(8,128)(2,1)}, bf16[1,1024,256]{2,1,0:T(8,128)(2,1...) custom-call(bf16[64,896]{1,0:T(8,128)(2,1)} %get-tuple-element.128.r, ...), custom_call_target="tpu_custom_call" | custom-call | flops 10000000000 | bytes 1000000 | tf_op jit(solution)/shard_map/forward/pallas_call | solution.py:895
  36.6 2.3 %collective-permute-start.4 = (f32[1,136,384]{2,1,0:T(8,128)}, f32[1,136,384]{2,1,0:T(8,128)S(1)}, u32[]{:S(2)}, u32[]{:S(2)}) collective-permute-start(f32[1,136,384]{2,1,0:T(8,128)} %get-tuple-element.139.own), channel_id=1, source_target_pairs={{0,4},{4,0},{8,12},{12,8},{16,20},{20,16},{24,28},{28,24},{1,5},{5... | collective-permute-start | bytes 626696 | tf_op jit(solution)/shard_map/ppermute | solution.py:748
  42.8 3.4 %collective-permute-start.5 = (f32[1,136,384]{2,1,0:T(8,128)}, f32[1,136,384]{2,1,0:T(8,128)S(1)}, u32[]{:S(2)}, u32[]{:S(2)}) collective-permute-start(f32[1,136,384]{2,1,0:T(8,128)} %get-tuple-element.142), channel_id=1, source_target_pairs={{0,8},{4,12},{8,16},{12,20},{16,24},{20,28},{1,9},{5,13},{9,17},{1... | collective-permute-start | bytes 626696 | tf_op jit(solution)/shard_map/ppermute | solution.py:744
  50.4 3.2 %fusion.2.refs_8_.refs_6_ = f32[1,1024,384]{2,1,0:T(8,128)} fusion(bf16[384,768]{1,0:T(8,128)(2,1)} %wout.1, bf16[1,1024,768]{2,1,0:T(8,128)(2,1)S(1)} %copy-done), kind=kOutput, calls=%fused_computation.2 | convolution fusion | flops 603979776 | bytes 3735552 | tf_op jit(solution)/shard_map/rsd,cd->rsc/dot_general | solution.py:927
  53.6 3.2 %collective-permute-done.6.refs_2_ = f32[1,136,384]{2,1,0:T(8,128)S(1)} collective-permute-done((f32[1,136,384]{2,1,0:T(8,128)}, f32[1,136,384]{2,1,0:T(8,128)S(1)}, u32[]{:S(2)}, u32[]{:S(2)}) %collective-permute-start.6) | collective-permute-done | bytes 208928 | tf_op jit(solution)/shard_map/ppermute | solution.py:744
  57.5 7.3 %mix.1 = (f32[1,1024,384]{2,1,0:T(8,128)}, f32[1,4,8,256]{3,2,1,0:T(8,128)}, f32[1,4,128,384]{3,2,1,0:T(8,128)}) custom-call(f32[1,136,384]{2,1,0:T(8,128)} %get-tuple-element.140.refs_0_, f32[1,136,384]{2,1,0:T(8,128)} %copy-done.11, f32[1,136,384]{2,1,0:T(8,128)} %copy-done.12, f32[1,136,384]{2,1,0:T(8,128)} %collective-permute-done.7.refs_3_, ...), custom_call_target="tpu_custom_call" | custom-call | flops 6000000000 | bytes 600000 | tf_op jit(solution)/shard_map/mix/pallas_call | solution.py:928
  69.0 2.3 %collective-permute-done.8.refs_1_ = f32[1,4,8,256]{3,2,1,0:T(8,128)S(1)} collective-permute-done((f32[1,4,8,256]{3,2,1,0:T(8,128)}, f32[1,4,8,256]{3,2,1,0:T(8,128)S(1)}, u32[]{:S(2)}, u32[]{:S(2)}) %collective-permute-start.8) | collective-permute-done | bytes 32800 | tf_op jit(solution)/shard_map/ppermute | solution.py:947
  72.9 7.5 %gate.1 = (f32[1,1024,384]{2,1,0:T(8,128)}, bf16[1,1024,384]{2,1,0:T(8,128)(2,1)}, bf16[1,1024,384]{2,1,0:T(8,128)(2,1)}, f32[1,4,128,384]{3,2,1,0:T(8,128)}, f3...) custom-call(f32[1,4,8,256]{3,2,1,0:T(8,128)} %get-tuple-element.151.refs_0_, ...), custom_call_target="tpu_custom_call" | custom-call | flops 6000000000 | bytes 600000 | tf_op jit(solution)/shard_map/gate/pallas_call | solution.py:949
  80.4 4.9 %branch.1 = (bf16[1,1024,192]{2,1,0:T(8,128)(2,1)}, bf16[1,1024,192]{2,1,0:T(8,128)(2,1)}, bf16[1,1024,192]{2,1,0:T(8,128)(2,1)}, bf16[1,1024,192]{2,1,0:T(8,128)(2,1)}) custom-call(s32[1]{0:T(128)} %bitcast.me.refs_4_.refs_6_, bf16[1,1024,384]{2,1,0:T(8,128)(2,1)} %get-tuple-element.182.normed_out, bf16[384,768]{1,0:T(8,128)(2,1)} %wout.1), custom_call_target="tpu_custom_call" | custom-call | flops 3000000000 | bytes 300000 | tf_op jit(solution)/shard_map/branch/pallas_call | solution.py:974
  94.2 5.5 %out.1 = bf16[768,768]{1,0:T(8,128)(2,1)} custom-call(bf16[1,1024,384]{2,1,0:T(8,128)(2,1)} %get-tuple-element.182.normed_out, bf16[1,1024,768]{2,1,0:T(8,128)(2,1)} %cot.1, bf16[1,1024,384]{2,1,0:T(8,128)(2,1)} %get-tuple-element.163.refs_19_.dgate.refs_21_, bf16[1,1024,768]{2,1,0:T(8,128)(2,1)} %get-tuple-element.133.refs_5_.refs_8_.normed.refs_10_), custom_call_target="tpu_custom_call" | custom-call | flops 5000000000 | bytes 500000 | tf_op jit(solution)/shard_map/out/pallas_call | solution.py:986
  99.7 7.3 %all-to-all-start = ((bf16[8,96,768]{2,1,0:T(8,128)(2,1)}), bf16[8,96,768]{2,1,0:T(8,128)(2,1)S(1)}, u32[]{:S(2)}, u32[]{:S(2)}) async-start(bf16[8,96,768]{2,1,0:T(8,128)(2,1)} %bitcast.24), calls=%async_computation | async-start | bytes 2359296 | tf_op jit(solution)/shard_map/all_to_all | solution.py:1001
  109.3 20.4 %backward.2 = (bf16[1,768,192]{2,1,0:T(8,128)(2,1)}, bf16[1,768,192]{2,1,0:T(8,128)(2,1)}, bf16[1,768,192]{2,1,0:T(8,128)(2,1)}, bf16[1,768,192]{2,1,0:T(8,128)(...) custom-call(f32[1,136,384]{2,1,0:T(8,128)} %get-tuple-element.156.re, ...), custom_call_target="tpu_custom_call" | custom-call | flops 15000000512 | bytes 1500000 | tf_op jit(solution)/shard_map/backward/pallas_call | solution.py:1047
  132.6 9.8 %backward.3 = (bf16[1,256,192]{2,1,0:T(8,128)(2,1)}, bf16[1,256,192]{2,1,0:T(8,128)(2,1)}, bf16[1,256,192]{2,1,0:T(8,128)(2,1)}, bf16[1,256,192]{2,1,0:T(8,128)(...) custom-call(f32[1,128,384]{2,1,0:T(8,128)} %get-tuple-element.183.re, ...), custom_call_target="tpu_custom_call" | custom-call | flops 15000000512 | bytes 1500000 | tf_op jit(solution)/shard_map/backward/pallas_call | solution.py:1047
  142.4 7.0 %collective-permute-done.19 = bf16[1,768,192]{2,1,0:T(8,128)(2,1)} collective-permute-done((bf16[1,768,192]{2,1,0:T(8,128)(2,1)}, bf16[1,768,192]{2,1,0:T(8,128)(2,1)}, u32[]{:S(2)}, u32[]{:S(2)}) %collective-permute-start.19) | collective-permute-done | bytes 294944 | tf_op jit(solution)/shard_map/ppermute | solution.py:748
  152.2 2.6 %collective-permute-start.23 = (bf16[1,256,192]{2,1,0:T(8,128)(2,1)}, bf16[1,256,192]{2,1,0:T(8,128)(2,1)S(1)}, u32[]{:S(2)}, u32[]{:S(2)}) collective-permute-start(bf16[1,256,192]{2,1,0:T(8,128)(2,1)} %get-tuple-element.213), channel_id=1, source_target_pairs={{0,1},{1,0},{2,3},{3,2},{4,5},{5,4},{6,7},{7,6},{8,9},{9,8},{10,11... | collective-permute-start | bytes 294920 | tf_op jit(solution)/shard_map/ppermute | solution.py:748
  157.7 5.2 %collective-permute-done.21.refs_2_ = bf16[80,768]{1,0:T(8,128)(2,1)S(1)} collective-permute-done((bf16[80,768]{1,0:T(8,128)(2,1)}, bf16[80,768]{1,0:T(8,128)(2,1)S(1)}, u32[]{:S(2)}, u32[]{:S(2)}) %collective-permute-start.21) | collective-permute-done | bytes 122912 | tf_op jit(solution)/shard_map/ppermute | solution.py:1099
  164.1 2.2 %merge.1 = (bf16[512,768]{1,0:T(8,128)(2,1)}, f32[1,16,192]{2,1,0:T(8,128)}) custom-call(bf16[416,768]{1,0:T(8,128)(2,1)} %get-tuple-element.207.packed, bf16[80,768]{1,0:T(8,128)(2,1)} %get-tuple-element.208.refs_0_, bf16[80,768]{1,0:T(8,128)(2,1)} %copy-done.14, bf16[80,768]{1,0:T(8,128)(2,1)} %copy-done.15, bf16[80,768]{1,0:T(8,128)(2,1)} %copy-done.16), custom_call_target="tpu_custom_call" | custom-call | flops 2000000000 | bytes 200000 | tf_op jit(solution)/shard_map/merge/pallas_call | solution.py:1104
  167.6 3.6 %all-to-all-start.1 = ((bf16[8,64,768]{2,1,0:T(8,128)(2,1)}), bf16[8,64,768]{2,1,0:T(8,128)(2,1)S(1)}, u32[]{:S(2)}, u32[]{:S(2)}) async-start(bf16[8,64,768]{2,1,0:T(8,128)(2,1)} %bitcast.25), calls=%async_computation.1 | async-start | bytes 1572864 | tf_op jit(solution)/shard_map/all_to_all | solution.py:1114
  177.2 4.8 %collective-permute-done.26 = bf16[1,768,192]{2,1,0:T(8,128)(2,1)} collective-permute-done((bf16[1,768,192]{2,1,0:T(8,128)(2,1)S(1)}, bf16[1,768,192]{2,1,0:T(8,128)(2,1)}, u32[]{:S(2)}, u32[]{:S(2)}) %collective-permute-start.26) | collective-permute-done | bytes 294944 | tf_op jit(solution)/shard_map/ppermute | solution.py:748
  183.9 11.3 %all_gather.6.late = bf16[512,768]{1,0:T(8,128)(2,1)} all-gather(bf16[64,768]{1,0:T(8,128)(2,1)S(1)} %reduce_sum.24), channel_id=1, replica_groups=mesh['seq'=8,'head'=4] {'seq'}, dimensions={0}, use_global_device_ids=true | all-gather | bytes 884736 | tf_op jit(solution)/shard_map/all_gather | solution.py:802
  198.7 4.2 %unpack.1 = (f32[192]{0:T(256)}, f32[768,2,384]{2,1,0:T(2,128)}, f32[2,32,768]{2,1,0:T(8,128)}, f32[6,768]{1,0:T(8,128)}, f32[4,384]{1,0:T(4,128)}, /*index=5*/f...) custom-call(bf16[512,768]{1,0:T(8,128)(2,1)} %all_gather.6.late, ...), custom_call_target="tpu_custom_call" | custom-call | flops 4000000000 | bytes 400000 | tf_op jit(solution)/shard_map/unpack/pallas_call | solution.py:1130
  (116 shorter events, 54.5 us)
Async XLA Ops:
  9.1 15.8 %collective-permute-start = (bf16[64,896]{1,0:T(8,128)(2,1)}, bf16[64,896]{1,0:T(8,128)(2,1)S(1)}, u32[]{:S(2)}, u32[]{:S(2)}) collective-permute-start(bf16[64,896]{1,0:T(8,128)(2,1)} %get-tuple-element.128.refs_0_), channel_id=1, source_target_pairs={{0,1},{1,2},{2,3},{3,0},{4,5},{5,6},{6,7},{7,4},{8,9},{9,10},{10,1... | collective-permute-start | bytes 344072 | tf_op jit(solution)/shard_map/ppermute | solution.py:866
  12.2 12.7 %collective-permute-start.1 = (bf16[64,896]{1,0:T(8,128)(2,1)}, bf16[64,896]{1,0:T(8,128)(2,1)S(1)}, u32[]{:S(2)}, u32[]{:S(2)}) collective-permute-start(bf16[64,896]{1,0:T(8,128)(2,1)} %get-tuple-element.128.refs_0_), channel_id=1, source_target_pairs={{0,2},{1,3},{2,0},{3,1},{4,6},{5,7},{6,4},{7,5},{8,10},{9,11},{10,... | collective-permute-start | bytes 344072 | tf_op jit(solution)/shard_map/ppermute | solution.py:866
  14.8 10.1 %collective-permute-start.2 = (bf16[64,896]{1,0:T(8,128)(2,1)}, bf16[64,896]{1,0:T(8,128)(2,1)S(1)}, u32[]{:S(2)}, u32[]{:S(2)}) collective-permute-start(bf16[64,896]{1,0:T(8,128)(2,1)} %get-tuple-element.128.refs_0_), channel_id=1, source_target_pairs={{0,3},{1,0},{2,1},{3,2},{4,7},{5,4},{6,5},{7,6},{8,11},{9,8},{10,9... | collective-permute-start | bytes 344072 | tf_op jit(solution)/shard_map/ppermute | solution.py:866
  16.1 8.7 %collective-permute-start.3 = (bf16[1,16,896]{2,1,0:T(8,128)(2,1)}, bf16[1,16,896]{2,1,0:T(8,128)(2,1)S(1)}, u32[]{:S(2)}, u32[]{:S(2)}) collective-permute-start(bf16[1,16,896]{2,1,0:T(8,128)(2,1)} %get-tuple-element.137), channel_id=1, source_target_pairs={{0,4},{4,8},{8,12},{12,16},{16,20},{20,24},{24,28},{1,5},{5,9},{9,... | collective-permute-start | bytes 86024 | tf_op jit(solution)/shard_map/ppermute | solution.py:744
  42.8 10.8 %collective-permute-start.5 = (f32[1,136,384]{2,1,0:T(8,128)}, f32[1,136,384]{2,1,0:T(8,128)S(1)}, u32[]{:S(2)}, u32[]{:S(2)}) collective-permute-start(f32[1,136,384]{2,1,0:T(8,128)} %get-tuple-element.142), channel_id=1, source_target_pairs={{0,8},{4,12},{8,16},{12,20},{16,24},{20,28},{1,9},{5,13},{9,17},{1... | collective-permute-start | bytes 626696 | tf_op jit(solution)/shard_map/ppermute | solution.py:744
  46.2 10.6 %collective-permute-start.6 = (f32[1,136,384]{2,1,0:T(8,128)}, f32[1,136,384]{2,1,0:T(8,128)S(1)}, u32[]{:S(2)}, u32[]{:S(2)}) collective-permute-start(f32[1,136,384]{2,1,0:T(8,128)} %get-tuple-element.142), channel_id=1, source_target_pairs={{0,16},{4,20},{8,24},{12,28},{1,17},{5,21},{9,25},{13,29},{2,18},{... | collective-permute-start | bytes 626696 | tf_op jit(solution)/shard_map/ppermute | solution.py:744
  48.4 8.4 %collective-permute-start.7 = (f32[1,136,384]{2,1,0:T(8,128)}, f32[1,136,384]{2,1,0:T(8,128)}, u32[]{:S(2)}, u32[]{:S(2)}) collective-permute-start(f32[1,136,384]{2,1,0:T(8,128)} %get-tuple-element.142), channel_id=1, source_target_pairs={{0,24},{4,28},{1,25},{5,29},{2,26},{6,30},{3,27},{7,31}} | collective-permute-start | bytes 626696 | tf_op jit(solution)/shard_map/ppermute | solution.py:744
  85.4 57.0 %collective-permute-start.15 = (bf16[1,1024,192]{2,1,0:T(8,128)(2,1)}, bf16[1,1024,192]{2,1,0:T(8,128)(2,1)S(1)}, u32[]{:S(2)}, u32[]{:S(2)}) collective-permute-start(bf16[1,1024,192]{2,1,0:T(8,128)(2,1)} %get-tuple-element.198), channel_id=1, source_target_pairs={{0,1},{1,0},{2,3},{3,2},{4,5},{5,4},{6,7},{7,6},{8,9},{9,8},{10,11... | collective-permute-start | bytes 1179656 | tf_op jit(solution)/shard_map/ppermute | solution.py:748
  85.7 56.7 %collective-permute-start.16 = (bf16[1,1024,192]{2,1,0:T(8,128)(2,1)}, bf16[1,1024,192]{2,1,0:T(8,128)(2,1)}, u32[]{:S(2)}, u32[]{:S(2)}) collective-permute-start(bf16[1,1024,192]{2,1,0:T(8,128)(2,1)} %get-tuple-element.199), channel_id=1, source_target_pairs={{0,2},{1,3},{2,0},{3,1},{4,6},{5,7},{6,4},{7,5},{8,10},{9,11},{10,... | collective-permute-start | bytes 1179656 | tf_op jit(solution)/shard_map/ppermute | solution.py:748
  90.4 16.9 %collective-permute-start.12 = (f32[1,136,384]{2,1,0:T(8,128)}, f32[1,136,384]{2,1,0:T(8,128)S(1)}, u32[]{:S(2)}, u32[]{:S(2)}) collective-permute-start(f32[1,136,384]{2,1,0:T(8,128)} %get-tuple-element.158), channel_id=1, source_target_pairs={{8,0},{12,4},{16,8},{20,12},{24,16},{28,20},{9,1},{13,5},{17,9},{2... | collective-permute-start | bytes 626696 | tf_op jit(solution)/shard_map/ppermute | solution.py:744
  91.6 17.6 %collective-permute-start.13 = (f32[1,136,384]{2,1,0:T(8,128)}, f32[1,136,384]{2,1,0:T(8,128)}, u32[]{:S(2)}, u32[]{:S(2)}) collective-permute-start(f32[1,136,384]{2,1,0:T(8,128)} %get-tuple-element.158), channel_id=1, source_target_pairs={{16,0},{20,4},{24,8},{28,12},{17,1},{21,5},{25,9},{29,13},{18,2},{... | collective-permute-start | bytes 626696 | tf_op jit(solution)/shard_map/ppermute | solution.py:744
  92.9 16.3 %collective-permute-start.14 = (f32[1,136,384]{2,1,0:T(8,128)}, f32[1,136,384]{2,1,0:T(8,128)}, u32[]{:S(2)}, u32[]{:S(2)}) collective-permute-start(f32[1,136,384]{2,1,0:T(8,128)} %get-tuple-element.158), channel_id=1, source_target_pairs={{24,0},{28,4},{25,1},{29,5},{26,2},{30,6},{27,3},{31,7}} | collective-permute-start | bytes 626696 | tf_op jit(solution)/shard_map/ppermute | solution.py:744
  99.7 29.9 %all-to-all-start = ((bf16[8,96,768]{2,1,0:T(8,128)(2,1)}), bf16[8,96,768]{2,1,0:T(8,128)(2,1)S(1)}, u32[]{:S(2)}, u32[]{:S(2)}) async-start(bf16[8,96,768]{2,1,0:T(8,128)(2,1)} %bitcast.24), calls=%async_computation | async-start | bytes 2359296 | tf_op jit(solution)/shard_map/all_to_all | solution.py:1001
  107.0 91.7 %all-gather.2.cloned.1.call-start = ((), (), s32[]{:S(2)}) async-start(), calls=%async_computation.2 | async-start | bytes 1327104 | tf_op jit(solution)/shard_map/all_gather | solution.py:802
  107.3 35.1 %collective-permute-start.17 = (bf16[1,1024,192]{2,1,0:T(8,128)(2,1)}, bf16[1,1024,192]{2,1,0:T(8,128)(2,1)}, u32[]{:S(2)}, u32[]{:S(2)}) collective-permute-start(bf16[1,1024,192]{2,1,0:T(8,128)(2,1)} %get-tuple-element.200), channel_id=1, source_target_pairs={{0,3},{1,2},{2,1},{3,0},{4,7},{5,6},{6,5},{7,4},{8,11},{9,10},{10,... | collective-permute-start | bytes 1179656 | tf_op jit(solution)/shard_map/ppermute | solution.py:748
  129.6 12.8 %collective-permute-start.18 = (bf16[1,768,192]{2,1,0:T(8,128)(2,1)}, bf16[1,768,192]{2,1,0:T(8,128)(2,1)}, u32[]{:S(2)}, u32[]{:S(2)}) collective-permute-start(bf16[1,768,192]{2,1,0:T(8,128)(2,1)} %get-tuple-element.201), channel_id=1, source_target_pairs={{0,1},{1,0},{2,3},{3,2},{4,5},{5,4},{6,7},{7,6},{8,9},{9,8},{10,11... | collective-permute-start | bytes 884744 | tf_op jit(solution)/shard_map/ppermute | solution.py:748
  129.7 19.8 %collective-permute-start.19 = (bf16[1,768,192]{2,1,0:T(8,128)(2,1)}, bf16[1,768,192]{2,1,0:T(8,128)(2,1)}, u32[]{:S(2)}, u32[]{:S(2)}) collective-permute-start(bf16[1,768,192]{2,1,0:T(8,128)(2,1)} %get-tuple-element.202), channel_id=1, source_target_pairs={{0,1},{1,0},{2,3},{3,2},{4,5},{5,4},{6,7},{7,6},{8,9},{9,8},{10,11... | collective-permute-start | bytes 884744 | tf_op jit(solution)/shard_map/ppermute | solution.py:748
  151.4 11.5 %collective-permute-start.21 = (bf16[80,768]{1,0:T(8,128)(2,1)}, bf16[80,768]{1,0:T(8,128)(2,1)S(1)}, u32[]{:S(2)}, u32[]{:S(2)}) collective-permute-start(bf16[80,768]{1,0:T(8,128)(2,1)} %get-tuple-element.210), channel_id=1, source_target_pairs={{0,2},{1,3},{2,0},{3,1},{4,6},{5,7},{6,4},{7,5},{8,10},{9,11},{10,... | collective-permute-start | bytes 368648 | tf_op jit(solution)/shard_map/ppermute | solution.py:1099
  151.4 11.5 %collective-permute-start.22 = (bf16[80,768]{1,0:T(8,128)(2,1)}, bf16[80,768]{1,0:T(8,128)(2,1)S(1)}, u32[]{:S(2)}, u32[]{:S(2)}) collective-permute-start(bf16[80,768]{1,0:T(8,128)(2,1)} %get-tuple-element.211), channel_id=1, source_target_pairs={{0,1},{1,2},{2,3},{3,0},{4,5},{5,6},{6,7},{7,4},{8,9},{9,10},{10,1... | collective-permute-start | bytes 368648 | tf_op jit(solution)/shard_map/ppermute | solution.py:1099
  152.2 15.3 %collective-permute-start.23 = (bf16[1,256,192]{2,1,0:T(8,128)(2,1)}, bf16[1,256,192]{2,1,0:T(8,128)(2,1)S(1)}, u32[]{:S(2)}, u32[]{:S(2)}) collective-permute-start(bf16[1,256,192]{2,1,0:T(8,128)(2,1)} %get-tuple-element.213), channel_id=1, source_target_pairs={{0,1},{1,0},{2,3},{3,2},{4,5},{5,4},{6,7},{7,6},{8,9},{9,8},{10,11... | collective-permute-start | bytes 294920 | tf_op jit(solution)/shard_map/ppermute | solution.py:748
  154.9 28.4 %collective-permute-start.24 = (bf16[1,256,192]{2,1,0:T(8,128)(2,1)}, bf16[1,256,192]{2,1,0:T(8,128)(2,1)}, u32[]{:S(2)}, u32[]{:S(2)}) collective-permute-start(bf16[1,256,192]{2,1,0:T(8,128)(2,1)} %get-tuple-element.216), channel_id=1, source_target_pairs={{0,1},{1,0},{2,3},{3,2},{4,5},{5,4},{6,7},{7,6},{8,9},{9,8},{10,11... | collective-permute-start | bytes 294920 | tf_op jit(solution)/shard_map/ppermute | solution.py:748
  156.0 26.0 %collective-permute-start.26 = (bf16[1,768,192]{2,1,0:T(8,128)(2,1)S(1)}, bf16[1,768,192]{2,1,0:T(8,128)(2,1)}, u32[]{:S(2)}, u32[]{:S(2)}) collective-permute-start(bf16[1,768,192]{2,1,0:T(8,128)(2,1)S(1)} %add_convert_fusion.1), channel_id=1, source_target_pairs={{0,2},{1,3},{2,0},{3,1},{4,6},{5,7},{6,4},{7,5},{8,10},{9,11},{10,... | collective-permute-start | bytes 884744 | tf_op jit(solution)/shard_map/ppermute | solution.py:748
  167.6 16.2 %all-to-all-start.1 = ((bf16[8,64,768]{2,1,0:T(8,128)(2,1)}), bf16[8,64,768]{2,1,0:T(8,128)(2,1)S(1)}, u32[]{:S(2)}, u32[]{:S(2)}) async-start(bf16[8,64,768]{2,1,0:T(8,128)(2,1)} %bitcast.25), calls=%async_computation.1 | async-start | bytes 1572864 | tf_op jit(solution)/shard_map/all_to_all | solution.py:1114
  175.5 19.7 %collective-permute-start.25 = (bf16[1,256,192]{2,1,0:T(8,128)(2,1)S(1)}, bf16[1,256,192]{2,1,0:T(8,128)(2,1)S(1)}, u32[]{:S(2)}, u32[]{:S(2)}) collective-permute-start(bf16[1,256,192]{2,1,0:T(8,128)(2,1)S(1)} %add_convert_fusion.2), channel_id=1, source_target_pairs={{0,2},{1,3},{2,0},{3,1},{4,6},{5,7},{6,4},{7,5},{8,10},{9,11},{10,... | collective-permute-start | bytes 294920 | tf_op jit(solution)/shard_map/ppermute | solution.py:748
  (32 other events, 149.8 us)
Sparse Core Ops, SparseCore 0:
  132.7 23.8 all-gather.1
